TPU v7x, 32 devices: a whole 2x2x4 slice. The times are simulated.
32 devices in a mesh: expert: 8 (over z, x), tensor: 4 (over y, core).
Axes of the slice: x: 2, y: 2, z: 4, core: 2. Of those that a mesh axis runs over, the one named last changes fastest.
Arguments:
- tokens: bfloat16 [4096, 768], P('expert'), may hold values from -6 to 6
- norm_first: bfloat16 [768], replicated, may hold values from 0.5 to 1.5
- w_query: bfloat16 [768, 768], P(None, 'tensor'), may hold values from -0.078125 to 0.078125
- w_key: bfloat16 [768, 768], P(None, 'tensor'), may hold values from -0.078125 to 0.078125
- w_value: bfloat16 [768, 768], P(None, 'tensor'), may hold values from -0.21875 to 0.21875
- w_output: bfloat16 [768, 768], P('tensor'), may hold values from -0.875 to 0.875
- bias_table: bfloat16 [32, 12], P(None, 'tensor'), may hold values from -4 to 4
- norm_second: bfloat16 [768], replicated, may hold values from 0.5 to 1.5
- w_router: bfloat16 [768, 8], replicated, may hold values from -0.15625 to 0.15625
- w_expert_in: bfloat16 [8, 768, 3072], P('expert', None, 'tensor'), may hold values from -0.21875 to 0.21875
- w_expert_out: bfloat16 [8, 3072, 768], P('expert', 'tensor'), may hold values from -0.625 to 0.625
- routes: int32 [4096, 1], P('expert'), may hold values from 0 to 7; in each aligned block of 512 rows (0 to 511, 512 to 1023, ...) at most 96 rows name the same one
- cotangent: bfloat16 [4096, 768], P('expert'), may hold values from -6 to 6
Outputs:
- layer_out: bfloat16 [4096, 768], P('expert')
- grad_tokens: float32 [4096, 768], P('expert')
- grad_norm_first: float32 [768], replicated
- grad_w_query: float32 [768, 768], P('expert', 'tensor')
- grad_w_key: float32 [768, 768], P('expert', 'tensor')
- grad_w_value: float32 [768, 768], P('expert', 'tensor')
- grad_w_output: float32 [768, 768], P('tensor', 'expert')
- grad_bias_table: float32 [32, 12], P(None, 'tensor')
- grad_norm_second: float32 [768], replicated
- grad_w_router: float32 [768, 8], replicated
- grad_w_expert_in: float32 [8, 768, 3072], P('expert', None, 'tensor')
- grad_w_expert_out: float32 [8, 3072, 768], P('expert', 'tensor')
Inputs may be any that keep to these rules, and one draw needn't show every extreme that they name: `routes`: in each aligned block of 512 tokens no expert is named by more than 96 tokens, a bound that some block reaches.
All inputs are finite; a program needn't handle non-finite values.
Results may differ from a plain program's by a relative error of at most 0.014.
Values may be sent and summed in bfloat16 or wider, within the bound.
No kernel may reach another device: no remote copies, remote signals or barrier semaphores. Data moves between devices by JAX's collectives and lax.ppermute only.
A program may use at most 128 MiB of HBM per device.

v0:
```python
import functools

import jax
import jax.numpy as jnp
from jax import lax
from jax.experimental import pallas as pl
from jax.experimental.pallas import tpu as pltpu
from jax.sharding import PartitionSpec as P

BUCKETS = 32
LEN = 512
TENSOR = 4

EPSILON = 1e-06
THRESHOLDS = (12, 16, 23, 32, 46, 64, 91)
BF16 = jnp.bfloat16
F32 = jnp.float32
GELU_SCALE = (2.0 / 3.141592653589793) ** 0.5
GELU_CUBE = 0.044715
MIB = 1024 * 1024


def dot(left, right):
    return jnp.dot(left, right, preferred_element_type=F32)


def dot_t(left, right):
    return lax.dot_general(left, right, (((1,), (1,)), ((), ())), preferred_element_type=F32)


def t_dot(left, right):
    return lax.dot_general(left, right, (((0,), (0,)), ((), ())), preferred_element_type=F32)


def inv_rms_of(values):
    return lax.rsqrt(jnp.mean(values * values, axis=-1, keepdims=True) + EPSILON)


def rms_norm_back(values, inv_rms, gain, grad):
    scaled = gain * grad
    inner = jnp.mean(scaled * values, axis=-1, keepdims=True)
    return inv_rms * scaled - values * (inv_rms * inv_rms * inv_rms * inner)


TILE = 128


def bias_tiles(table_ref, head):
    row = lax.broadcasted_iota(jnp.int32, (TILE, TILE), 0)
    col = lax.broadcasted_iota(jnp.int32, (TILE, TILE), 1)
    tiles = []
    for offset in (-1, 0, 1):
        shift = col - row + offset * TILE
        distance = jnp.abs(shift)

        def chain(base):
            tile = jnp.full((TILE, TILE), table_ref[head, base], F32)
            for n in range(1, 8):
                tile = jnp.where(distance >= n, table_ref[head, base + n], tile)
            for n, threshold in enumerate((8,) + THRESHOLDS):
                tile = jnp.where(distance >= threshold, table_ref[head, base + 8 + n], tile)
            return tile

        if offset < 0:
            tiles.append(chain(0))
        elif offset > 0:
            tiles.append(chain(16))
        else:
            tiles.append(jnp.where(shift > 0, chain(16), chain(0)))
    return tiles


def bias_rows(table_ref, tiles, head, block):
    parts = []
    for other in range(LEN // TILE):
        offset = other - block
        if offset < -1:
            parts.append(jnp.full((TILE, TILE), table_ref[head, 15], F32))
        elif offset > 1:
            parts.append(jnp.full((TILE, TILE), table_ref[head, 31], F32))
        else:
            parts.append(tiles[offset + 1])
    return jnp.concatenate(parts, axis=1)


def head_columns(values, head, size):
    lane = lax.broadcasted_iota(jnp.int32, values.shape, 1)
    return jnp.where((lane >= head * size) & (lane < (head + 1) * size), values, jnp.zeros_like(values))


def attend_kernel(heads, size, table_ref, tokens_ref, gain_ref, wq_ref, wk_ref, wv_ref, normed_ref, q_ref, k_ref, v_ref, mixed_ref, total_ref):
    values = tokens_ref[...].astype(F32)
    normed = (values * inv_rms_of(values) * gain_ref[0:1, :]).astype(BF16)
    normed_ref[...] = normed
    normed_ref.leave()
    q_ref[...] = dot_t(normed, wq_ref[...]).astype(BF16)
    q_ref.leave()
    k_ref[...] = dot_t(normed, wk_ref[...]).astype(BF16)
    k_ref.leave()
    v_ref[...] = dot_t(normed, wv_ref[...]).astype(BF16)
    v_ref.leave()
    all_tiles = [bias_tiles(table_ref, head) for head in range(heads)]
    keys = k_ref[...]
    head_values = [head_columns(v_ref[...], head, size) for head in range(heads)]
    for block in range(LEN // TILE):
        rows = pl.ds(block * TILE, TILE)
        queries = q_ref[rows, :]
        mixed = None
        lane = lax.broadcasted_iota(jnp.int32, (TILE, TILE), 1)
        totals = jnp.zeros((TILE, TILE), F32)
        for head in range(heads):
            scores = dot_t(head_columns(queries, head, size), keys)
            scores = scores + bias_rows(table_ref, all_tiles[head], head, block)
            row_max = jnp.max(scores, axis=-1, keepdims=True)
            exponent = jnp.exp(scores - row_max)
            row_total = jnp.sum(exponent, axis=-1, keepdims=True)
            weights = (exponent * (1.0 / row_total)).astype(BF16)
            part = dot(weights, head_values[head])
            mixed = part if mixed is None else mixed + part
            totals = jnp.where(lane == head, row_max + jnp.log(row_total), totals)
        mixed_ref[rows, :] = mixed.astype(BF16)
        total_ref[rows, :] = totals


class Input:
    def __init__(self, copies, buffer):
        self.copies, self.buffer, self.shape = copies, buffer, buffer.shape
        for copy in copies:
            copy.start()

    def __getitem__(self, index):
        for copy in self.copies:
            copy.wait()
        self.copies = ()
        return self.buffer[index]


class Output:
    def __init__(self, copy, buffer):
        self.copy, self.buffer, self.shape, self.left = copy, buffer, buffer.shape, False

    def __getitem__(self, index):
        return self.buffer[index]

    def __setitem__(self, index, values):
        self.buffer[index] = values

    def leave(self):
        if not self.left:
            self.copy.start()
        self.left = True


def call(kernel, name, outs, smem, operands, scratch=(), limit=60, flops=10**5, moved=10**4):
    groups = [entry if isinstance(entry, tuple) else (entry,) for entry in operands]
    arrays = [array for group in groups for array in group]
    anywhere = pl.BlockSpec(memory_space=pl.ANY)
    held = [
        pltpu.VMEM((len(group),) * (len(group) > 1) + group[0].shape, group[0].dtype) for group in groups
    ] + [pltpu.VMEM(shape, kind) for shape, kind in outs]

    def body(*refs):
        refs = list(refs)

        def take(count):
            taken = refs[:count]
            del refs[:count]
            return taken

        scalars, sources, targets = take(len(smem)), take(len(arrays)), take(len(outs))
        in_buffers, out_buffers = take(len(groups)), take(len(outs))
        in_sems, out_sems = take(2)
        inputs, number = [], 0
        for group, buffer in zip(groups, in_buffers):
            copies = []
            for m in range(len(group)):
                place = buffer if len(group) == 1 else buffer.at[scalars[0][0, 0] ^ m]
                copies.append(pltpu.make_async_copy(sources[number], place, in_sems.at[number]))
                number += 1
            inputs.append(Input(copies, buffer))
        outputs = [
            Output(pltpu.make_async_copy(buffer, target, out_sems.at[i]), buffer)
            for i, (buffer, target) in enumerate(zip(out_buffers, targets))
        ]
        kernel(*scalars, *inputs, *outputs, *refs)
        for entry in inputs:
            for copy in entry.copies:
                copy.wait()
        for entry in outputs:
            entry.leave()
        for entry in outputs:
            entry.copy.wait()

    return pl.pallas_call(
        body,
        out_shape=tuple(jax.ShapeDtypeStruct(shape, kind) for shape, kind in outs),
        in_specs=[pl.BlockSpec(memory_space=pltpu.SMEM)] * len(smem) + [anywhere] * len(arrays),
        out_specs=(anywhere,) * len(outs),
        scratch_shapes=held
        + [pltpu.SemaphoreType.DMA((len(arrays),)), pltpu.SemaphoreType.DMA((len(outs),))]
        + [pltpu.VMEM(shape, kind) for shape, kind in scratch],
        compiler_params=pltpu.CompilerParams(vmem_limit_bytes=limit * MIB),
        cost_estimate=pl.CostEstimate(flops=flops, bytes_accessed=moved, transcendentals=0),
        name=name,
    )(*smem, *arrays)


def attend(tokens, gains, weights, table, heads):
    rows, columns = tokens.shape[0], weights[0].shape[0]
    small = ((rows, columns), BF16)
    return call(
        functools.partial(attend_kernel, heads, columns // heads),
        "attend",
        ((tokens.shape, BF16), small, small, small, small, ((rows, TILE), F32)),
        (table,),
        (tokens, gains, *weights),
    )


def hidden_kernel(tensor_ref, place_ref, tokens_ref, mixed_ref, weight_ref, gain_ref, router_ref, routes_ref, cot_ref, hidden_ref, own_ref, gate_ref, both):
    width = tokens_ref.shape[1]
    experts = router_ref.shape[0]
    gain = gain_ref[1:2, :]
    for block in range(tokens_ref.shape[0] // TILE):
        rows = pl.ds(block * TILE, TILE)
        hidden = tokens_ref[rows, :].astype(F32)
        for m in range(TENSOR):
            hidden = hidden + dot(mixed_ref[m, rows, :], weight_ref[m])
        hidden_ref[rows, :] = hidden
        normed = (hidden * inv_rms_of(hidden) * gain).astype(BF16)
        probs = softmax(dot_t(normed, router_ref[...]))
        lane = lax.broadcasted_iota(jnp.int32, (TILE, experts), 1)
        gate = jnp.sum(jnp.where(lane == routes_ref[rows, :], probs, 0.0), axis=-1, keepdims=True)
        gate_ref[rows, :] = jnp.broadcast_to(gate, (TILE, TILE))
        both[rows, :width] = normed
        both[rows, width:] = (cot_ref[rows, :].astype(F32) * gate).astype(BF16)
    hidden_ref.leave()
    gate_ref.leave()
    slots = own_ref.shape[0]
    row = lax.broadcasted_iota(jnp.int32, (slots, place_ref.shape[1]), 0)
    own_ref[...] = dot((row == place_ref[...]).astype(BF16), both[...]).astype(BF16)


def softmax(values):
    exponent = jnp.exp(values - jnp.max(values, axis=-1, keepdims=True))
    return exponent / jnp.sum(exponent, axis=-1, keepdims=True)


def expert_kernel(me_ref, f_a, b_a, f_b, b_b, in_ref, out_ref, router_ref, keep_ref, send_ref, active_ref, pre_ref, grad_ref):
    rows = f_a.shape[0]
    experts = router_ref.shape[0]
    lane = lax.broadcasted_iota(jnp.int32, (rows, experts), 1)
    own_hot = (lane == me_ref[0, 0]).astype(F32)
    total = None
    for place, (forward, backward) in enumerate(((f_b, b_b), (f_a, b_a))):
        pre = dot(forward[...], in_ref[...])
        square = pre * pre
        bent = jnp.tanh(GELU_SCALE * (pre + GELU_CUBE * square * pre))
        active = (0.5 * pre * (1.0 + bent)).astype(BF16)
        slope = 0.5 * (1.0 + bent) + 0.5 * pre * (1.0 - bent * bent) * (
            GELU_SCALE * (1.0 + 3.0 * GELU_CUBE * square)
        )
        grad_active = dot_t(backward[...], out_ref[...])
        grad_pre = (grad_active * slope).astype(BF16)
        gate_grad = jnp.sum(active.astype(F32) * grad_active, axis=1, keepdims=True)
        probs = softmax(dot_t(forward[...], router_ref[...]))
        grad_logits = (gate_grad * (own_hot - probs)).astype(BF16)
        back = dot_t(grad_pre, in_ref[...]) + dot(grad_logits, router_ref[...])
        where = pl.ds((1 - place) * rows, rows)
        active_ref[where, :] = active
        pre_ref[where, :] = grad_pre
        if place == 0:
            send_ref[...] = back.astype(BF16)
            send_ref.leave()
        else:
            keep_ref[...] = back
        part = t_dot(grad_logits, forward[...])
        total = part if total is None else total + part
    grad_ref[...] = total


def expert_pair(me, first, second, weight_in, weight_out, router):
    rows, width = first[0].shape
    hidden = weight_in.shape[1]
    return call(
        expert_kernel,
        "expert_pair",
        (
            ((rows, width), F32), ((rows, width), BF16), ((2 * rows, hidden), BF16), ((2 * rows, hidden), BF16),
            (router.shape, F32),
        ),
        (me,),
        (*first, *second, weight_in, weight_out, router),

    )


def result_kernel(active_a, active_b, out_ref, keep_ref, send_ref):
    rows = active_a.shape[0] // 2
    for place, active in enumerate((active_a, active_b)):
        where = pl.ds(place * rows, rows)
        keep_ref[where, :] = dot(active[pl.ds(0, rows), :], out_ref[...])
        send_ref[where, :] = dot(active[pl.ds(rows, rows), :], out_ref[...]).astype(BF16)


def expert_grad_kernel(f0, f1, f2, f3, b0, b1, b2, b3, active_a, active_b, pre_a, pre_b, in_ref, out_ref):
    rows = f0.shape[0]
    forward = jnp.concatenate([f0[...], f1[...], f2[...], f3[...]], axis=0)
    pre = jnp.concatenate([pre_a[...], pre_b[...]], axis=0)
    in_ref[...] = t_dot(forward, pre)
    backward = jnp.concatenate([b0[...], b1[...], b2[...], b3[...]], axis=0)
    active = jnp.concatenate([active_a[...], active_b[...]], axis=0)
    out_ref[...] = t_dot(active, backward)


def back_kernel(
    heads, size, table_ref, core_ref, place_ref, r0, r1, r2, r3, hidden_ref, cot_ref, gain_ref, wo_ref, mixed_ref,
    normed_ref, q_ref, k_ref, v_ref, total_ref, wq_ref, wk_ref, wv_ref, router_a, router_b,
    grad_ref, sums_ref, keep_ref, send_ref, small_ref, gm_ref, attn_ref, qb_ref, kacc, vacc, part_ref,
):
    tok_rows, width = hidden_ref.shape
    columns = q_ref.shape[1]
    chunk = r0.shape[0]
    gain = gain_ref[1:2, :]
    count = LEN // TILE
    norm_part = None
    for block in range(count):
        rows = pl.ds(block * TILE, TILE)
        place = place_ref[rows, :]
        back = None
        for m, returned in enumerate((r0, r1, r2, r3)):
            lane = lax.broadcasted_iota(jnp.int32, (TILE, chunk), 1) + m * chunk
            found = dot((lane == place).astype(BF16), returned[...])
            back = found if back is None else back + found
        hidden = hidden_ref[rows, :]
        inv = inv_rms_of(hidden)
        summed = jnp.sum((back * hidden * inv).reshape(TILE // 8, 8, width), axis=0)
        norm_part = summed if norm_part is None else norm_part + summed
        grad = cot_ref[rows, :].astype(F32) + rms_norm_back(hidden, inv, gain, back)
        grad_ref[rows, :] = grad
        low = grad.astype(BF16)
        attn_ref[rows, :] = low
        gm_ref[rows, :] = dot_t(low, wo_ref[...]).astype(BF16)
    grad_ref.leave()
    keys, all_values = k_ref[...], v_ref[...]
    kacc[...] = jnp.zeros_like(kacc)
    vacc[...] = jnp.zeros_like(vacc)
    all_tiles = [bias_tiles(table_ref, head) for head in range(heads)]
    head_keys = [head_columns(keys, head, size) for head in range(heads)]
    near = [[None] * 3 for _ in range(heads)]
    far = [[None] * 2 for _ in range(heads)]
    for block in range(count):
        rows = pl.ds(block * TILE, TILE)
        queries, grads, totals = q_ref[rows, :], gm_ref[rows, :], total_ref[rows, :]
        query_back = None
        for head in range(heads):
            head_queries = head_columns(queries, head, size)
            head_grads = head_columns(grads, head, size)
            scores = dot_t(head_queries, keys)
            scores = scores + bias_rows(table_ref, all_tiles[head], head, block)
            probs = jnp.exp(scores - totals[:, head : head + 1])
            probs_grad = dot_t(head_grads, all_values)
            inner = jnp.sum(probs_grad * probs, axis=-1, keepdims=True)
            score_grad = (probs * (probs_grad - inner)).astype(BF16)
            part = dot(score_grad, head_keys[head])
            query_back = part if query_back is None else query_back + part
            kacc[...] += t_dot(score_grad, head_queries)
            vacc[...] += t_dot(probs.astype(BF16), head_grads)
            wide = score_grad.astype(F32)
            for other in range(count):
                offset = other - block
                tile = wide[:, other * TILE : (other + 1) * TILE]
                if abs(offset) <= 1:
                    held = near[head][offset + 1]
                    near[head][offset + 1] = tile if held is None else held + tile
                else:
                    side = 0 if offset < 0 else 1
                    summed = jnp.sum(tile.reshape(TILE // 8, 8, TILE), axis=0)
                    held = far[head][side]
                    far[head][side] = summed if held is None else held + summed
        qb_ref[rows, :] = query_back.astype(BF16)
    key_back, value_back = kacc[...].astype(BF16), vacc[...].astype(BF16)
    query_back = qb_ref[...]
    part_ref[...] = dot(query_back, wq_ref[...]) + dot(key_back, wk_ref[...]) + dot(value_back, wv_ref[...])
    half = tok_rows // 2
    extra = keep_ref.shape[0] - half
    core = core_ref[0, 0]
    keep_ref[pl.ds(0, half), :] = part_ref[pl.ds(pl.multiple_of(core * half, half), half), :]
    send_ref[pl.ds(0, half), :] = part_ref[pl.ds(pl.multiple_of((1 - core) * half, half), half), :].astype(BF16)
    router = (router_a[...] + router_b[...]).astype(BF16).astype(F32)
    if extra > router.shape[0]:
        router = jnp.concatenate([router, jnp.zeros((extra - router.shape[0], width), F32)], axis=0)
    keep_ref[pl.ds(half, extra), :] = router
    send_ref[pl.ds(half, extra), :] = router.astype(BF16)
    send_ref.leave()
    keep_ref.leave()
    empty = jnp.zeros((tok_rows, columns), BF16)
    sums_ref[:, : 2 * columns] = t_dot(
        normed_ref[...], jnp.concatenate([query_back, key_back], axis=1)
    ).astype(BF16)
    sums_ref[:, 2 * columns :] = (
        t_dot(normed_ref[...], jnp.concatenate([value_back, empty], axis=1))
        + t_dot(attn_ref[...], jnp.concatenate([empty, mixed_ref[...]], axis=1))
    ).astype(BF16)
    sums_ref.leave()
    bias = bias_sums(heads, near, far)
    bias_row = lax.dot_general(
        jnp.ones((8, TILE), F32), bias, (((1,), (1,)), ((), ())),
        precision=lax.Precision.HIGHEST, preferred_element_type=F32,
    )
    bias_row = jnp.concatenate([bias_row, jnp.zeros((8, width - heads * BUCKETS), F32)], axis=1)
    norm_row = jnp.broadcast_to(jnp.sum(norm_part, axis=0, keepdims=True), (8, width))
    line = lax.broadcasted_iota(jnp.int32, (8, width), 0)
    small_ref[...] = jnp.where(line == 0, norm_row, jnp.where(line == 1, bias_row, 0.0))


def bias_sums(heads, near, far):
    row = lax.broadcasted_iota(jnp.int32, (TILE, TILE), 0)
    col = lax.broadcasted_iota(jnp.int32, (TILE, TILE), 1)

    def fold(values):
        return jnp.sum(values.reshape(TILE // 8, 8, TILE), axis=0)

    edges = tuple(range(8)) + (8,) + THRESHOLDS + (1 << 20,)
    pieces = []
    for head in range(heads):
        for sign in (0, 1):
            for n in range(16):
                piece = jnp.zeros((8, TILE), F32)
                for offset in ((-1, 0) if sign == 0 else (0, 1)):
                    low = 0 if offset == 0 else 1
                    if edges[n + 1] <= low or edges[n] > (TILE - 1 if offset == 0 else 2 * TILE - 1):
                        continue
                    shift = col - row + offset * TILE
                    distance = jnp.abs(shift)
                    inside = (distance >= edges[n]) & (distance < edges[n + 1])
                    if offset == 0:
                        inside = inside & ((shift > 0) if sign else (shift <= 0))
                    piece = piece + fold(jnp.where(inside, near[head][offset + 1], 0.0))
                if n == 15:
                    piece = piece + far[head][sign]
                pieces.append(jnp.sum(piece, axis=0, keepdims=True))
    return jnp.concatenate(pieces, axis=0)


def swap(values, axis, mask):
    size = lax.axis_size(axis)
    return lax.ppermute(values, axis, [(i, i ^ mask) for i in range(size)])


def gather_tensor(values):
    far = swap(values, "tensor", 2)
    near = swap(values, "tensor", 1)
    return values, near, far, swap(far, "tensor", 1)


def exchange_expert(blocks):
    return lax.all_to_all(blocks, "expert", split_axis=0, concat_axis=0, tiled=True)


def after(values, done):
    return lax.optimization_barrier((values, done))[0]


def sum_expert(values, done):
    mask = 1
    while mask < lax.axis_size("expert"):
        if 2 * mask >= lax.axis_size("expert"):
            values = after(values, done)
        values = values + swap(values, "expert", mask)
        mask = 2 * mask
    return values


def on_device(
    tokens,
    norm_first,
    w_query,
    w_key,
    w_value,
    w_output,
    bias_table,
    norm_second,
    w_router,
    w_expert_in,
    w_expert_out,
    routes,
    cotangent,
):
    tok_rows, width = tokens.shape
    experts = w_router.shape[1]
    capacity = max(2, 3 * tok_rows // (2 * experts))
    quarter = -(-capacity // TENSOR)
    heads_here = bias_table.shape[1]
    columns = w_query.shape[1]
    chunk_rows = experts * quarter
    half = tok_rows // 2
    extra = max(16, experts)
    my_tensor = lax.axis_index("tensor")
    my_expert = lax.axis_index("expert").astype(jnp.int32).reshape(1, 1)
    core = (my_tensor & 1).astype(jnp.int32)
    weight_in = w_expert_in[0]
    weight_out = w_expert_out[0]
    router = w_router.T
    weights = (w_query.T, w_key.T, w_value.T)
    table = bias_table.T.astype(F32)
    gains = jnp.stack([norm_first, norm_second]).astype(F32)

    normed, queries, keys, values, mixed, totals = attend(tokens, gains, weights, table, heads_here)

    chosen = routes[:, 0]
    route_hot = chosen[:, None] == jnp.arange(experts, dtype=jnp.int32)[None, :]
    places = jnp.arange(tok_rows, dtype=jnp.int32)
    before = (places[:, None] > places[None, :]).astype(BF16)
    earlier = dot(before, route_hot.astype(BF16))
    slot_index = jnp.sum(jnp.where(route_hot, earlier, 0.0), axis=1).astype(jnp.int32)
    chunk = (slot_index // quarter) ^ my_tensor
    place = (chunk * experts + chosen) * quarter + slot_index % quarter

    output_parts = gather_tensor(w_output)
    hidden, own, gate = call(
        hidden_kernel,
        "hidden",
        (((tok_rows, width), F32), ((chunk_rows, 2 * width), BF16), ((tok_rows, TILE), F32)),
        (my_tensor.astype(jnp.int32).reshape(1, 1),),
        (
            place[None, :], tokens, gather_tensor(after(mixed, output_parts[2])), output_parts, gains, router,
            routes, cotangent,
        ),
        scratch=(((tok_rows, 2 * width), BF16),),
    )
    arrived = exchange_expert(own.reshape(experts, quarter, 2 * width)).reshape(chunk_rows, 2 * width)
    forward, backward = arrived[:, :width], arrived[:, width:]
    forward_far, backward_far = swap(forward, "tensor", 2), swap(backward, "tensor", 2)
    forward_near, backward_near = swap(forward, "tensor", 1), swap(backward, "tensor", 1)

    keep_a, send_a, active_a, pre_a, router_a = expert_pair(
        my_expert, (forward, backward), (forward_near, backward_near), weight_in, weight_out, router
    )
    forward_diag = swap(after(forward_far, active_a), "tensor", 1)
    backward_diag = swap(after(backward_far, active_a), "tensor", 1)
    got_a = swap(send_a, "tensor", 1)
    keep_b, send_b, active_b, pre_b, router_b = expert_pair(
        my_expert, (forward_far, backward_far), (forward_diag, backward_diag), weight_in, weight_out, router
    )
    other = (keep_b + swap(send_b, "tensor", 1).astype(F32)).astype(BF16)
    other_back = swap(other, "tensor", 2)

    keep_r, send_r = call(
        result_kernel,
        "expert_result",
        (((2 * chunk_rows, width), F32), ((2 * chunk_rows, width), BF16)),
        (),
        (after(active_a, other), active_b, weight_out),
    )
    own_back = ((keep_a + got_a.astype(F32)) + other_back.astype(F32)).astype(BF16)
    own_back = after(own_back, send_r)
    home = exchange_expert(own_back.reshape(experts, quarter, width)).reshape(chunk_rows, width)
    got_r = swap(send_r, "tensor", 1).astype(F32)
    far_result = swap((keep_r[chunk_rows:] + got_r[chunk_rows:]).astype(BF16), "tensor", 2)
    grad_expert_in, grad_expert_out = call(
        expert_grad_kernel,
        "expert_grads",
        ((weight_in.shape, F32), (weight_out.shape, F32)),
        (),
        (
            forward, forward_near, forward_far, forward_diag, backward, backward_near, backward_far, backward_diag,
            after(active_a, got_r), active_b, pre_a, pre_b,
        ),
    )
    own_result = ((keep_r[:chunk_rows] + got_r[:chunk_rows]) + far_result.astype(F32)).astype(BF16)
    home = after(home, (own_result, grad_expert_in))
    result = exchange_expert(after(own_result, home).reshape(experts, quarter, width)).reshape(chunk_rows, width)
    home_far = swap(home, "tensor", 2)
    returned_back = (home, swap(home, "tensor", 1), home_far, after(swap(home_far, "tensor", 1), result))

    small = ((8, width), F32)
    grad_hidden, sums, keep, send, small = call(
        functools.partial(back_kernel, heads_here, columns // heads_here),
        "layer_back",
        (
            ((tok_rows, width), F32), ((width, 4 * columns), BF16), ((half + extra, width), F32),
            ((half + extra, width), BF16), ((8, width), F32),
        ),
        (table, core.reshape(1, 1)),
        (
            place[:, None], *returned_back, hidden, cotangent, gains, w_output, mixed, normed,
            queries, keys, values, totals, *weights, router_a, router_b,
        ),
        scratch=(
            ((tok_rows, columns), BF16), ((tok_rows, width), BF16), ((tok_rows, columns), BF16),
            ((tok_rows, columns), F32), ((tok_rows, columns), F32), ((tok_rows, width), F32),
        ),
    )

    pair = (keep + swap(send, "tensor", 1).astype(F32)).astype(BF16)
    total = (pair.astype(F32) + swap(pair, "tensor", 2).astype(F32)).astype(BF16)
    near = swap(total[:half], "tensor", 1)
    low = jnp.where(core == 1, near, total[:half]).astype(F32)
    high = jnp.where(core == 1, total[:half], near).astype(F32)
    normed_back = jnp.concatenate([low, high])
    inputs = tokens.astype(F32)
    inv_first = inv_rms_of(inputs)
    gain_first = gains[0:1]
    norm_first_part = jnp.sum(normed_back * inputs * inv_first, axis=0, keepdims=True)
    grad_tokens = grad_hidden + rms_norm_back(inputs, inv_first, gain_first, normed_back)

    returned = gather_tensor(after(result, total))
    place_hot = (
        place[:, None] == jnp.arange(TENSOR * chunk_rows, dtype=jnp.int32)[None, :]
    ).astype(BF16)
    layer_out = (hidden + gate[:, :1] * dot(place_hot, jnp.concatenate(returned))).astype(BF16)

    grads = exchange_expert(sums.reshape(lax.axis_size("expert"), -1, 4 * columns))
    grads = jnp.sum(grads.astype(F32), axis=0)
    small = sum_expert(jnp.concatenate([total[half : half + experts].astype(F32), norm_first_part, small[:2]]), grads)
    bias_size = BUCKETS * heads_here
    return (
        layer_out,
        grad_tokens,
        small[experts],
        grads[:, :columns],
        grads[:, columns : 2 * columns],
        grads[:, 2 * columns : 3 * columns],
        grads[:, 3 * columns :].T,
        small[experts + 2, :bias_size].reshape(heads_here, BUCKETS).T,
        small[experts + 1],
        small[:experts].T,
        grad_expert_in[None],
        grad_expert_out[None],
    )


def solution(mesh):
    return jax.shard_map(
        on_device,
        mesh=mesh,
        in_specs=(
            P("expert", None),
            P(),
            P(None, "tensor"),
            P(None, "tensor"),
            P(None, "tensor"),
            P("tensor", None),
            P(None, "tensor"),
            P(),
            P(),
            P("expert", None, "tensor"),
            P("expert", "tensor", None),
            P("expert", None),
            P("expert", None),
        ),
        out_specs=(
            P("expert", None),
            P("expert", None),
            P(),
            P("expert", "tensor"),
            P("expert", "tensor"),
            P("expert", "tensor"),
            P("tensor", "expert"),
            P(None, "tensor"),
            P(),
            P(),
            P("expert", None, "tensor"),
            P("expert", "tensor", None),
        ),
        check_vma=False,
    )
```

profile of v0, /device:TPU:0, one launch (start us, length us, event | category | flops | bytes accessed | tf_op | source)
XLA Modules:
  0.0 192.8 jit_solution(16581932563213214498)
XLA Ops:
  0.7 3.0 %collective-permute-start = (bf16[192,768]{1,0:T(8,128)(2,1)}, bf16[192,768]{1,0:T(8,128)(2,1)S(1)}, u32[]{:S(2)}, u32[]{:S(2)}) collective-permute-start(bf16[192,768]{1,0:T(8,128)(2,1)} %refs_10_.1), channel_id=1, source_target_pairs={{0,2},{1,3},{2,0},{3,1},{4,6},{5,7},{6,4},{7,5},{8,10},{9,11},{10,... | collective-permute-start | bytes 884744 | tf_op jit(solution)/shard_map/ppermute | solution.py:448
  3.7 1.3 convert_bitcast_fusion.refs_0_
  4.9 0.7 stack.10
  6.9 7.9 %attend.1 = (bf16[512,768]{1,0:T(8,128)(2,1)}, bf16[512,192]{1,0:T(8,128)(2,1)}, bf16[512,192]{1,0:T(8,128)(2,1)}, bf16[512,192]{1,0:T(8,128)(2,1)}, bf16[512,192]{1,0:T(8,128)(2,1)}, /*index=5*/f32[512,128]{1,0:T(8,128)}) custom-call(f32[3,32]{1,0:T(4,128)} %convert_bitcast_fusion.refs_0_, bf16[512,768]{1,0:T(8,128)(2,1)} %refs_2_.1, ...), custom_call_target="tpu_custom_call" | custom-call | flops 100000 | bytes 10000 | tf_op jit(solution)/shard_map/attend/pallas_call | solution.py:194
  15.8 0.9 copy.58.refs_13_
  16.7 7.4 %collective-permute-done.2.refs_5_ = bf16[512,192]{1,0:T(8,128)(2,1)S(1)} collective-permute-done((bf16[512,192]{1,0:T(8,128)(2,1)}, bf16[512,192]{1,0:T(8,128)(2,1)S(1)}, u32[]{:S(2)}, u32[]{:S(2)}) %collective-permute-start.2) | collective-permute-done | bytes 196640 | tf_op jit(solution)/shard_map/ppermute | solution.py:448
  24.9 0.9 collective-permute-done.3.refs_6_
  25.7 0.7 copy-done.22
  26.4 6.6 %hidden.1 = (f32[512,768]{1,0:T(8,128)}, bf16[192,1536]{1,0:T(8,128)(2,1)}, f32[512,128]{1,0:T(8,128)}) custom-call(s32[1,1]{1,0:T(1,128)} %bitcast.refs_0_, s32[1,512]{1,0:T(1,128)} %fusion.24.refs_1_, bf16[512,768]{1,0:T(8,128)(2,1)} %refs_2_.1, bf16[512,192]{1,0:T(8,128)(2,1)} %get-tuple-element.52.refs_3_.refs_11_, bf16[512,192]{1,0:T(8,128)(2,1)} %copy-done.21, ...), custom_call_target="tpu_custom_call" | custom-call | flops 100000 | bytes 10000 | tf_op jit(solution)/shard_map/hidden/pallas_call | solution.py:194
  33.0 22.6 %all_to_all.20 = bf16[8,24,1536]{2,1,0:T(8,128)(2,1)S(1)} all-to-all(bf16[8,24,1536]{2,1,0:T(8,128)(2,1)} %bitcast.52), channel_id=1, replica_groups=mesh['expert'=8,'tensor'=4] {'expert'}, dimensions={0} | all-to-all | bytes 1179648 | tf_op jit(solution)/shard_map/all_to_all | solution.py:458
  56.8 1.5 collective-permute-start.9
  58.4 0.7 copy-done.5
  59.2 7.5 %expert_pair.2 = (f32[192,768]{1,0:T(8,128)}, bf16[192,768]{1,0:T(8,128)(2,1)}, bf16[384,768]{1,0:T(8,128)(2,1)}, bf16[384,768]{1,0:T(8,128)(2,1)}, f32[8,768]{1,0:T(8,128)}) custom-call(s32[1,1]{1,0:T(1,128)} %bitcast.12.refs_0_, bf16[192,768]{1,0:T(8,128)(2,1)} %copy-done.2, bf16[192,768]{1,0:T(8,128)(2,1)} %copy-done.1, bf16[192,768]{1,0:T(8,128)(2,1)} %copy-done.5, ...), custom_call_target="tpu_custom_call" | custom-call | flops 100000 | bytes 10000 | tf_op jit(solution)/shard_map/expert_pair/pallas_call | solution.py:194
  66.8 4.8 %collective-permute-done.9.refs_2_.refs_6_ = bf16[192,768]{1,0:T(8,128)(2,1)S(1)} collective-permute-done((bf16[192,768]{1,0:T(8,128)(2,1)S(1)}, bf16[192,768]{1,0:T(8,128)(2,1)S(1)}, u32[]{:S(2)}, u32[]{:S(2)}) %collective-permute-start.9) | collective-permute-done | bytes 294944 | tf_op jit(solution)/shard_map/ppermute | solution.py:448
  71.7 1.6 collective-permute-done.11.refs_4_.refs_7_
  73.3 0.7 copy-done.10
  74.0 7.5 %expert_pair.3 = (f32[192,768]{1,0:T(8,128)}, bf16[192,768]{1,0:T(8,128)(2,1)}, bf16[384,768]{1,0:T(8,128)(2,1)}, bf16[384,768]{1,0:T(8,128)(2,1)}, f32[8,768]{1,0:T(8,128)}) custom-call(s32[1,1]{1,0:T(1,128)} %bitcast.12.refs_0_, bf16[192,768]{1,0:T(8,128)(2,1)} %copy-done.7, bf16[192,768]{1,0:T(8,128)(2,1)} %copy-done.8, bf16[192,768]{1,0:T(8,128)(2,1)} %copy-done.9, ...), custom_call_target="tpu_custom_call" | custom-call | flops 100000 | bytes 10000 | tf_op jit(solution)/shard_map/expert_pair/pallas_call | solution.py:194
  81.6 1.6 collective-permute-done.12
  83.3 1.2 add_convert_fusion.4
  84.5 4.0 %expert_result.1 = (f32[384,768]{1,0:T(8,128)}, bf16[384,768]{1,0:T(8,128)(2,1)}) custom-call(bf16[384,768]{1,0:T(8,128)(2,1)} %get-tuple-element.68.refs_0_.refs_8_, bf16[384,768]{1,0:T(8,128)(2,1)} %get-tuple-element.62.refs_1_.refs_9_, bf16[768,768]{1,0:T(8,128)(2,1)} %bitcast.38), custom_call_target="tpu_custom_call" | custom-call | flops 100000 | bytes 10000 | tf_op jit(solution)/shard_map/expert_result/pallas_call | solution.py:194
  89.6 1.2 collective-permute-done.13
  91.5 7.4 %collective-permute-done.16 = bf16[192,768]{1,0:T(8,128)(2,1)S(1)} collective-permute-done((bf16[192,768]{1,0:T(8,128)(2,1)S(1)}, bf16[192,768]{1,0:T(8,128)(2,1)S(1)}, u32[]{:S(2)}, u32[]{:S(2)}) %collective-permute-start.16) | collective-permute-done | bytes 294944 | tf_op jit(solution)/shard_map/ppermute | solution.py:448
  98.9 0.8 add_convert_fusion.3
  99.7 3.4 %all-to-all-start.1 = ((bf16[8,24,768]{2,1,0:T(8,128)(2,1)}), bf16[8,24,768]{2,1,0:T(8,128)(2,1)S(1)}, u32[]{:S(2)}, u32[]{:S(2)}) async-start(bf16[8,24,768]{2,1,0:T(8,128)(2,1)} %bitcast.17), calls=%async_computation.1 | async-start | bytes 589824 | tf_op jit(solution)/shard_map/all_to_all | solution.py:458
  103.2 6.8 %expert_grads.1 = (f32[768,768]{1,0:T(8,128)}, f32[768,768]{1,0:T(8,128)}) custom-call(bf16[192,768]{1,0:T(8,128)(2,1)} %copy-done.2, bf16[192,768]{1,0:T(8,128)(2,1)} %copy-done.5, bf16[192,768]{1,0:T(8,128)(2,1)} %copy-done.7, bf16[192,768]{1,0:T(8,128)(2,1)} %copy-done.9, bf16[192,768]{1,0:T(8,128)(2,1)} %copy-done.1, bf16[192,768]{1,0:T(8,128)(2,1)} %copy-done.6, ...), custom_call_target="tpu_custom_call" | custom-call | flops 100000 | bytes 10000 | tf_op jit(solution)/shard_map/expert_grads/pallas_call | solution.py:194
  110.0 0.8 fusion.19
  110.8 1.0 all-to-all-done.1
  112.5 5.0 %all-to-all-start.2 = ((bf16[8,24,768]{2,1,0:T(8,128)(2,1)}), bf16[8,24,768]{2,1,0:T(8,128)(2,1)S(1)}, u32[]{:S(2)}, u32[]{:S(2)}) async-start(bf16[8,24,768]{2,1,0:T(8,128)(2,1)} %bitcast.19), calls=%async_computation.2 | async-start | bytes 589824 | tf_op jit(solution)/shard_map/all_to_all | solution.py:458
  118.6 0.8 fusion.31
  119.4 6.6 %all-to-all-done.2 = bf16[8,24,768]{2,1,0:T(8,128)(2,1)S(1)} async-done(((bf16[8,24,768]{2,1,0:T(8,128)(2,1)}), bf16[8,24,768]{2,1,0:T(8,128)(2,1)S(1)}, u32[]{:S(2)}, u32[]{:S(2)}) %all-to-all-start.2) | async-done | bytes 294944 | tf_op jit(solution)/shard_map/all_to_all | solution.py:458
  126.8 18.5 %layer_back.1 = (f32[512,768]{1,0:T(8,128)}, bf16[768,768]{1,0:T(8,128)(2,1)}, f32[272,768]{1,0:T(8,128)}, bf16[272,768]{1,0:T(8,128)(2,1)}, f32[8,768]{1,0:T(8,128)}) custom-call(f32[3,32]{1,0:T(4,128)} %convert_bitcast_fusion.refs_0_, s32[1,1]{1,0:T(1,128)} %bitcast.21.refs_1_, s32[512,1]{1,0:T(8,128)} %get-tuple-element.143.refs_2_, ...), custom_call_target="tpu_custom_call" | custom-call | flops 100000 | bytes 10000 | tf_op jit(solution)/shard_map/layer_back/pallas_call | solution.py:194
  145.4 2.0 %collective-permute-done.20 = bf16[272,768]{1,0:T(8,128)(2,1)S(1)} collective-permute-done((bf16[272,768]{1,0:T(8,128)(2,1)}, bf16[272,768]{1,0:T(8,128)(2,1)S(1)}, u32[]{:S(2)}, u32[]{:S(2)}) %collective-permute-start.20) | collective-permute-done | bytes 417824 | tf_op jit(solution)/shard_map/ppermute | solution.py:448
  147.3 1.2 add_convert_fusion.2
  148.6 1.6 collective-permute-start.21
  150.4 3.6 %all-to-all-start.3 = ((bf16[8,96,768]{2,1,0:T(8,128)(2,1)}), bf16[8,96,768]{2,1,0:T(8,128)(2,1)S(1)}, u32[]{:S(2)}, u32[]{:S(2)}) async-start(bf16[8,96,768]{2,1,0:T(8,128)(2,1)} %bitcast.51), calls=%async_computation.3 | async-start | bytes 2359296 | tf_op jit(solution)/shard_map/all_to_all | solution.py:458
  154.0 6.3 %collective-permute-done.21 = bf16[272,768]{1,0:T(8,128)(2,1)S(1)} collective-permute-done((bf16[272,768]{1,0:T(8,128)(2,1)S(1)}, bf16[272,768]{1,0:T(8,128)(2,1)S(1)}, u32[]{:S(2)}, u32[]{:S(2)}) %collective-permute-start.21) | collective-permute-done | bytes 417824 | tf_op jit(solution)/shard_map/ppermute | solution.py:448
  160.6 1.6 collective-permute-start.23
  162.2 1.1 slice_reduce_fusion
  163.2 0.7 slice.69
  164.2 5.8 %collective-permute-done.23 = bf16[192,768]{1,0:T(8,128)(2,1)S(1)} collective-permute-done((bf16[192,768]{1,0:T(8,128)(2,1)S(1)}, bf16[192,768]{1,0:T(8,128)(2,1)S(1)}, u32[]{:S(2)}, u32[]{:S(2)}) %collective-permute-start.23) | collective-permute-done | bytes 294944 | tf_op jit(solution)/shard_map/ppermute | solution.py:448
  170.1 0.8 fusion.6
  171.0 5.3 %collective-permute-done.26 = f32[11,768]{1,0:T(8,128)S(1)} collective-permute-done((f32[11,768]{1,0:T(8,128)S(1)}, f32[11,768]{1,0:T(8,128)S(1)}, u32[]{:S(2)}, u32[]{:S(2)}) %collective-permute-start.26) | collective-permute-done | bytes 33824 | tf_op jit(solution)/shard_map/ppermute | solution.py:448
  176.4 1.6 fusion.2
  178.0 5.9 %collective-permute-done.27 = f32[11,768]{1,0:T(8,128)S(1)} collective-permute-done((f32[11,768]{1,0:T(8,128)S(1)}, f32[11,768]{1,0:T(8,128)S(1)}, u32[]{:S(2)}, u32[]{:S(2)}) %collective-permute-start.27) | collective-permute-done | bytes 33824 | tf_op jit(solution)/shard_map/ppermute | solution.py:448
  183.9 1.8 add_convert_fusion
  185.9 0.8 slice_bitcast_fusion
  186.7 0.7 copy.70
  187.4 3.5 %collective-permute-done.28 = f32[11,768]{1,0:T(8,128)S(1)} collective-permute-done((f32[11,768]{1,0:T(8,128)S(1)}, f32[11,768]{1,0:T(8,128)S(1)}, u32[]{:S(2)}, u32[]{:S(2)}) %collective-permute-start.28) | collective-permute-done | bytes 33824 | tf_op jit(solution)/shard_map/ppermute | solution.py:448
  (124 shorter events, 12.2 us)
Async XLA Ops:
  0.6 14.2 %copy-start.24 = (s32[512,1]{0,1:T(1,128)S(1)}, s32[512,1]{0,1:T(1,128)}, u32[]{:S(2)}) copy-start(s32[512,1]{0,1:T(1,128)} %param.24) | copy-start | bytes 6148
  0.7 14.5 %collective-permute-start = (bf16[192,768]{1,0:T(8,128)(2,1)}, bf16[192,768]{1,0:T(8,128)(2,1)S(1)}, u32[]{:S(2)}, u32[]{:S(2)}) collective-permute-start(bf16[192,768]{1,0:T(8,128)(2,1)} %refs_10_.1), channel_id=1, source_target_pairs={{0,2},{1,3},{2,0},{3,1},{4,6},{5,7},{6,4},{7,5},{8,10},{9,11},{10,... | collective-permute-start | bytes 884744 | tf_op jit(solution)/shard_map/ppermute | solution.py:448
  3.7 21.1 %collective-permute-start.4 = (bf16[192,768]{1,0:T(8,128)(2,1)}, bf16[192,768]{1,0:T(8,128)(2,1)S(1)}, u32[]{:S(2)}, u32[]{:S(2)}) collective-permute-start(bf16[192,768]{1,0:T(8,128)(2,1)} %refs_10_.1), channel_id=1, source_target_pairs={{0,1},{1,0},{2,3},{3,2},{4,5},{5,4},{6,7},{7,6},{8,9},{9,8},{10,11... | collective-permute-start | bytes 884744 | tf_op jit(solution)/shard_map/ppermute | solution.py:448
  15.2 10.5 %copy-start.14 = (bf16[192,768]{1,0:T(8,128)(2,1)}, bf16[192,768]{1,0:T(8,128)(2,1)S(1)}, u32[]{:S(2)}) copy-start(bf16[192,768]{1,0:T(8,128)(2,1)S(1)} %collective-permute-done.refs_9_) | copy-start | bytes 884740
  15.2 9.0 %collective-permute-start.2 = (bf16[512,192]{1,0:T(8,128)(2,1)}, bf16[512,192]{1,0:T(8,128)(2,1)S(1)}, u32[]{:S(2)}, u32[]{:S(2)}) collective-permute-start(bf16[512,192]{1,0:T(8,128)(2,1)} %get-tuple-element.52.refs_3_.refs_11_), channel_id=1, source_target_pairs={{0,2},{1,3},{2,0},{3,1},{4,6},{5,7},{6,4},{7,5},{8,10},{9,11},{10,... | collective-permute-start | bytes 589832 | tf_op jit(solution)/shard_map/ppermute | solution.py:448
  15.3 9.5 %collective-permute-start.5 = (bf16[192,768]{1,0:T(8,128)(2,1)S(1)}, bf16[192,768]{1,0:T(8,128)(2,1)S(1)}, u32[]{:S(2)}, u32[]{:S(2)}) collective-permute-start(bf16[192,768]{1,0:T(8,128)(2,1)S(1)} %collective-permute-done.refs_9_), channel_id=1, source_target_pairs={{0,1},{1,0},{2,3},{3,2},{4,5},{5,4},{6,7},{7,6},{8,9},{9,8},{10,11... | collective-permute-start | bytes 884744 | tf_op jit(solution)/shard_map/ppermute | solution.py:448
  16.7 8.1 %collective-permute-start.1 = (bf16[512,192]{1,0:T(8,128)(2,1)}, bf16[512,192]{1,0:T(8,128)(2,1)S(1)}, u32[]{:S(2)}, u32[]{:S(2)}) collective-permute-start(bf16[512,192]{1,0:T(8,128)(2,1)} %get-tuple-element.52.refs_3_.refs_11_), channel_id=1, source_target_pairs={{0,1},{1,0},{2,3},{3,2},{4,5},{5,4},{6,7},{7,6},{8,9},{9,8},{10,11... | collective-permute-start | bytes 589832 | tf_op jit(solution)/shard_map/ppermute | solution.py:448
  24.2 1.5 collective-permute-start.3
  55.7 2.6 %copy-start.1 = (bf16[192,768]{1,0:T(8,128)(2,1)}, bf16[192,768]{1,0:T(8,128)(2,1)S(1)}, u32[]{:S(2)}) copy-start(bf16[192,768]{1,0:T(8,128)(2,1)S(1)} %get-tuple-element.146.refs_2_.refs_4_) | copy-start | bytes 884740
  55.7 2.6 %copy-start.2 = (bf16[192,768]{1,0:T(8,128)(2,1)}, bf16[192,768]{1,0:T(8,128)(2,1)S(1)}, u32[]{:S(2)}) copy-start(bf16[192,768]{1,0:T(8,128)(2,1)S(1)} %get-tuple-element.147.refs_1_.refs_0_) | copy-start | bytes 884740
  55.8 2.6 %collective-permute-start.6 = (bf16[192,768]{1,0:T(8,128)(2,1)S(1)}, bf16[192,768]{1,0:T(8,128)(2,1)S(1)}, u32[]{:S(2)}, u32[]{:S(2)}) collective-permute-start(bf16[192,768]{1,0:T(8,128)(2,1)S(1)} %get-tuple-element.147.refs_1_.refs_0_), channel_id=1, source_target_pairs={{0,1},{1,0},{2,3},{3,2},{4,5},{5,4},{6,7},{7,6},{8,9},{9,8},{10,11... | collective-permute-start | bytes 884744 | tf_op jit(solution)/shard_map/ppermute | solution.py:448
  55.8 2.5 %collective-permute-start.7 = (bf16[192,768]{1,0:T(8,128)(2,1)S(1)}, bf16[192,768]{1,0:T(8,128)(2,1)S(1)}, u32[]{:S(2)}, u32[]{:S(2)}) collective-permute-start(bf16[192,768]{1,0:T(8,128)(2,1)S(1)} %get-tuple-element.146.refs_2_.refs_4_), channel_id=1, source_target_pairs={{0,1},{1,0},{2,3},{3,2},{4,5},{5,4},{6,7},{7,6},{8,9},{9,8},{10,11... | collective-permute-start | bytes 884744 | tf_op jit(solution)/shard_map/ppermute | solution.py:448
  56.3 10.4 %collective-permute-start.8 = (bf16[192,768]{1,0:T(8,128)(2,1)S(1)}, bf16[192,768]{1,0:T(8,128)(2,1)S(1)}, u32[]{:S(2)}, u32[]{:S(2)}) collective-permute-start(bf16[192,768]{1,0:T(8,128)(2,1)S(1)} %get-tuple-element.147.refs_1_.refs_0_), channel_id=1, source_target_pairs={{0,2},{1,3},{2,0},{3,1},{4,6},{5,7},{6,4},{7,5},{8,10},{9,11},{10,... | collective-permute-start | bytes 884744 | tf_op jit(solution)/shard_map/ppermute | solution.py:448
  56.8 14.8 %collective-permute-start.9 = (bf16[192,768]{1,0:T(8,128)(2,1)S(1)}, bf16[192,768]{1,0:T(8,128)(2,1)S(1)}, u32[]{:S(2)}, u32[]{:S(2)}) collective-permute-start(bf16[192,768]{1,0:T(8,128)(2,1)S(1)} %get-tuple-element.146.refs_2_.refs_4_), channel_id=1, source_target_pairs={{0,2},{1,3},{2,0},{3,1},{4,6},{5,7},{6,4},{7,5},{8,10},{9,11},{10,... | collective-permute-start | bytes 884744 | tf_op jit(solution)/shard_map/ppermute | solution.py:448
  66.7 6.5 %copy-start.7 = (bf16[192,768]{1,0:T(8,128)(2,1)}, bf16[192,768]{1,0:T(8,128)(2,1)S(1)}, u32[]{:S(2)}) copy-start(bf16[192,768]{1,0:T(8,128)(2,1)S(1)} %collective-permute-done.8.refs_1_.refs_2_) | copy-start | bytes 884740
  66.7 4.9 %collective-permute-start.10 = (bf16[192,768]{1,0:T(8,128)(2,1)S(1)}, bf16[192,768]{1,0:T(8,128)(2,1)S(1)}, u32[]{:S(2)}, u32[]{:S(2)}) collective-permute-start(bf16[192,768]{1,0:T(8,128)(2,1)S(1)} %collective-permute-done.8.refs_1_.refs_2_), channel_id=1, source_target_pairs={{0,1},{1,0},{2,3},{3,2},{4,5},{5,4},{6,7},{7,6},{8,9},{9,8},{10,11... | collective-permute-start | bytes 884744 | tf_op jit(solution)/shard_map/ppermute | solution.py:448
  71.6 1.6 copy-start.8
  71.6 1.6 collective-permute-start.11
  71.7 1.6 copy-start.9
  81.4 1.9 collective-permute-start.12
  83.3 5.4 %copy-start.25 = (bf16[192,768]{1,0:T(8,128)(2,1)S(1)}, bf16[192,768]{1,0:T(8,128)(2,1)}, u32[]{:S(2)}) copy-start(bf16[192,768]{1,0:T(8,128)(2,1)} %get-tuple-element.66) | copy-start | bytes 884740
  88.5 2.4 %copy-start.12 = (f32[384,768]{1,0:T(8,128)S(1)}, f32[384,768]{1,0:T(8,128)}, u32[]{:S(2)}) copy-start(f32[384,768]{1,0:T(8,128)} %get-tuple-element.63) | copy-start | bytes 3538948
  88.5 2.3 %collective-permute-start.13 = (bf16[384,768]{1,0:T(8,128)(2,1)}, bf16[384,768]{1,0:T(8,128)(2,1)S(1)}, u32[]{:S(2)}, u32[]{:S(2)}) collective-permute-start(bf16[384,768]{1,0:T(8,128)(2,1)} %get-tuple-element.64), channel_id=1, source_target_pairs={{0,1},{1,0},{2,3},{3,2},{4,5},{5,4},{6,7},{7,6},{8,9},{9,8},{10,11... | collective-permute-start | bytes 1769480 | tf_op jit(solution)/shard_map/ppermute | solution.py:448
  88.7 10.2 %copy-start.13 = (f32[192,768]{1,0:T(8,128)S(1)}, f32[192,768]{1,0:T(8,128)}, u32[]{:S(2)}) copy-start(f32[192,768]{1,0:T(8,128)} %get-tuple-element.65) | copy-start | bytes 1769476
  88.7 2.8 %collective-permute-start.15 = (bf16[192,768]{1,0:T(8,128)(2,1)S(1)}, bf16[192,768]{1,0:T(8,128)(2,1)S(1)}, u32[]{:S(2)}, u32[]{:S(2)}) collective-permute-start(bf16[192,768]{1,0:T(8,128)(2,1)S(1)} %copy-done.25), channel_id=1, source_target_pairs={{0,1},{1,0},{2,3},{3,2},{4,5},{5,4},{6,7},{7,6},{8,9},{9,8},{10,11... | collective-permute-start | bytes 884744 | tf_op jit(solution)/shard_map/ppermute | solution.py:448
  89.1 9.9 %collective-permute-start.16 = (bf16[192,768]{1,0:T(8,128)(2,1)S(1)}, bf16[192,768]{1,0:T(8,128)(2,1)S(1)}, u32[]{:S(2)}, u32[]{:S(2)}) collective-permute-start(bf16[192,768]{1,0:T(8,128)(2,1)S(1)} %add_convert_fusion.4), channel_id=1, source_target_pairs={{0,2},{1,3},{2,0},{3,1},{4,6},{5,7},{6,4},{7,5},{8,10},{9,11},{10,... | collective-permute-start | bytes 884744 | tf_op jit(solution)/shard_map/ppermute | solution.py:448
  90.9 19.0 %collective-permute-start.14 = (bf16[192,768]{1,0:T(8,128)(2,1)S(1)}, bf16[192,768]{1,0:T(8,128)(2,1)S(1)}, u32[]{:S(2)}, u32[]{:S(2)}) collective-permute-start(bf16[192,768]{1,0:T(8,128)(2,1)S(1)} %fusion.17), channel_id=1, source_target_pairs={{0,2},{1,3},{2,0},{3,1},{4,6},{5,7},{6,4},{7,5},{8,10},{9,11},{10,... | collective-permute-start | bytes 884744 | tf_op jit(solution)/shard_map/ppermute | solution.py:448
  99.7 12.0 %all-to-all-start.1 = ((bf16[8,24,768]{2,1,0:T(8,128)(2,1)}), bf16[8,24,768]{2,1,0:T(8,128)(2,1)S(1)}, u32[]{:S(2)}, u32[]{:S(2)}) async-start(bf16[8,24,768]{2,1,0:T(8,128)(2,1)} %bitcast.17), calls=%async_computation.1 | async-start | bytes 589824 | tf_op jit(solution)/shard_map/all_to_all | solution.py:458
  111.7 7.7 %copy-start.11 = (bf16[8,24,768]{2,1,0:T(8,128)(2,1)}, bf16[8,24,768]{2,1,0:T(8,128)(2,1)S(1)}, u32[]{:S(2)}) copy-start(bf16[8,24,768]{2,1,0:T(8,128)(2,1)S(1)} %all-to-all-done.1) | copy-start | bytes 884740
  111.7 6.7 %collective-permute-start.18 = (bf16[192,768]{1,0:T(8,128)(2,1)S(1)}, bf16[192,768]{1,0:T(8,128)(2,1)S(1)}, u32[]{:S(2)}, u32[]{:S(2)}) collective-permute-start(bf16[192,768]{1,0:T(8,128)(2,1)S(1)} %bitcast.48), channel_id=1, source_target_pairs={{0,2},{1,3},{2,0},{3,1},{4,6},{5,7},{6,4},{7,5},{8,10},{9,11},{10,... | collective-permute-start | bytes 884744 | tf_op jit(solution)/shard_map/ppermute | solution.py:448
  112.5 13.4 %all-to-all-start.2 = ((bf16[8,24,768]{2,1,0:T(8,128)(2,1)}), bf16[8,24,768]{2,1,0:T(8,128)(2,1)S(1)}, u32[]{:S(2)}, u32[]{:S(2)}) async-start(bf16[8,24,768]{2,1,0:T(8,128)(2,1)} %bitcast.19), calls=%async_computation.2 | async-start | bytes 589824 | tf_op jit(solution)/shard_map/all_to_all | solution.py:458
  117.8 8.2 %collective-permute-start.17 = (bf16[192,768]{1,0:T(8,128)(2,1)S(1)}, bf16[192,768]{1,0:T(8,128)(2,1)S(1)}, u32[]{:S(2)}, u32[]{:S(2)}) collective-permute-start(bf16[192,768]{1,0:T(8,128)(2,1)S(1)} %bitcast.49), channel_id=1, source_target_pairs={{0,1},{1,0},{2,3},{3,2},{4,5},{5,4},{6,7},{7,6},{8,9},{9,8},{10,11... | collective-permute-start | bytes 884744 | tf_op jit(solution)/shard_map/ppermute | solution.py:448
  118.5 7.5 %copy-start.16 = (bf16[192,768]{1,0:T(8,128)(2,1)}, bf16[192,768]{1,0:T(8,128)(2,1)S(1)}, u32[]{:S(2)}) copy-start(bf16[192,768]{1,0:T(8,128)(2,1)S(1)} %collective-permute-done.18.refs_5_) | copy-start | bytes 884740
  118.5 7.5 %collective-permute-start.19 = (bf16[192,768]{1,0:T(8,128)(2,1)S(1)}, bf16[192,768]{1,0:T(8,128)(2,1)S(1)}, u32[]{:S(2)}, u32[]{:S(2)}) collective-permute-start(bf16[192,768]{1,0:T(8,128)(2,1)S(1)} %collective-permute-done.18.refs_5_), channel_id=1, source_target_pairs={{0,1},{1,0},{2,3},{3,2},{4,5},{5,4},{6,7},{7,6},{8,9},{9,8},{10,11... | collective-permute-start | bytes 884744 | tf_op jit(solution)/shard_map/ppermute | solution.py:448
  145.3 4.9 %copy-start = (bf16[512,768]{1,0:T(8,128)(2,1)S(1)}, bf16[512,768]{1,0:T(8,128)(2,1)}, u32[]{:S(2)}) copy-start(bf16[512,768]{1,0:T(8,128)(2,1)} %refs_2_.1) | copy-start | bytes 2359300
  145.3 2.0 %collective-permute-start.20 = (bf16[272,768]{1,0:T(8,128)(2,1)}, bf16[272,768]{1,0:T(8,128)(2,1)S(1)}, u32[]{:S(2)}, u32[]{:S(2)}) collective-permute-start(bf16[272,768]{1,0:T(8,128)(2,1)} %get-tuple-element.83), channel_id=1, source_target_pairs={{0,1},{1,0},{2,3},{3,2},{4,5},{5,4},{6,7},{7,6},{8,9},{9,8},{10,11... | collective-permute-start | bytes 1253384 | tf_op jit(solution)/shard_map/ppermute | solution.py:448
  148.6 11.7 %collective-permute-start.21 = (bf16[272,768]{1,0:T(8,128)(2,1)S(1)}, bf16[272,768]{1,0:T(8,128)(2,1)S(1)}, u32[]{:S(2)}, u32[]{:S(2)}) collective-permute-start(bf16[272,768]{1,0:T(8,128)(2,1)S(1)} %add_convert_fusion.2), channel_id=1, source_target_pairs={{0,2},{1,3},{2,0},{3,1},{4,6},{5,7},{6,4},{7,5},{8,10},{9,11},{10,... | collective-permute-start | bytes 1253384 | tf_op jit(solution)/shard_map/ppermute | solution.py:448
  150.4 35.2 %all-to-all-start.3 = ((bf16[8,96,768]{2,1,0:T(8,128)(2,1)}), bf16[8,96,768]{2,1,0:T(8,128)(2,1)S(1)}, u32[]{:S(2)}, u32[]{:S(2)}) async-start(bf16[8,96,768]{2,1,0:T(8,128)(2,1)} %bitcast.51), calls=%async_computation.3 | async-start | bytes 2359296 | tf_op jit(solution)/shard_map/all_to_all | solution.py:458
  154.0 6.6 %copy-start.23 = (f32[2,768]{1,0:T(2,128)S(1)}, f32[2,768]{1,0:T(2,128)}, u32[]{:S(2)}) copy-start(f32[2,768]{1,0:T(2,128)} %maximum_convert_fusion.refs_2_.refs_11_.refs_9_) | copy-start | bytes 18436
  160.5 9.6 %collective-permute-start.25 = (bf16[256,768]{1,0:T(8,128)(2,1)S(1)}, bf16[256,768]{1,0:T(8,128)(2,1)S(1)}, u32[]{:S(2)}, u32[]{:S(2)}) collective-permute-start(bf16[256,768]{1,0:T(8,128)(2,1)S(1)} %slice.83), channel_id=1, source_target_pairs={{0,1},{1,0},{2,3},{3,2},{4,5},{5,4},{6,7},{7,6},{8,9},{9,8},{10,11... | collective-permute-start | bytes 1179656 | tf_op jit(solution)/shard_map/ppermute | solution.py:448
  160.6 9.5 %collective-permute-start.23 = (bf16[192,768]{1,0:T(8,128)(2,1)S(1)}, bf16[192,768]{1,0:T(8,128)(2,1)S(1)}, u32[]{:S(2)}, u32[]{:S(2)}) collective-permute-start(bf16[192,768]{1,0:T(8,128)(2,1)S(1)} %bitcast.53), channel_id=1, source_target_pairs={{0,2},{1,3},{2,0},{3,1},{4,6},{5,7},{6,4},{7,5},{8,10},{9,11},{10,... | collective-permute-start | bytes 884744 | tf_op jit(solution)/shard_map/ppermute | solution.py:448
  164.0 19.8 %collective-permute-start.22 = (bf16[192,768]{1,0:T(8,128)(2,1)S(1)}, bf16[192,768]{1,0:T(8,128)(2,1)S(1)}, u32[]{:S(2)}, u32[]{:S(2)}) collective-permute-start(bf16[192,768]{1,0:T(8,128)(2,1)S(1)} %bitcast.54), channel_id=1, source_target_pairs={{0,1},{1,0},{2,3},{3,2},{4,5},{5,4},{6,7},{7,6},{8,9},{9,8},{10,11... | collective-permute-start | bytes 884744 | tf_op jit(solution)/shard_map/ppermute | solution.py:448
  164.2 12.2 %copy-start.4 = (f32[512,768]{1,0:T(8,128)S(1)}, f32[512,768]{1,0:T(8,128)}, u32[]{:S(2)}) copy-start(f32[512,768]{1,0:T(8,128)} %get-tuple-element.85) | copy-start | bytes 4718596
  170.0 13.8 %collective-permute-start.24 = (bf16[192,768]{1,0:T(8,128)(2,1)S(1)}, bf16[192,768]{1,0:T(8,128)(2,1)S(1)}, u32[]{:S(2)}, u32[]{:S(2)}) collective-permute-start(bf16[192,768]{1,0:T(8,128)(2,1)S(1)} %collective-permute-done.23), channel_id=1, source_target_pairs={{0,1},{1,0},{2,3},{3,2},{4,5},{5,4},{6,7},{7,6},{8,9},{9,8},{10,11... | collective-permute-start | bytes 884744 | tf_op jit(solution)/shard_map/ppermute | solution.py:448
  170.9 5.4 %collective-permute-start.26 = (f32[11,768]{1,0:T(8,128)S(1)}, f32[11,768]{1,0:T(8,128)S(1)}, u32[]{:S(2)}, u32[]{:S(2)}) collective-permute-start(f32[11,768]{1,0:T(8,128)S(1)} %pad_maximum_fusion.1), channel_id=1, source_target_pairs={{0,4},{4,0},{8,12},{12,8},{16,20},{20,16},{24,28},{28,24},{1,5},{5... | collective-permute-start | bytes 101384 | tf_op jit(solution)/shard_map/ppermute | solution.py:448
  176.3 7.5 %collective-permute-start.27 = (f32[11,768]{1,0:T(8,128)S(1)}, f32[11,768]{1,0:T(8,128)S(1)}, u32[]{:S(2)}, u32[]{:S(2)}) collective-permute-start(f32[11,768]{1,0:T(8,128)S(1)} %fusion.30), channel_id=1, source_target_pairs={{0,8},{4,12},{8,0},{12,4},{16,24},{20,28},{24,16},{28,20},{1,9},{5... | collective-permute-start | bytes 101384 | tf_op jit(solution)/shard_map/ppermute | solution.py:448
  176.4 7.5 %copy-start.3 = (f32[512,768]{1,0:T(8,128)S(1)}, f32[512,768]{1,0:T(8,128)}, u32[]{:S(2)}) copy-start(f32[512,768]{1,0:T(8,128)} %get-tuple-element.53.refs_7_) | copy-start | bytes 4718596
  185.8 5.1 %collective-permute-start.28 = (f32[11,768]{1,0:T(8,128)S(1)}, f32[11,768]{1,0:T(8,128)S(1)}, u32[]{:S(2)}, u32[]{:S(2)}) collective-permute-start(f32[11,768]{1,0:T(8,128)S(1)} %add.135), channel_id=1, source_target_pairs={{0,16},{4,20},{8,24},{12,28},{16,0},{20,4},{24,8},{28,12},{1,17},{... | collective-permute-start | bytes 101384 | tf_op jit(solution)/shard_map/ppermute | solution.py:448
  (10 other events, 8.8 us)
where the time goes:
time: 194 us; the launch traced here: 193 us
  waiting for transfers between devices  61.9 us (32%)
  Pallas kernels  58.7 us (30%)
  starting transfers between devices  24.6 us (13%)
  blocking collectives  22.6 us (12%)
  local copies, waits for them, and re-layouts  11.2 us (6%)
  other arithmetic  10.5 us (5%)
  matrix products  2.04 us (1%)
    pallas_call x7, Pallas kernels, call(): pl.pallas_call(body, out_shape=tuple((jax.ShapeDtypeStruct(shape, kind) f...  58.7 us
    ppermute x29, waiting for transfers between devices, swap(): return lax.ppermute(values, axis, [(i, i ^ mask) for i in range(size)])  54.3 us
    all_to_all x1, blocking collectives, exchange_expert(): lax.all_to_all(blocks, 'expert', split_axis=0, concat_axis=0, tiled=True)  22.6 us
    ppermute x29, starting transfers between devices, swap(): return lax.ppermute(values, axis, [(i, i ^ mask) for i in range(size)])  12.6 us
    all_to_all x3, starting transfers between devices, exchange_expert(): lax.all_to_all(blocks, 'expert', split_axis=0, concat_axis=0, tiled=True)  12 us
    all_to_all x3, waiting for transfers between devices, exchange_expert(): lax.all_to_all(blocks, 'expert', split_axis=0, concat_axis=0, tiled=True)  7.55 us
    unnamed x54, local copies, waits for them, and re-layouts  4.73 us
  transfers between devices with their start and end apart: 32, of which 16 were waited for; matrix products, arithmetic and copies ran while one was open for 8% of the time, Pallas kernels for 12%

commit v1 on v0

--- a/solution.py
+++ b/solution.py
@@ -10,6 +10,7 @@
 BUCKETS = 32
 LEN = 512
 TENSOR = 4
+PAIRED = 8
 
 EPSILON = 1e-06
 THRESHOLDS = (12, 16, 23, 32, 46, 64, 91)
@@ -45,29 +46,39 @@
 TILE = 128
 
 
+def skew(tile):
+    return pltpu.roll(tile, 0, 1, stride=1, stride_axis=0)
+
+
+def diagonal_sums(tile):
+    row = lax.broadcasted_iota(jnp.int32, (TILE, TILE), 0)
+    turn = (row + lax.broadcasted_iota(jnp.int32, (TILE, TILE), 1) == TILE - 1).astype(F32)
+    turned = lax.dot_general(
+        turn, tile, (((1,), (0,)), ((), ())), precision=lax.Precision.HIGHEST, preferred_element_type=F32
+    )
+    return jnp.sum(pltpu.roll(turned, 1, 1, stride=1, stride_axis=0), axis=0, keepdims=True)
+
+
 def bias_tiles(table_ref, head):
-    row = lax.broadcasted_iota(jnp.int32, (TILE, TILE), 0)
-    col = lax.broadcasted_iota(jnp.int32, (TILE, TILE), 1)
-    tiles = []
-    for offset in (-1, 0, 1):
-        shift = col - row + offset * TILE
-        distance = jnp.abs(shift)
-
-        def chain(base):
-            tile = jnp.full((TILE, TILE), table_ref[head, base], F32)
-            for n in range(1, 8):
-                tile = jnp.where(distance >= n, table_ref[head, base + n], tile)
-            for n, threshold in enumerate((8,) + THRESHOLDS):
-                tile = jnp.where(distance >= threshold, table_ref[head, base + 8 + n], tile)
-            return tile
-
-        if offset < 0:
-            tiles.append(chain(0))
-        elif offset > 0:
-            tiles.append(chain(16))
-        else:
-            tiles.append(jnp.where(shift > 0, chain(16), chain(0)))
-    return tiles
+    lane = lax.broadcasted_iota(jnp.int32, (8, TILE), 1)
+    place = lax.broadcasted_iota(jnp.int32, (TILE, TILE), 1)
+
+    def chain(base, distance):
+        line = jnp.full((8, TILE), table_ref[head, base], F32)
+        for n in range(1, 8):
+            line = jnp.where(distance >= n, table_ref[head, base + n], line)
+        for n, threshold in enumerate((8,) + THRESHOLDS):
+            line = jnp.where(distance >= threshold, table_ref[head, base + 8 + n], line)
+        return jnp.broadcast_to(line[0:1, :], (TILE, TILE))
+
+    ahead = skew(jnp.where(place == 0, table_ref[head, 0], chain(16, lane)))
+    behind = skew(chain(0, TILE - lane))
+    upper = place >= lax.broadcasted_iota(jnp.int32, (TILE, TILE), 0)
+    return [
+        jnp.where(upper, behind, table_ref[head, 15]),
+        jnp.where(upper, ahead, behind),
+        jnp.where(upper, table_ref[head, 31], ahead),
+    ]
 
 
 def bias_rows(table_ref, tiles, head, block):
@@ -88,11 +99,9 @@
     return jnp.where((lane >= head * size) & (lane < (head + 1) * size), values, jnp.zeros_like(values))
 
 
-def attend_kernel(heads, size, table_ref, tokens_ref, gain_ref, wq_ref, wk_ref, wv_ref, normed_ref, q_ref, k_ref, v_ref, mixed_ref, total_ref):
+def attend_kernel(heads, size, table_ref, tokens_ref, gain_ref, wq_ref, wk_ref, wv_ref, q_ref, k_ref, v_ref, mixed_ref, total_ref):
     values = tokens_ref[...].astype(F32)
-    normed = (values * inv_rms_of(values) * gain_ref[0:1, :]).astype(BF16)
-    normed_ref[...] = normed
-    normed_ref.leave()
+    normed = (values * inv_rms_of(values) * gain_ref[...].astype(F32).reshape(1, -1)).astype(BF16)
     q_ref[...] = dot_t(normed, wq_ref[...]).astype(BF16)
     q_ref.leave()
     k_ref[...] = dot_t(normed, wk_ref[...]).astype(BF16)
@@ -211,7 +220,7 @@
     return call(
         functools.partial(attend_kernel, heads, columns // heads),
         "attend",
-        ((tokens.shape, BF16), small, small, small, small, ((rows, TILE), F32)),
+        (small, small, small, small, ((rows, TILE), F32)),
         (table,),
         (tokens, gains, *weights),
     )
@@ -220,7 +229,7 @@
 def hidden_kernel(tensor_ref, place_ref, tokens_ref, mixed_ref, weight_ref, gain_ref, router_ref, routes_ref, cot_ref, hidden_ref, own_ref, gate_ref, both):
     width = tokens_ref.shape[1]
     experts = router_ref.shape[0]
-    gain = gain_ref[1:2, :]
+    gain = gain_ref[...].astype(F32).reshape(1, -1)
     for block in range(tokens_ref.shape[0] // TILE):
         rows = pl.ds(block * TILE, TILE)
         hidden = tokens_ref[rows, :].astype(F32)
@@ -246,7 +255,7 @@
     return exponent / jnp.sum(exponent, axis=-1, keepdims=True)
 
 
-def expert_kernel(me_ref, f_a, b_a, f_b, b_b, in_ref, out_ref, router_ref, keep_ref, send_ref, active_ref, pre_ref, grad_ref):
+def expert_kernel(me_ref, f_b, in_ref, b_b, out_ref, router_ref, f_a, b_a, keep_ref, send_ref, keep_r_ref, send_r_ref, active_ref, pre_ref, grad_ref):
     rows = f_a.shape[0]
     experts = router_ref.shape[0]
     lane = lax.broadcasted_iota(jnp.int32, (rows, experts), 1)
@@ -272,8 +281,12 @@
         if place == 0:
             send_ref[...] = back.astype(BF16)
             send_ref.leave()
+            send_r_ref[...] = dot(active, out_ref[...]).astype(BF16)
+            send_r_ref.leave()
         else:
             keep_ref[...] = back
+            keep_ref.leave()
+            keep_r_ref[...] = dot(active, out_ref[...])
         part = t_dot(grad_logits, forward[...])
         total = part if total is None else total + part
     grad_ref[...] = total
@@ -286,21 +299,14 @@
         expert_kernel,
         "expert_pair",
         (
-            ((rows, width), F32), ((rows, width), BF16), ((2 * rows, hidden), BF16), ((2 * rows, hidden), BF16),
+            ((rows, width), F32), ((rows, width), BF16), ((rows, width), F32), ((rows, width), BF16),
+            ((2 * rows, hidden), BF16), ((2 * rows, hidden), BF16),
             (router.shape, F32),
         ),
         (me,),
-        (*first, *second, weight_in, weight_out, router),
-
-    )
-
-
-def result_kernel(active_a, active_b, out_ref, keep_ref, send_ref):
-    rows = active_a.shape[0] // 2
-    for place, active in enumerate((active_a, active_b)):
-        where = pl.ds(place * rows, rows)
-        keep_ref[where, :] = dot(active[pl.ds(0, rows), :], out_ref[...])
-        send_ref[where, :] = dot(active[pl.ds(rows, rows), :], out_ref[...]).astype(BF16)
+        (second[0], weight_in, second[1], weight_out, router, *first),
+
+    )
 
 
 def expert_grad_kernel(f0, f1, f2, f3, b0, b1, b2, b3, active_a, active_b, pre_a, pre_b, in_ref, out_ref):
@@ -313,18 +319,26 @@
     out_ref[...] = t_dot(active, backward)
 
 
-def back_kernel(
-    heads, size, table_ref, core_ref, place_ref, r0, r1, r2, r3, hidden_ref, cot_ref, gain_ref, wo_ref, mixed_ref,
-    normed_ref, q_ref, k_ref, v_ref, total_ref, wq_ref, wk_ref, wv_ref, router_a, router_b,
-    grad_ref, sums_ref, keep_ref, send_ref, small_ref, gm_ref, attn_ref, qb_ref, kacc, vacc, part_ref,
+def packed(rows, count):
+    size = rows.shape[0] // count
+    return jnp.concatenate([rows[n * size : (n + 1) * size] for n in range(count)], axis=1)
+
+
+def unpacked(rows, count):
+    size = rows.shape[1] // count
+    return jnp.concatenate([rows[:, n * size : (n + 1) * size] for n in range(count)], axis=0)
+
+
+def hidden_back_kernel(
+    devices, place_ref, hidden_ref, r0, r1, r2, r3, cot_ref, gain_ref, wo_ref, mixed_ref,
+    grad_ref, gm_ref, turned_ref, norm_ref, sums_ref, attn_ref,
 ):
     tok_rows, width = hidden_ref.shape
-    columns = q_ref.shape[1]
+    columns = mixed_ref.shape[1]
     chunk = r0.shape[0]
-    gain = gain_ref[1:2, :]
-    count = LEN // TILE
+    gain = gain_ref[...].astype(F32).reshape(1, -1)
     norm_part = None
-    for block in range(count):
+    for block in range(tok_rows // TILE):
         rows = pl.ds(block * TILE, TILE)
         place = place_ref[rows, :]
         back = None
@@ -342,9 +356,34 @@
         attn_ref[rows, :] = low
         gm_ref[rows, :] = dot_t(low, wo_ref[...]).astype(BF16)
     grad_ref.leave()
+    gm_ref.leave()
+    unit = lax.broadcasted_iota(jnp.int32, (columns, columns), 0)
+    unit = (unit == lax.broadcasted_iota(jnp.int32, (columns, columns), 1)).astype(BF16)
+    sums = dot(dot_t(unit, mixed_ref[...]).astype(BF16), attn_ref[...]).T
+    if devices == PAIRED:
+        size = width // devices
+        sums = jnp.concatenate([packed(sums[n * size : (n + 1) * size], 4) for n in range(devices)], axis=0)
+    sums_ref[...] = sums.astype(BF16)
+    sums_ref.leave()
+    turned_ref[...] = dot_t(wo_ref[...], attn_ref[...]).astype(BF16)
+    norm_ref[...] = norm_part
+
+
+def back_kernel(
+    heads, size, devices, table_ref, core_ref, q_ref, k_ref, v_ref, gm_ref, turned_ref, total_ref,
+    tokens_ref, gain_ref, wq_ref, wk_ref, wv_ref, router_a, router_b, norm_ref,
+    sums_ref, keep_ref, send_ref, small_ref, back_t, turn_t, part_ref, normed_ref, qb_ref,
+):
+    tok_rows, width = tokens_ref.shape
+    columns = q_ref.shape[1]
+    count = LEN // TILE
     keys, all_values = k_ref[...], v_ref[...]
-    kacc[...] = jnp.zeros_like(kacc)
-    vacc[...] = jnp.zeros_like(vacc)
+    back_t[...] = jnp.zeros_like(back_t)
+    inputs = tokens_ref[...].astype(F32)
+    inv_first = inv_rms_of(inputs)
+    normed_ref[...] = (inputs * inv_first * gain_ref[...].astype(F32).reshape(1, -1)).astype(BF16)
+    turn_t[pl.ds(0, columns), :] = dot_t(wq_ref[...], normed_ref[...]).astype(BF16)
+    turn_t[pl.ds(columns, columns), :] = turned_ref[...]
     all_tiles = [bias_tiles(table_ref, head) for head in range(heads)]
     head_keys = [head_columns(keys, head, size) for head in range(heads)]
     near = [[None] * 3 for _ in range(heads)]
@@ -364,8 +403,10 @@
             score_grad = (probs * (probs_grad - inner)).astype(BF16)
             part = dot(score_grad, head_keys[head])
             query_back = part if query_back is None else query_back + part
-            kacc[...] += t_dot(score_grad, head_queries)
-            vacc[...] += t_dot(probs.astype(BF16), head_grads)
+            mine = pl.ds(head * size, size)
+            back_t[mine, :] += dot(turn_t[mine, rows], score_grad)
+            mine = pl.ds(columns + head * size, size)
+            back_t[mine, :] += dot(turn_t[mine, rows], probs.astype(BF16))
             wide = score_grad.astype(F32)
             for other in range(count):
                 offset = other - block
@@ -379,68 +420,78 @@
                     held = far[head][side]
                     far[head][side] = summed if held is None else held + summed
         qb_ref[rows, :] = query_back.astype(BF16)
-    key_back, value_back = kacc[...].astype(BF16), vacc[...].astype(BF16)
     query_back = qb_ref[...]
-    part_ref[...] = dot(query_back, wq_ref[...]) + dot(key_back, wk_ref[...]) + dot(value_back, wv_ref[...])
+    key_t = back_t[pl.ds(0, columns), :].astype(BF16)
+    value_t = back_t[pl.ds(columns, columns), :].astype(BF16)
+    part_ref[...] = dot(query_back, wq_ref[...]) + t_dot(key_t, wk_ref[...]) + t_dot(value_t, wv_ref[...])
     half = tok_rows // 2
-    extra = keep_ref.shape[0] - half
     core = core_ref[0, 0]
-    keep_ref[pl.ds(0, half), :] = part_ref[pl.ds(pl.multiple_of(core * half, half), half), :]
-    send_ref[pl.ds(0, half), :] = part_ref[pl.ds(pl.multiple_of((1 - core) * half, half), half), :].astype(BF16)
-    router = (router_a[...] + router_b[...]).astype(BF16).astype(F32)
-    if extra > router.shape[0]:
-        router = jnp.concatenate([router, jnp.zeros((extra - router.shape[0], width), F32)], axis=0)
-    keep_ref[pl.ds(half, extra), :] = router
-    send_ref[pl.ds(half, extra), :] = router.astype(BF16)
+    keep_ref[...] = part_ref[pl.ds(pl.multiple_of(core * half, half), half), :]
+    keep_ref.leave()
+    send_ref[...] = part_ref[pl.ds(pl.multiple_of((1 - core) * half, half), half), :].astype(BF16)
     send_ref.leave()
-    keep_ref.leave()
-    empty = jnp.zeros((tok_rows, columns), BF16)
-    sums_ref[:, : 2 * columns] = t_dot(
-        normed_ref[...], jnp.concatenate([query_back, key_back], axis=1)
-    ).astype(BF16)
-    sums_ref[:, 2 * columns :] = (
-        t_dot(normed_ref[...], jnp.concatenate([value_back, empty], axis=1))
-        + t_dot(attn_ref[...], jnp.concatenate([empty, mixed_ref[...]], axis=1))
-    ).astype(BF16)
+    bias_row = jnp.concatenate([bias_sums(heads, near, far), jnp.zeros((8, width - TILE), F32)], axis=1)
+    norm_row = jnp.broadcast_to(jnp.sum(norm_ref[...], axis=0, keepdims=True), (8, width))
+    first_part = jnp.sum(part_ref[...] * tokens_ref[...].astype(F32) * inv_first, axis=0, keepdims=True)
+    line = lax.broadcasted_iota(jnp.int32, (8, width), 0)
+    lines = jnp.where(line == 0, first_part, jnp.where(line == 1, norm_row, jnp.where(line == 2, bias_row, 0.0)))
+    small = jnp.concatenate([router_a[...] + router_b[...], lines], axis=0)
+    small_ref[...] = small
+    small_ref.leave()
+    unit = lax.broadcasted_iota(jnp.int32, (columns, columns), 0)
+    unit = (unit == lax.broadcasted_iota(jnp.int32, (columns, columns), 1)).astype(BF16)
+    turned = (dot_t(unit, query_back).astype(BF16), key_t, value_t)
+    parts = [dot(rows, normed_ref[...]) for rows in turned]
+    sums = jnp.concatenate(parts, axis=0).T
+    if devices == PAIRED:
+        size = width // devices
+        blocks = [sums[n * size : (n + 1) * size] for n in range(devices)]
+        sums = jnp.concatenate(
+            [
+                piece
+                for block in blocks
+                for piece in (packed(block[:, : 2 * columns], 2), packed(block[:, 2 * columns :], 4), small)
+            ],
+            axis=0,
+        )
+    sums_ref[...] = sums.astype(BF16)
     sums_ref.leave()
-    bias = bias_sums(heads, near, far)
-    bias_row = lax.dot_general(
-        jnp.ones((8, TILE), F32), bias, (((1,), (1,)), ((), ())),
-        precision=lax.Precision.HIGHEST, preferred_element_type=F32,
-    )
-    bias_row = jnp.concatenate([bias_row, jnp.zeros((8, width - heads * BUCKETS), F32)], axis=1)
-    norm_row = jnp.broadcast_to(jnp.sum(norm_part, axis=0, keepdims=True), (8, width))
-    line = lax.broadcasted_iota(jnp.int32, (8, width), 0)
-    small_ref[...] = jnp.where(line == 0, norm_row, jnp.where(line == 1, bias_row, 0.0))
 
 
 def bias_sums(heads, near, far):
-    row = lax.broadcasted_iota(jnp.int32, (TILE, TILE), 0)
-    col = lax.broadcasted_iota(jnp.int32, (TILE, TILE), 1)
-
-    def fold(values):
-        return jnp.sum(values.reshape(TILE // 8, 8, TILE), axis=0)
-
+    upper = lax.broadcasted_iota(jnp.int32, (TILE, TILE), 1) >= lax.broadcasted_iota(jnp.int32, (TILE, TILE), 0)
     edges = tuple(range(8)) + (8,) + THRESHOLDS + (1 << 20,)
-    pieces = []
+    lane = lax.broadcasted_iota(jnp.int32, (TILE, TILE), 0)
+    place = lax.broadcasted_iota(jnp.int32, (TILE, TILE), 1)
+    total = jnp.zeros((8, TILE), F32)
+
+    def bucket(distance):
+        found = jnp.zeros((TILE, TILE), jnp.int32)
+        for n in range(1, 16):
+            found = jnp.where(distance >= edges[n], n, found)
+        return found
+
     for head in range(heads):
-        for sign in (0, 1):
-            for n in range(16):
-                piece = jnp.zeros((8, TILE), F32)
-                for offset in ((-1, 0) if sign == 0 else (0, 1)):
-                    low = 0 if offset == 0 else 1
-                    if edges[n + 1] <= low or edges[n] > (TILE - 1 if offset == 0 else 2 * TILE - 1):
-                        continue
-                    shift = col - row + offset * TILE
-                    distance = jnp.abs(shift)
-                    inside = (distance >= edges[n]) & (distance < edges[n + 1])
-                    if offset == 0:
-                        inside = inside & ((shift > 0) if sign else (shift <= 0))
-                    piece = piece + fold(jnp.where(inside, near[head][offset + 1], 0.0))
-                if n == 15:
-                    piece = piece + far[head][sign]
-                pieces.append(jnp.sum(piece, axis=0, keepdims=True))
-    return jnp.concatenate(pieces, axis=0)
+        before, here, beyond = near[head]
+        start = head * BUCKETS
+        ahead = diagonal_sums(jnp.where(upper, here, beyond))
+        behind = diagonal_sums(jnp.where(upper, before, here))
+        outside = (
+            jnp.sum(jnp.where(upper, 0.0, before), axis=0, keepdims=True) + jnp.sum(far[head][0], axis=0, keepdims=True),
+            jnp.sum(jnp.where(upper, beyond, 0.0), axis=0, keepdims=True) + jnp.sum(far[head][1], axis=0, keepdims=True),
+        )
+        targets = (
+            start + jnp.where(lane == 0, 0, 16 + bucket(lane)),
+            start + bucket(TILE - lane),
+            jnp.full((TILE, TILE), start + 15, jnp.int32),
+            jnp.full((TILE, TILE), start + 31, jnp.int32),
+        )
+        for row, target in zip((ahead, behind, *outside), targets):
+            total = total + lax.dot_general(
+                jnp.broadcast_to(row, (8, TILE)), (place == target).astype(F32), (((1,), (0,)), ((), ())),
+                precision=lax.Precision.HIGHEST, preferred_element_type=F32,
+            )
+    return total
 
 
 def swap(values, axis, mask):
@@ -462,11 +513,9 @@
     return lax.optimization_barrier((values, done))[0]
 
 
-def sum_expert(values, done):
+def sum_expert(values):
     mask = 1
     while mask < lax.axis_size("expert"):
-        if 2 * mask >= lax.axis_size("expert"):
-            values = after(values, done)
         values = values + swap(values, "expert", mask)
         mask = 2 * mask
     return values
@@ -495,7 +544,8 @@
     columns = w_query.shape[1]
     chunk_rows = experts * quarter
     half = tok_rows // 2
-    extra = max(16, experts)
+    devices = lax.axis_size("expert")
+    paired = devices == PAIRED
     my_tensor = lax.axis_index("tensor")
     my_expert = lax.axis_index("expert").astype(jnp.int32).reshape(1, 1)
     core = (my_tensor & 1).astype(jnp.int32)
@@ -504,9 +554,8 @@
     router = w_router.T
     weights = (w_query.T, w_key.T, w_value.T)
     table = bias_table.T.astype(F32)
-    gains = jnp.stack([norm_first, norm_second]).astype(F32)
-
-    normed, queries, keys, values, mixed, totals = attend(tokens, gains, weights, table, heads_here)
+
+    queries, keys, values, mixed, totals = attend(tokens, norm_first, weights, table, heads_here)
 
     chosen = routes[:, 0]
     route_hot = chosen[:, None] == jnp.arange(experts, dtype=jnp.int32)[None, :]
@@ -524,7 +573,7 @@
         (((tok_rows, width), F32), ((chunk_rows, 2 * width), BF16), ((tok_rows, TILE), F32)),
         (my_tensor.astype(jnp.int32).reshape(1, 1),),
         (
-            place[None, :], tokens, gather_tensor(after(mixed, output_parts[2])), output_parts, gains, router,
+            place[None, :], tokens, gather_tensor(after(mixed, output_parts[2])), output_parts, norm_second, router,
             routes, cotangent,
         ),
         scratch=(((tok_rows, 2 * width), BF16),),
@@ -534,30 +583,24 @@
     forward_far, backward_far = swap(forward, "tensor", 2), swap(backward, "tensor", 2)
     forward_near, backward_near = swap(forward, "tensor", 1), swap(backward, "tensor", 1)
 
-    keep_a, send_a, active_a, pre_a, router_a = expert_pair(
+    keep_a, send_a, kept_result, send_result, active_a, pre_a, router_a = expert_pair(
         my_expert, (forward, backward), (forward_near, backward_near), weight_in, weight_out, router
     )
     forward_diag = swap(after(forward_far, active_a), "tensor", 1)
     backward_diag = swap(after(backward_far, active_a), "tensor", 1)
     got_a = swap(send_a, "tensor", 1)
-    keep_b, send_b, active_b, pre_b, router_b = expert_pair(
+    keep_b, send_b, far_result, far_send, active_b, pre_b, router_b = expert_pair(
         my_expert, (forward_far, backward_far), (forward_diag, backward_diag), weight_in, weight_out, router
     )
     other = (keep_b + swap(send_b, "tensor", 1).astype(F32)).astype(BF16)
     other_back = swap(other, "tensor", 2)
 
-    keep_r, send_r = call(
-        result_kernel,
-        "expert_result",
-        (((2 * chunk_rows, width), F32), ((2 * chunk_rows, width), BF16)),
-        (),
-        (after(active_a, other), active_b, weight_out),
-    )
     own_back = ((keep_a + got_a.astype(F32)) + other_back.astype(F32)).astype(BF16)
-    own_back = after(own_back, send_r)
     home = exchange_expert(own_back.reshape(experts, quarter, width)).reshape(chunk_rows, width)
-    got_r = swap(send_r, "tensor", 1).astype(F32)
-    far_result = swap((keep_r[chunk_rows:] + got_r[chunk_rows:]).astype(BF16), "tensor", 2)
+
+    far_result = (far_result + swap(after(far_send, other), "tensor", 1).astype(F32)).astype(BF16)
+    kept_result = kept_result + swap(after(send_result, other), "tensor", 1).astype(F32)
+    other_result = swap(after(far_result, own_back), "tensor", 2)
     grad_expert_in, grad_expert_out = call(
         expert_grad_kernel,
         "expert_grads",
@@ -565,67 +608,101 @@
         (),
         (
             forward, forward_near, forward_far, forward_diag, backward, backward_near, backward_far, backward_diag,
-            after(active_a, got_r), active_b, pre_a, pre_b,
-        ),
-    )
-    own_result = ((keep_r[:chunk_rows] + got_r[:chunk_rows]) + far_result.astype(F32)).astype(BF16)
+            after(active_a, own_back), active_b, pre_a, pre_b,
+        ),
+    )
+    own_result = (kept_result + other_result.astype(F32)).astype(BF16)
     home = after(home, (own_result, grad_expert_in))
-    result = exchange_expert(after(own_result, home).reshape(experts, quarter, width)).reshape(chunk_rows, width)
     home_far = swap(home, "tensor", 2)
-    returned_back = (home, swap(home, "tensor", 1), home_far, after(swap(home_far, "tensor", 1), result))
-
-    small = ((8, width), F32)
-    grad_hidden, sums, keep, send, small = call(
-        functools.partial(back_kernel, heads_here, columns // heads_here),
+    returned_back = (home, swap(home, "tensor", 1), home_far, swap(home_far, "tensor", 1))
+
+    grad_hidden, grad_mixed, turned, norm_part, output_sums = call(
+        functools.partial(hidden_back_kernel, devices),
+        "hidden_back",
+        (
+            ((tok_rows, width), F32), ((tok_rows, columns), BF16), ((columns, tok_rows), BF16), ((8, width), F32),
+            ((width // 4, 4 * columns) if paired else (width, columns), BF16),
+        ),
+        (),
+        (place[:, None], hidden, *returned_back, cotangent, norm_second, w_output, mixed),
+        scratch=(((tok_rows, width), BF16),),
+    )
+
+    own_result = own_result.reshape(experts, quarter, width)
+    if paired:
+        both = exchange_expert(
+            jnp.concatenate([own_result, output_sums.reshape(experts, quarter, width)], axis=1)
+        )
+        result, output_sums = both[:, :quarter].reshape(chunk_rows, width), both[:, quarter:]
+    else:
+        result = exchange_expert(own_result).reshape(chunk_rows, width)
+        both = output_sums = exchange_expert(output_sums.reshape(devices, -1, columns))
+    sums, keep, send, small = call(
+        functools.partial(back_kernel, heads_here, columns // heads_here, devices),
         "layer_back",
         (
-            ((tok_rows, width), F32), ((width, 4 * columns), BF16), ((half + extra, width), F32),
-            ((half + extra, width), BF16), ((8, width), F32),
+            ((3 * width // 4 + devices * (experts + 8), 4 * columns) if paired else (width, 3 * columns), BF16),
+            ((half, width), F32), ((half, width), BF16), ((experts + 8, width), F32),
         ),
         (table, core.reshape(1, 1)),
         (
-            place[:, None], *returned_back, hidden, cotangent, gains, w_output, mixed, normed,
-            queries, keys, values, totals, *weights, router_a, router_b,
+            queries, keys, values, grad_mixed, turned, totals, tokens, norm_first, *weights,
+            router_a, router_b, norm_part,
         ),
         scratch=(
-            ((tok_rows, columns), BF16), ((tok_rows, width), BF16), ((tok_rows, columns), BF16),
-            ((tok_rows, columns), F32), ((tok_rows, columns), F32), ((tok_rows, width), F32),
-        ),
-    )
+            ((2 * columns, tok_rows), F32), ((2 * columns, tok_rows), BF16), ((tok_rows, width), F32),
+            ((tok_rows, width), BF16), ((tok_rows, columns), BF16),
+        ),
+    )
+    sums, keep, send, small = lax.optimization_barrier((sums, keep, send, small, both))[:4]
+
+    sums = exchange_expert(sums.reshape(devices, -1, sums.shape[1]))
 
     pair = (keep + swap(send, "tensor", 1).astype(F32)).astype(BF16)
     total = (pair.astype(F32) + swap(pair, "tensor", 2).astype(F32)).astype(BF16)
-    near = swap(total[:half], "tensor", 1)
-    low = jnp.where(core == 1, near, total[:half]).astype(F32)
-    high = jnp.where(core == 1, total[:half], near).astype(F32)
+    result_far = swap(after(result, total), "tensor", 2)
+
+    grads = jnp.sum(sums.astype(F32), axis=0)
+    grad_output = jnp.sum(output_sums.astype(F32), axis=0)
+    if paired:
+        split = width // PAIRED // 2
+        small = grads[3 * split // 2 :]
+        grads = jnp.concatenate([unpacked(grads[:split], 2), unpacked(grads[split : 3 * split // 2], 4)], axis=1)
+        grad_output = unpacked(grad_output, 4)
+    else:
+        small = sum_expert(small)
+
+    near = swap(total, "tensor", 1)
+    low = jnp.where(core == 1, near, total).astype(F32)
+    high = jnp.where(core == 1, total, near).astype(F32)
     normed_back = jnp.concatenate([low, high])
     inputs = tokens.astype(F32)
-    inv_first = inv_rms_of(inputs)
-    gain_first = gains[0:1]
-    norm_first_part = jnp.sum(normed_back * inputs * inv_first, axis=0, keepdims=True)
-    grad_tokens = grad_hidden + rms_norm_back(inputs, inv_first, gain_first, normed_back)
-
-    returned = gather_tensor(after(result, total))
+    grad_tokens = grad_hidden + rms_norm_back(
+        inputs, inv_rms_of(inputs), norm_first.astype(F32)[None, :], normed_back
+    )
+
+    returned = (result, swap(after(result, total), "tensor", 1), result_far, swap(result_far, "tensor", 1))
     place_hot = (
         place[:, None] == jnp.arange(TENSOR * chunk_rows, dtype=jnp.int32)[None, :]
     ).astype(BF16)
     layer_out = (hidden + gate[:, :1] * dot(place_hot, jnp.concatenate(returned))).astype(BF16)
 
-    grads = exchange_expert(sums.reshape(lax.axis_size("expert"), -1, 4 * columns))
-    grads = jnp.sum(grads.astype(F32), axis=0)
-    small = sum_expert(jnp.concatenate([total[half : half + experts].astype(F32), norm_first_part, small[:2]]), grads)
+    summed = small[: experts + 1]
+    summed = after(summed, result_far)
+    summed = summed + swap(summed, "tensor", 1)
+    summed = summed + swap(summed, "tensor", 2)
     bias_size = BUCKETS * heads_here
     return (
         layer_out,
         grad_tokens,
-        small[experts],
+        summed[experts],
         grads[:, :columns],
         grads[:, columns : 2 * columns],
-        grads[:, 2 * columns : 3 * columns],
-        grads[:, 3 * columns :].T,
+        grads[:, 2 * columns :],
+        grad_output.T,
         small[experts + 2, :bias_size].reshape(heads_here, BUCKETS).T,
         small[experts + 1],
-        small[:experts].T,
+        summed[:experts].T,
         grad_expert_in[None],
         grad_expert_out[None],
     )

time: 194 us -> 187 us (0.964)
  waiting for transfers between devices: 61.9 us -> 58.5 us
  local copies, waits for them, and re-layouts: 11.2 us -> 8.05 us
  Pallas kernels: 58.7 us -> 56.4 us
    ppermute x29, waiting for transfers between devices: 54.3 us -> 47.3 us  [swap(): return lax.ppermute(values, axis, [(i, i ^ mask) for i in range(size)])]
    all_to_all x3, waiting for transfers between devices: 7.55 us -> 11.2 us  [exchange_expert(): lax.all_to_all(blocks, 'expert', split_axis=0, concat_axis=0, tiled=True)]
    concatenate x1 -> x2, other arithmetic: 0.01 us -> 2.56 us  [the longest x1 1.82 us: on_device(): jnp.concatenate([own_result, output_sums.reshape(experts, quarter, width)...]
    pallas_call x7, Pallas kernels: 58.7 us -> 56.4 us  [call(): pl.pallas_call(body, out_shape=tuple((jax.ShapeDtypeStruct(shape, kind) f...]
    unnamed x54 -> x60, local copies, waits for them, and re-layouts: 4.73 us -> 4.63 us
  transfers between devices with their start and end apart: 32 -> 32, of which waited for: 16 -> 17; matrix products, arithmetic and copies ran while one was open for 8% -> 7% of each run, Pallas kernels for 12% -> 19%
where the time goes in v1:
time: 187 us; the launch traced here: 186 us
  waiting for transfers between devices  58.5 us (31%)
  Pallas kernels  56.4 us (30%)
  starting transfers between devices  26.4 us (14%)
  blocking collectives  22.6 us (12%)
  other arithmetic  11.1 us (6%)
  local copies, waits for them, and re-layouts  8.05 us (4%)
  matrix products  2.04 us (1%)
    pallas_call x7, Pallas kernels, call(): pl.pallas_call(body, out_shape=tuple((jax.ShapeDtypeStruct(shape, kind) f...  56.4 us
    ppermute x29, waiting for transfers between devices, swap(): return lax.ppermute(values, axis, [(i, i ^ mask) for i in range(size)])  47.3 us
    all_to_all x1, blocking collectives, exchange_expert(): lax.all_to_all(blocks, 'expert', split_axis=0, concat_axis=0, tiled=True)  22.6 us
    ppermute x29, starting transfers between devices, swap(): return lax.ppermute(values, axis, [(i, i ^ mask) for i in range(size)])  13.8 us
    all_to_all x3, starting transfers between devices, exchange_expert(): lax.all_to_all(blocks, 'expert', split_axis=0, concat_axis=0, tiled=True)  12.6 us
    all_to_all x3, waiting for transfers between devices, exchange_expert(): lax.all_to_all(blocks, 'expert', split_axis=0, concat_axis=0, tiled=True)  11.2 us
    unnamed x60, local copies, waits for them, and re-layouts  4.63 us
  transfers between devices with their start and end apart: 32, of which 17 were waited for; matrix products, arithmetic and copies ran while one was open for 7% of the time, Pallas kernels for 19%

profile of v1, /device:TPU:0, one launch (start us, length us, event | category | flops | bytes accessed | tf_op | source)
XLA Modules:
  0.0 186.3 jit_solution(640077016161466148)
XLA Ops:
  0.7 3.0 %collective-permute-start = (bf16[192,768]{1,0:T(8,128)(2,1)}, bf16[192,768]{1,0:T(8,128)(2,1)S(1)}, u32[]{:S(2)}, u32[]{:S(2)}) collective-permute-start(bf16[192,768]{1,0:T(8,128)(2,1)} %refs_8_.2), channel_id=1, source_target_pairs={{0,2},{1,3},{2,0},{3,1},{4,6},{5,7},{6,4},{7,5},{8,10},{9,11},{10,... | collective-permute-start | bytes 884744 | tf_op jit(solution)/shard_map/ppermute | solution.py:499
  3.7 1.3 convert_bitcast_fusion.refs_0_
  4.9 7.7 %attend.1 = (bf16[512,192]{1,0:T(8,128)(2,1)}, bf16[512,192]{1,0:T(8,128)(2,1)}, bf16[512,192]{1,0:T(8,128)(2,1)}, bf16[512,192]{1,0:T(8,128)(2,1)}, f32[512,128]{1,0:T(8,128)}) custom-call(f32[3,32]{1,0:T(4,128)} %convert_bitcast_fusion.refs_0_, bf16[512,768]{1,0:T(8,128)(2,1)} %refs_8_.3, bf16[768]{0:T(1024)(128)(2,1)} %refs_9_.1, ...), custom_call_target="tpu_custom_call" | custom-call | flops 100000 | bytes 10000 | tf_op jit(solution)/shard_map/attend/pallas_call | solution.py:203
  13.7 0.8 copy.52.refs_13_
  14.5 7.5 %collective-permute-done.2.refs_5_ = bf16[512,192]{1,0:T(8,128)(2,1)S(1)} collective-permute-done((bf16[512,192]{1,0:T(8,128)(2,1)}, bf16[512,192]{1,0:T(8,128)(2,1)S(1)}, u32[]{:S(2)}, u32[]{:S(2)}) %collective-permute-start.2) | collective-permute-done | bytes 196640 | tf_op jit(solution)/shard_map/ppermute | solution.py:499
  22.0 0.6 fusion.19.refs_1_
  22.7 0.8 collective-permute-done.3.refs_6_
  23.6 0.7 copy-done.23
  24.3 6.6 %hidden.1 = (f32[512,768]{1,0:T(8,128)}, bf16[192,1536]{1,0:T(8,128)(2,1)}, f32[512,128]{1,0:T(8,128)}) custom-call(s32[1,1]{1,0:T(1,128)} %bitcast.refs_0_, s32[1,512]{1,0:T(1,128)} %fusion.19.refs_1_, bf16[512,768]{1,0:T(8,128)(2,1)} %refs_8_.3, bf16[512,192]{1,0:T(8,128)(2,1)} %get-tuple-element.58.refs_3_.refs_9_, bf16[512,192]{1,0:T(8,128)(2,1)} %copy-done.22, ...), custom_call_target="tpu_custom_call" | custom-call | flops 100000 | bytes 10000 | tf_op jit(solution)/shard_map/hidden/pallas_call | solution.py:203
  30.9 22.6 %all_to_all.20 = bf16[8,24,1536]{2,1,0:T(8,128)(2,1)S(1)} all-to-all(bf16[8,24,1536]{2,1,0:T(8,128)(2,1)} %bitcast.52), channel_id=1, replica_groups=mesh['expert'=8,'tensor'=4] {'expert'}, dimensions={0} | all-to-all | bytes 1179648 | tf_op jit(solution)/shard_map/all_to_all | solution.py:509
  54.6 1.5 collective-permute-start.10
  56.2 0.7 copy-done.5
  57.0 7.6 %expert_pair.2 = (f32[192,768]{1,0:T(8,128)}, bf16[192,768]{1,0:T(8,128)(2,1)}, f32[192,768]{1,0:T(8,128)}, bf16[192,768]{1,0:T(8,128)(2,1)}, bf16[384,768]{1,0:...) custom-call(s32[1,1]{1,0:T(1,128)} %bitcast.12.refs_0_, bf16[192,768]{1,0:T(8,128)(2,1)} %copy-done.5, ...), custom_call_target="tpu_custom_call" | custom-call | flops 100000 | bytes 10000 | tf_op jit(solution)/shard_map/expert_pair/pallas_call | solution.py:203
  64.7 4.7 %collective-permute-done.10.refs_7_.refs_6_ = bf16[192,768]{1,0:T(8,128)(2,1)S(1)} collective-permute-done((bf16[192,768]{1,0:T(8,128)(2,1)S(1)}, bf16[192,768]{1,0:T(8,128)(2,1)S(1)}, u32[]{:S(2)}, u32[]{:S(2)}) %collective-permute-start.10) | collective-permute-done | bytes 294944 | tf_op jit(solution)/shard_map/ppermute | solution.py:499
  69.5 1.6 collective-permute-done.11.refs_3_.refs_7_
  71.1 0.7 copy-done.10
  71.8 7.6 %expert_pair.3 = (f32[192,768]{1,0:T(8,128)}, bf16[192,768]{1,0:T(8,128)(2,1)}, f32[192,768]{1,0:T(8,128)}, bf16[192,768]{1,0:T(8,128)(2,1)}, bf16[384,768]{1,0:...) custom-call(s32[1,1]{1,0:T(1,128)} %bitcast.12.refs_0_, bf16[192,768]{1,0:T(8,128)(2,1)} %copy-done.9, ...), custom_call_target="tpu_custom_call" | custom-call | flops 100000 | bytes 10000 | tf_op jit(solution)/shard_map/expert_pair/pallas_call | solution.py:203
  79.6 1.6 collective-permute-done.12
  81.2 1.1 add_convert_fusion.6
  83.4 0.8 collective-permute-done.14
  84.4 7.6 %collective-permute-done.16 = bf16[192,768]{1,0:T(8,128)(2,1)S(1)} collective-permute-done((bf16[192,768]{1,0:T(8,128)(2,1)S(1)}, bf16[192,768]{1,0:T(8,128)(2,1)S(1)}, u32[]{:S(2)}, u32[]{:S(2)}) %collective-permute-start.16) | collective-permute-done | bytes 294944 | tf_op jit(solution)/shard_map/ppermute | solution.py:499
  92.0 0.8 add_convert_fusion.4
  93.3 3.6 %all-to-all-start.1 = ((bf16[8,24,768]{2,1,0:T(8,128)(2,1)}), bf16[8,24,768]{2,1,0:T(8,128)(2,1)S(1)}, u32[]{:S(2)}, u32[]{:S(2)}) async-start(bf16[8,24,768]{2,1,0:T(8,128)(2,1)} %bitcast.18), calls=%async_computation.1 | async-start | bytes 589824 | tf_op jit(solution)/shard_map/all_to_all | solution.py:509
  97.0 6.8 %expert_grads.1 = (f32[768,768]{1,0:T(8,128)}, f32[768,768]{1,0:T(8,128)}) custom-call(bf16[192,768]{1,0:T(8,128)(2,1)} %copy-done.2, bf16[192,768]{1,0:T(8,128)(2,1)} %copy-done.5, bf16[192,768]{1,0:T(8,128)(2,1)} %copy-done.7, bf16[192,768]{1,0:T(8,128)(2,1)} %copy-done.9, bf16[192,768]{1,0:T(8,128)(2,1)} %copy-done.1, bf16[192,768]{1,0:T(8,128)(2,1)} %copy-done.6, ...), custom_call_target="tpu_custom_call" | custom-call | flops 100000 | bytes 10000 | tf_op jit(solution)/shard_map/expert_grads/pallas_call | solution.py:203
  103.9 1.8 all-to-all-done.1
  105.7 1.5 collective-permute-start.19
  107.8 4.6 %collective-permute-done.19.refs_4_ = bf16[192,768]{1,0:T(8,128)(2,1)S(1)} collective-permute-done((bf16[192,768]{1,0:T(8,128)(2,1)S(1)}, bf16[192,768]{1,0:T(8,128)(2,1)S(1)}, u32[]{:S(2)}, u32[]{:S(2)}) %collective-permute-start.19) | collective-permute-done | bytes 294944 | tf_op jit(solution)/shard_map/ppermute | solution.py:499
  112.6 0.8 fusion.25
  114.1 0.6 copy-done.20
  114.7 6.2 %hidden_back.1 = (f32[512,768]{1,0:T(8,128)}, bf16[512,192]{1,0:T(8,128)(2,1)}, bf16[192,512]{1,0:T(8,128)(2,1)}, f32[8,768]{1,0:T(8,128)}, bf16[192,768]{1,0:T(8,128)(2,1)}) custom-call(s32[512,1]{1,0:T(8,128)} %get-tuple-element.129.refs_0_, f32[512,768]{1,0:T(8,128)} %get-tuple-element.59.refs_1_, bf16[192,768]{1,0:T(8,128)(2,1)} %bitcast.51, ...), custom_call_target="tpu_custom_call" | custom-call | flops 100000 | bytes 10000 | tf_op jit(solution)/shard_map/hidden_back/pallas_call | solution.py:203
  121.0 1.8 pad_maximum_fusion.1
  122.8 5.1 %all-to-all-start.2 = ((bf16[8,48,768]{2,1,0:T(8,128)(2,1)}), bf16[8,48,768]{2,1,0:T(8,128)(2,1)S(1)}, u32[]{:S(2)}, u32[]{:S(2)}) async-start(bf16[8,48,768]{2,1,0:T(8,128)(2,1)} %pad_maximum_fusion.1), calls=%async_computation.2 | async-start | bytes 1179648 | tf_op jit(solution)/shard_map/all_to_all | solution.py:509
  127.9 13.9 %layer_back.1 = (bf16[704,768]{1,0:T(8,128)(2,1)}, f32[256,768]{1,0:T(8,128)}, bf16[256,768]{1,0:T(8,128)(2,1)}, f32[16,768]{1,0:T(8,128)}) custom-call(f32[3,32]{1,0:T(4,128)} %convert_bitcast_fusion.refs_0_, s32[1,1]{1,0:T(1,128)} %bitcast.22.refs_1_, bf16[512,192]{1,0:T(8,128)(2,1)} %get-tuple-element.83.refs_2_, ...), custom_call_target="tpu_custom_call" | custom-call | flops 100000 | bytes 10000 | tf_op jit(solution)/shard_map/layer_back/pallas_call | solution.py:203
  141.8 2.2 %all-to-all-done.2 = bf16[8,48,768]{2,1,0:T(8,128)(2,1)S(1)} async-done(((bf16[8,48,768]{2,1,0:T(8,128)(2,1)}), bf16[8,48,768]{2,1,0:T(8,128)(2,1)S(1)}, u32[]{:S(2)}, u32[]{:S(2)}) %all-to-all-start.2) | async-done | bytes 589856 | tf_op jit(solution)/shard_map/all_to_all | solution.py:509
  144.1 1.9 %collective-permute-done.21 = bf16[256,768]{1,0:T(8,128)(2,1)S(1)} collective-permute-done((bf16[256,768]{1,0:T(8,128)(2,1)}, bf16[256,768]{1,0:T(8,128)(2,1)S(1)}, u32[]{:S(2)}, u32[]{:S(2)}) %collective-permute-start.21) | collective-permute-done | bytes 393248 | tf_op jit(solution)/shard_map/ppermute | solution.py:499
  146.0 1.2 add_convert_fusion.2
  147.2 1.6 collective-permute-start.22
  148.9 3.9 %all-to-all-start.3 = ((bf16[8,88,768]{2,1,0:T(8,128)(2,1)}), bf16[8,88,768]{2,1,0:T(8,128)(2,1)S(1)}, u32[]{:S(2)}, u32[]{:S(2)}) async-start(bf16[8,88,768]{2,1,0:T(8,128)(2,1)} %bitcast.23), calls=%async_computation.3 | async-start | bytes 2162688 | tf_op jit(solution)/shard_map/all_to_all | solution.py:509
  152.8 5.6 %collective-permute-done.22 = bf16[256,768]{1,0:T(8,128)(2,1)S(1)} collective-permute-done((bf16[256,768]{1,0:T(8,128)(2,1)S(1)}, bf16[256,768]{1,0:T(8,128)(2,1)S(1)}, u32[]{:S(2)}, u32[]{:S(2)}) %collective-permute-start.22) | collective-permute-done | bytes 393248 | tf_op jit(solution)/shard_map/ppermute | solution.py:499
  158.7 1.6 collective-permute-start.24
  160.4 0.7 copy.64
  161.3 6.8 %collective-permute-done.24 = bf16[192,768]{1,0:T(8,128)(2,1)S(1)} collective-permute-done((bf16[192,768]{1,0:T(8,128)(2,1)S(1)}, bf16[192,768]{1,0:T(8,128)(2,1)S(1)}, u32[]{:S(2)}, u32[]{:S(2)}) %collective-permute-start.24) | collective-permute-done | bytes 294944 | tf_op jit(solution)/shard_map/ppermute | solution.py:499
  168.7 1.6 fusion.3
  170.3 1.8 add_convert_fusion
  172.1 7.2 %all-to-all-done.3 = bf16[8,88,768]{2,1,0:T(8,128)(2,1)S(1)} async-done(((bf16[8,88,768]{2,1,0:T(8,128)(2,1)}), bf16[8,88,768]{2,1,0:T(8,128)(2,1)S(1)}, u32[]{:S(2)}, u32[]{:S(2)}) %all-to-all-start.3) | async-done | bytes 1081376 | tf_op jit(solution)/shard_map/all_to_all | solution.py:509
  179.6 0.7 pad_maximum_fusion.2
  181.5 0.7 reshape_squeeze.3
  182.2 2.9 %collective-permute-done.28 = f32[9,768]{1,0:T(8,128)S(1)} collective-permute-done((f32[9,768]{1,0:T(8,128)S(1)}, f32[9,768]{1,0:T(8,128)S(1)}, u32[]{:S(2)}, u32[]{:S(2)}) %collective-permute-start.28) | collective-permute-done | bytes 27680 | tf_op jit(solution)/shard_map/ppermute | solution.py:499
  (127 shorter events, 9.9 us)
Async XLA Ops:
  0.6 12.1 %copy-start.25 = (s32[512,1]{0,1:T(1,128)S(1)}, s32[512,1]{0,1:T(1,128)}, u32[]{:S(2)}) copy-start(s32[512,1]{0,1:T(1,128)} %param.24) | copy-start | bytes 6148
  0.7 12.3 %collective-permute-start = (bf16[192,768]{1,0:T(8,128)(2,1)}, bf16[192,768]{1,0:T(8,128)(2,1)S(1)}, u32[]{:S(2)}, u32[]{:S(2)}) collective-permute-start(bf16[192,768]{1,0:T(8,128)(2,1)} %refs_8_.2), channel_id=1, source_target_pairs={{0,2},{1,3},{2,0},{3,1},{4,6},{5,7},{6,4},{7,5},{8,10},{9,11},{10,... | collective-permute-start | bytes 884744 | tf_op jit(solution)/shard_map/ppermute | solution.py:499
  3.7 19.0 %collective-permute-start.4 = (bf16[192,768]{1,0:T(8,128)(2,1)}, bf16[192,768]{1,0:T(8,128)(2,1)S(1)}, u32[]{:S(2)}, u32[]{:S(2)}) collective-permute-start(bf16[192,768]{1,0:T(8,128)(2,1)} %refs_8_.2), channel_id=1, source_target_pairs={{0,1},{1,0},{2,3},{3,2},{4,5},{5,4},{6,7},{7,6},{8,9},{9,8},{10,11... | collective-permute-start | bytes 884744 | tf_op jit(solution)/shard_map/ppermute | solution.py:499
  13.0 10.6 %copy-start.15 = (bf16[192,768]{1,0:T(8,128)(2,1)}, bf16[192,768]{1,0:T(8,128)(2,1)S(1)}, u32[]{:S(2)}) copy-start(bf16[192,768]{1,0:T(8,128)(2,1)S(1)} %collective-permute-done.refs_9_) | copy-start | bytes 884740
  13.0 9.0 %collective-permute-start.2 = (bf16[512,192]{1,0:T(8,128)(2,1)}, bf16[512,192]{1,0:T(8,128)(2,1)S(1)}, u32[]{:S(2)}, u32[]{:S(2)}) collective-permute-start(bf16[512,192]{1,0:T(8,128)(2,1)} %get-tuple-element.58.refs_3_.refs_9_), channel_id=1, source_target_pairs={{0,2},{1,3},{2,0},{3,1},{4,6},{5,7},{6,4},{7,5},{8,10},{9,11},{10,... | collective-permute-start | bytes 589832 | tf_op jit(solution)/shard_map/ppermute | solution.py:499
  13.2 9.5 %collective-permute-start.5 = (bf16[192,768]{1,0:T(8,128)(2,1)S(1)}, bf16[192,768]{1,0:T(8,128)(2,1)S(1)}, u32[]{:S(2)}, u32[]{:S(2)}) collective-permute-start(bf16[192,768]{1,0:T(8,128)(2,1)S(1)} %collective-permute-done.refs_9_), channel_id=1, source_target_pairs={{0,1},{1,0},{2,3},{3,2},{4,5},{5,4},{6,7},{7,6},{8,9},{9,8},{10,11... | collective-permute-start | bytes 884744 | tf_op jit(solution)/shard_map/ppermute | solution.py:499
  14.5 8.1 %collective-permute-start.1 = (bf16[512,192]{1,0:T(8,128)(2,1)}, bf16[512,192]{1,0:T(8,128)(2,1)S(1)}, u32[]{:S(2)}, u32[]{:S(2)}) collective-permute-start(bf16[512,192]{1,0:T(8,128)(2,1)} %get-tuple-element.58.refs_3_.refs_9_), channel_id=1, source_target_pairs={{0,1},{1,0},{2,3},{3,2},{4,5},{5,4},{6,7},{7,6},{8,9},{9,8},{10,11... | collective-permute-start | bytes 589832 | tf_op jit(solution)/shard_map/ppermute | solution.py:499
  22.0 1.5 collective-permute-start.3
  53.5 2.6 %copy-start.1 = (bf16[192,768]{1,0:T(8,128)(2,1)}, bf16[192,768]{1,0:T(8,128)(2,1)S(1)}, u32[]{:S(2)}) copy-start(bf16[192,768]{1,0:T(8,128)(2,1)S(1)} %get-tuple-element.132.refs_7_.refs_4_) | copy-start | bytes 884740
  53.6 2.6 %copy-start.2 = (bf16[192,768]{1,0:T(8,128)(2,1)}, bf16[192,768]{1,0:T(8,128)(2,1)S(1)}, u32[]{:S(2)}) copy-start(bf16[192,768]{1,0:T(8,128)(2,1)S(1)} %get-tuple-element.133.refs_6_.refs_0_) | copy-start | bytes 884740
  53.6 2.6 %collective-permute-start.6 = (bf16[192,768]{1,0:T(8,128)(2,1)S(1)}, bf16[192,768]{1,0:T(8,128)(2,1)S(1)}, u32[]{:S(2)}, u32[]{:S(2)}) collective-permute-start(bf16[192,768]{1,0:T(8,128)(2,1)S(1)} %get-tuple-element.133.refs_6_.refs_0_), channel_id=1, source_target_pairs={{0,1},{1,0},{2,3},{3,2},{4,5},{5,4},{6,7},{7,6},{8,9},{9,8},{10,11... | collective-permute-start | bytes 884744 | tf_op jit(solution)/shard_map/ppermute | solution.py:499
  53.6 2.5 %collective-permute-start.7 = (bf16[192,768]{1,0:T(8,128)(2,1)S(1)}, bf16[192,768]{1,0:T(8,128)(2,1)S(1)}, u32[]{:S(2)}, u32[]{:S(2)}) collective-permute-start(bf16[192,768]{1,0:T(8,128)(2,1)S(1)} %get-tuple-element.132.refs_7_.refs_4_), channel_id=1, source_target_pairs={{0,1},{1,0},{2,3},{3,2},{4,5},{5,4},{6,7},{7,6},{8,9},{9,8},{10,11... | collective-permute-start | bytes 884744 | tf_op jit(solution)/shard_map/ppermute | solution.py:499
  54.1 10.5 %collective-permute-start.8 = (bf16[192,768]{1,0:T(8,128)(2,1)S(1)}, bf16[192,768]{1,0:T(8,128)(2,1)S(1)}, u32[]{:S(2)}, u32[]{:S(2)}) collective-permute-start(bf16[192,768]{1,0:T(8,128)(2,1)S(1)} %get-tuple-element.133.refs_6_.refs_0_), channel_id=1, source_target_pairs={{0,2},{1,3},{2,0},{3,1},{4,6},{5,7},{6,4},{7,5},{8,10},{9,11},{10,... | collective-permute-start | bytes 884744 | tf_op jit(solution)/shard_map/ppermute | solution.py:499
  54.6 14.8 %collective-permute-start.10 = (bf16[192,768]{1,0:T(8,128)(2,1)S(1)}, bf16[192,768]{1,0:T(8,128)(2,1)S(1)}, u32[]{:S(2)}, u32[]{:S(2)}) collective-permute-start(bf16[192,768]{1,0:T(8,128)(2,1)S(1)} %get-tuple-element.132.refs_7_.refs_4_), channel_id=1, source_target_pairs={{0,2},{1,3},{2,0},{3,1},{4,6},{5,7},{6,4},{7,5},{8,10},{9,11},{10,... | collective-permute-start | bytes 884744 | tf_op jit(solution)/shard_map/ppermute | solution.py:499
  64.6 6.4 %copy-start.7 = (bf16[192,768]{1,0:T(8,128)(2,1)}, bf16[192,768]{1,0:T(8,128)(2,1)S(1)}, u32[]{:S(2)}) copy-start(bf16[192,768]{1,0:T(8,128)(2,1)S(1)} %collective-permute-done.8.refs_6_.refs_2_) | copy-start | bytes 884740
  64.6 17.9 %copy-start.28 = (bf16[192,768]{1,0:T(8,128)(2,1)S(1)}, bf16[192,768]{1,0:T(8,128)(2,1)}, u32[]{:S(2)}) copy-start(bf16[192,768]{1,0:T(8,128)(2,1)} %get-tuple-element.74) | copy-start | bytes 884740
  64.6 18.8 %copy-start.27 = (bf16[192,768]{1,0:T(8,128)(2,1)S(1)}, bf16[192,768]{1,0:T(8,128)(2,1)}, u32[]{:S(2)}) copy-start(bf16[192,768]{1,0:T(8,128)(2,1)} %get-tuple-element.69) | copy-start | bytes 884740
  64.6 4.8 %collective-permute-start.9 = (bf16[192,768]{1,0:T(8,128)(2,1)S(1)}, bf16[192,768]{1,0:T(8,128)(2,1)S(1)}, u32[]{:S(2)}, u32[]{:S(2)}) collective-permute-start(bf16[192,768]{1,0:T(8,128)(2,1)S(1)} %collective-permute-done.8.refs_6_.refs_2_), channel_id=1, source_target_pairs={{0,1},{1,0},{2,3},{3,2},{4,5},{5,4},{6,7},{7,6},{8,9},{9,8},{10,11... | collective-permute-start | bytes 884744 | tf_op jit(solution)/shard_map/ppermute | solution.py:499
  69.5 1.6 collective-permute-start.11
  79.3 4.9 %copy-start.12 = (f32[192,768]{1,0:T(8,128)S(1)}, f32[192,768]{1,0:T(8,128)}, u32[]{:S(2)}) copy-start(f32[192,768]{1,0:T(8,128)} %get-tuple-element.70) | copy-start | bytes 1769476
  79.3 12.6 %copy-start.14 = (f32[192,768]{1,0:T(8,128)S(1)}, f32[192,768]{1,0:T(8,128)}, u32[]{:S(2)}) copy-start(f32[192,768]{1,0:T(8,128)} %get-tuple-element.73) | copy-start | bytes 1769476
  79.4 1.9 collective-permute-start.12
  82.3 1.9 collective-permute-start.14
  82.6 1.9 collective-permute-start.15
  82.9 9.1 %collective-permute-start.16 = (bf16[192,768]{1,0:T(8,128)(2,1)S(1)}, bf16[192,768]{1,0:T(8,128)(2,1)S(1)}, u32[]{:S(2)}, u32[]{:S(2)}) collective-permute-start(bf16[192,768]{1,0:T(8,128)(2,1)S(1)} %add_convert_fusion.6), channel_id=1, source_target_pairs={{0,2},{1,3},{2,0},{3,1},{4,6},{5,7},{6,4},{7,5},{8,10},{9,11},{10,... | collective-permute-start | bytes 884744 | tf_op jit(solution)/shard_map/ppermute | solution.py:499
  83.4 20.4 %collective-permute-start.13 = (bf16[192,768]{1,0:T(8,128)(2,1)S(1)}, bf16[192,768]{1,0:T(8,128)(2,1)S(1)}, u32[]{:S(2)}, u32[]{:S(2)}) collective-permute-start(bf16[192,768]{1,0:T(8,128)(2,1)S(1)} %copy-done.27), channel_id=1, source_target_pairs={{0,1},{1,0},{2,3},{3,2},{4,5},{5,4},{6,7},{7,6},{8,9},{9,8},{10,11... | collective-permute-start | bytes 884744 | tf_op jit(solution)/shard_map/ppermute | solution.py:499
  92.8 11.0 %collective-permute-start.17 = (bf16[192,768]{1,0:T(8,128)(2,1)S(1)}, bf16[192,768]{1,0:T(8,128)(2,1)S(1)}, u32[]{:S(2)}, u32[]{:S(2)}) collective-permute-start(bf16[192,768]{1,0:T(8,128)(2,1)S(1)} %add_convert_fusion.5), channel_id=1, source_target_pairs={{0,2},{1,3},{2,0},{3,1},{4,6},{5,7},{6,4},{7,5},{8,10},{9,11},{10,... | collective-permute-start | bytes 884744 | tf_op jit(solution)/shard_map/ppermute | solution.py:499
  93.3 12.4 %all-to-all-start.1 = ((bf16[8,24,768]{2,1,0:T(8,128)(2,1)}), bf16[8,24,768]{2,1,0:T(8,128)(2,1)S(1)}, u32[]{:S(2)}, u32[]{:S(2)}) async-start(bf16[8,24,768]{2,1,0:T(8,128)(2,1)} %bitcast.18), calls=%async_computation.1 | async-start | bytes 589824 | tf_op jit(solution)/shard_map/all_to_all | solution.py:509
  97.0 6.9 %copy-start.13 = (f32[192,768]{1,0:T(8,128)S(1)}, f32[192,768]{1,0:T(8,128)}, u32[]{:S(2)}) copy-start(f32[192,768]{1,0:T(8,128)} %get-tuple-element.62) | copy-start | bytes 1769476
  105.7 8.3 %copy-start.11 = (bf16[8,24,768]{2,1,0:T(8,128)(2,1)}, bf16[8,24,768]{2,1,0:T(8,128)(2,1)S(1)}, u32[]{:S(2)}) copy-start(bf16[8,24,768]{2,1,0:T(8,128)(2,1)S(1)} %all-to-all-done.1) | copy-start | bytes 884740
  105.7 6.7 %collective-permute-start.19 = (bf16[192,768]{1,0:T(8,128)(2,1)S(1)}, bf16[192,768]{1,0:T(8,128)(2,1)S(1)}, u32[]{:S(2)}, u32[]{:S(2)}) collective-permute-start(bf16[192,768]{1,0:T(8,128)(2,1)S(1)} %bitcast.49), channel_id=1, source_target_pairs={{0,2},{1,3},{2,0},{3,1},{4,6},{5,7},{6,4},{7,5},{8,10},{9,11},{10,... | collective-permute-start | bytes 884744 | tf_op jit(solution)/shard_map/ppermute | solution.py:499
  107.8 5.6 %collective-permute-start.18 = (bf16[192,768]{1,0:T(8,128)(2,1)S(1)}, bf16[192,768]{1,0:T(8,128)(2,1)S(1)}, u32[]{:S(2)}, u32[]{:S(2)}) collective-permute-start(bf16[192,768]{1,0:T(8,128)(2,1)S(1)} %bitcast.50), channel_id=1, source_target_pairs={{0,1},{1,0},{2,3},{3,2},{4,5},{5,4},{6,7},{7,6},{8,9},{9,8},{10,11... | collective-permute-start | bytes 884744 | tf_op jit(solution)/shard_map/ppermute | solution.py:499
  112.4 1.6 copy-start.18
  112.4 1.6 collective-permute-start.20
  122.8 21.3 %all-to-all-start.2 = ((bf16[8,48,768]{2,1,0:T(8,128)(2,1)}), bf16[8,48,768]{2,1,0:T(8,128)(2,1)S(1)}, u32[]{:S(2)}, u32[]{:S(2)}) async-start(bf16[8,48,768]{2,1,0:T(8,128)(2,1)} %pad_maximum_fusion.1), calls=%async_computation.2 | async-start | bytes 1179648 | tf_op jit(solution)/shard_map/all_to_all | solution.py:509
  141.8 7.0 %copy-start.26 = (bf16[768]{0:T(1024)(128)(2,1)S(1)}, bf16[768]{0:T(1024)(128)(2,1)}, u32[]{:S(2)}) copy-start(bf16[768]{0:T(1024)(128)(2,1)} %refs_9_.1) | copy-start | bytes 4612
  141.8 7.0 %copy-start.24 = (f32[512,128]{1,0:T(8,128)S(1)}, f32[512,128]{1,0:T(8,128)}, u32[]{:S(2)}) copy-start(f32[512,128]{1,0:T(8,128)} %get-tuple-element.60) | copy-start | bytes 786436
  144.1 1.9 %collective-permute-start.21 = (bf16[256,768]{1,0:T(8,128)(2,1)}, bf16[256,768]{1,0:T(8,128)(2,1)S(1)}, u32[]{:S(2)}, u32[]{:S(2)}) collective-permute-start(bf16[256,768]{1,0:T(8,128)(2,1)} %get-tuple-element.96), channel_id=1, source_target_pairs={{0,1},{1,0},{2,3},{3,2},{4,5},{5,4},{6,7},{7,6},{8,9},{9,8},{10,11... | collective-permute-start | bytes 1179656 | tf_op jit(solution)/shard_map/ppermute | solution.py:499
  147.2 11.2 %collective-permute-start.22 = (bf16[256,768]{1,0:T(8,128)(2,1)S(1)}, bf16[256,768]{1,0:T(8,128)(2,1)S(1)}, u32[]{:S(2)}, u32[]{:S(2)}) collective-permute-start(bf16[256,768]{1,0:T(8,128)(2,1)S(1)} %add_convert_fusion.2), channel_id=1, source_target_pairs={{0,2},{1,3},{2,0},{3,1},{4,6},{5,7},{6,4},{7,5},{8,10},{9,11},{10,... | collective-permute-start | bytes 1179656 | tf_op jit(solution)/shard_map/ppermute | solution.py:499
  148.9 30.3 %all-to-all-start.3 = ((bf16[8,88,768]{2,1,0:T(8,128)(2,1)}), bf16[8,88,768]{2,1,0:T(8,128)(2,1)S(1)}, u32[]{:S(2)}, u32[]{:S(2)}) async-start(bf16[8,88,768]{2,1,0:T(8,128)(2,1)} %bitcast.23), calls=%async_computation.3 | async-start | bytes 2162688 | tf_op jit(solution)/shard_map/all_to_all | solution.py:509
  158.5 9.7 %copy-start = (bf16[512,768]{1,0:T(8,128)(2,1)S(1)}, bf16[512,768]{1,0:T(8,128)(2,1)}, u32[]{:S(2)}) copy-start(bf16[512,768]{1,0:T(8,128)(2,1)} %refs_8_.3) | copy-start | bytes 2359300
  158.5 9.6 %collective-permute-start.26 = (bf16[256,768]{1,0:T(8,128)(2,1)S(1)}, bf16[256,768]{1,0:T(8,128)(2,1)S(1)}, u32[]{:S(2)}, u32[]{:S(2)}) collective-permute-start(bf16[256,768]{1,0:T(8,128)(2,1)S(1)} %add_convert_fusion.1), channel_id=1, source_target_pairs={{0,1},{1,0},{2,3},{3,2},{4,5},{5,4},{6,7},{7,6},{8,9},{9,8},{10,11... | collective-permute-start | bytes 1179656 | tf_op jit(solution)/shard_map/ppermute | solution.py:499
  158.7 9.5 %collective-permute-start.24 = (bf16[192,768]{1,0:T(8,128)(2,1)S(1)}, bf16[192,768]{1,0:T(8,128)(2,1)S(1)}, u32[]{:S(2)}, u32[]{:S(2)}) collective-permute-start(bf16[192,768]{1,0:T(8,128)(2,1)S(1)} %bitcast.53), channel_id=1, source_target_pairs={{0,2},{1,3},{2,0},{3,1},{4,6},{5,7},{6,4},{7,5},{8,10},{9,11},{10,... | collective-permute-start | bytes 884744 | tf_op jit(solution)/shard_map/ppermute | solution.py:499
  161.1 7.6 %copy-start.4 = (f32[512,768]{1,0:T(8,128)S(1)}, f32[512,768]{1,0:T(8,128)}, u32[]{:S(2)}) copy-start(f32[512,768]{1,0:T(8,128)} %get-tuple-element.98) | copy-start | bytes 4718596
  161.1 9.2 %collective-permute-start.23 = (bf16[192,768]{1,0:T(8,128)(2,1)S(1)}, bf16[192,768]{1,0:T(8,128)(2,1)S(1)}, u32[]{:S(2)}, u32[]{:S(2)}) collective-permute-start(bf16[192,768]{1,0:T(8,128)(2,1)S(1)} %bitcast.54), channel_id=1, source_target_pairs={{0,1},{1,0},{2,3},{3,2},{4,5},{5,4},{6,7},{7,6},{8,9},{9,8},{10,11... | collective-permute-start | bytes 884744 | tf_op jit(solution)/shard_map/ppermute | solution.py:499
  168.2 2.1 %collective-permute-start.25 = (bf16[192,768]{1,0:T(8,128)(2,1)S(1)}, bf16[192,768]{1,0:T(8,128)(2,1)S(1)}, u32[]{:S(2)}, u32[]{:S(2)}) collective-permute-start(bf16[192,768]{1,0:T(8,128)(2,1)S(1)} %collective-permute-done.24), channel_id=1, source_target_pairs={{0,1},{1,0},{2,3},{3,2},{4,5},{5,4},{6,7},{7,6},{8,9},{9,8},{10,11... | collective-permute-start | bytes 884744 | tf_op jit(solution)/shard_map/ppermute | solution.py:499
  179.5 1.4 collective-permute-start.27
  180.9 4.2 %collective-permute-start.28 = (f32[9,768]{1,0:T(8,128)S(1)}, f32[9,768]{1,0:T(8,128)S(1)}, u32[]{:S(2)}, u32[]{:S(2)}) collective-permute-start(f32[9,768]{1,0:T(8,128)S(1)} %add.131), channel_id=1, source_target_pairs={{0,2},{1,3},{2,0},{3,1},{4,6},{5,7},{6,4},{7,5},{8,10},{9,11},{10,... | collective-permute-start | bytes 82952 | tf_op jit(solution)/shard_map/ppermute | solution.py:499
  (13 other events, 13.4 us)

commit v2 on v1

--- a/solution.py
+++ b/solution.py
@@ -134,13 +134,25 @@
 class Input:
     def __init__(self, copies, buffer):
         self.copies, self.buffer, self.shape = copies, buffer, buffer.shape
-        for copy in copies:
-            copy.start()
-
-    def __getitem__(self, index):
+        self.begun, self.later = False, ()
+
+    def begin(self):
+        if not self.begun:
+            for copy in self.copies:
+                copy.start()
+        self.begun = True
+
+    def land(self):
+        self.begin()
         for copy in self.copies:
             copy.wait()
         self.copies = ()
+        for entry in self.later:
+            entry.begin()
+        self.later = ()
+
+    def __getitem__(self, index):
+        self.land()
         return self.buffer[index]
 
 
@@ -160,7 +172,7 @@
         self.left = True
 
 
-def call(kernel, name, outs, smem, operands, scratch=(), limit=60, flops=10**5, moved=10**4):
+def call(kernel, name, outs, smem, operands, scratch=(), first=None, limit=60, flops=10**5, moved=10**4):
     groups = [entry if isinstance(entry, tuple) else (entry,) for entry in operands]
     arrays = [array for group in groups for array in group]
     anywhere = pl.BlockSpec(memory_space=pl.ANY)
@@ -187,14 +199,16 @@
                 copies.append(pltpu.make_async_copy(sources[number], place, in_sems.at[number]))
                 number += 1
             inputs.append(Input(copies, buffer))
+        for entry in inputs[:first]:
+            entry.begin()
+            entry.later = inputs[len(inputs) if first is None else first :]
         outputs = [
             Output(pltpu.make_async_copy(buffer, target, out_sems.at[i]), buffer)
             for i, (buffer, target) in enumerate(zip(out_buffers, targets))
         ]
         kernel(*scalars, *inputs, *outputs, *refs)
         for entry in inputs:
-            for copy in entry.copies:
-                copy.wait()
+            entry.land()
         for entry in outputs:
             entry.leave()
         for entry in outputs:
@@ -331,7 +345,7 @@
 
 def hidden_back_kernel(
     devices, place_ref, hidden_ref, r0, r1, r2, r3, cot_ref, gain_ref, wo_ref, mixed_ref,
-    grad_ref, gm_ref, turned_ref, norm_ref, sums_ref, attn_ref,
+    router_a, router_b, grad_ref, gm_ref, turned_ref, norm_ref, sums_ref, router_ref, attn_ref,
 ):
     tok_rows, width = hidden_ref.shape
     columns = mixed_ref.shape[1]
@@ -360,9 +374,12 @@
     unit = lax.broadcasted_iota(jnp.int32, (columns, columns), 0)
     unit = (unit == lax.broadcasted_iota(jnp.int32, (columns, columns), 1)).astype(BF16)
     sums = dot(dot_t(unit, mixed_ref[...]).astype(BF16), attn_ref[...]).T
+    router = router_a[...] + router_b[...]
+    router_ref[...] = router
     if devices == PAIRED:
         size = width // devices
-        sums = jnp.concatenate([packed(sums[n * size : (n + 1) * size], 4) for n in range(devices)], axis=0)
+        blocks = [packed(sums[n * size : (n + 1) * size], 4) for n in range(devices)]
+        sums = jnp.concatenate([piece for block in blocks for piece in (block, router)], axis=0)
     sums_ref[...] = sums.astype(BF16)
     sums_ref.leave()
     turned_ref[...] = dot_t(wo_ref[...], attn_ref[...]).astype(BF16)
@@ -371,7 +388,7 @@
 
 def back_kernel(
     heads, size, devices, table_ref, core_ref, q_ref, k_ref, v_ref, gm_ref, turned_ref, total_ref,
-    tokens_ref, gain_ref, wq_ref, wk_ref, wv_ref, router_a, router_b, norm_ref,
+    tokens_ref, gain_ref, wq_ref, wk_ref, wv_ref, norm_ref,
     sums_ref, keep_ref, send_ref, small_ref, back_t, turn_t, part_ref, normed_ref, qb_ref,
 ):
     tok_rows, width = tokens_ref.shape
@@ -379,10 +396,9 @@
     count = LEN // TILE
     keys, all_values = k_ref[...], v_ref[...]
     back_t[...] = jnp.zeros_like(back_t)
-    inputs = tokens_ref[...].astype(F32)
-    inv_first = inv_rms_of(inputs)
-    normed_ref[...] = (inputs * inv_first * gain_ref[...].astype(F32).reshape(1, -1)).astype(BF16)
-    turn_t[pl.ds(0, columns), :] = dot_t(wq_ref[...], normed_ref[...]).astype(BF16)
+    unit = lax.broadcasted_iota(jnp.int32, (columns, columns), 0)
+    unit = (unit == lax.broadcasted_iota(jnp.int32, (columns, columns), 1)).astype(BF16)
+    turn_t[pl.ds(0, columns), :] = dot_t(unit, q_ref[...]).astype(BF16)
     turn_t[pl.ds(columns, columns), :] = turned_ref[...]
     all_tiles = [bias_tiles(table_ref, head) for head in range(heads)]
     head_keys = [head_columns(keys, head, size) for head in range(heads)]
@@ -420,6 +436,9 @@
                     held = far[head][side]
                     far[head][side] = summed if held is None else held + summed
         qb_ref[rows, :] = query_back.astype(BF16)
+    inputs = tokens_ref[...].astype(F32)
+    inv_first = inv_rms_of(inputs)
+    normed_ref[...] = (inputs * inv_first * gain_ref[...].astype(F32).reshape(1, -1)).astype(BF16)
     query_back = qb_ref[...]
     key_t = back_t[pl.ds(0, columns), :].astype(BF16)
     value_t = back_t[pl.ds(columns, columns), :].astype(BF16)
@@ -435,11 +454,9 @@
     first_part = jnp.sum(part_ref[...] * tokens_ref[...].astype(F32) * inv_first, axis=0, keepdims=True)
     line = lax.broadcasted_iota(jnp.int32, (8, width), 0)
     lines = jnp.where(line == 0, first_part, jnp.where(line == 1, norm_row, jnp.where(line == 2, bias_row, 0.0)))
-    small = jnp.concatenate([router_a[...] + router_b[...], lines], axis=0)
+    small = lines
     small_ref[...] = small
     small_ref.leave()
-    unit = lax.broadcasted_iota(jnp.int32, (columns, columns), 0)
-    unit = (unit == lax.broadcasted_iota(jnp.int32, (columns, columns), 1)).astype(BF16)
     turned = (dot_t(unit, query_back).astype(BF16), key_t, value_t)
     parts = [dot(rows, normed_ref[...]) for rows in turned]
     sums = jnp.concatenate(parts, axis=0).T
@@ -616,51 +633,50 @@
     home_far = swap(home, "tensor", 2)
     returned_back = (home, swap(home, "tensor", 1), home_far, swap(home_far, "tensor", 1))
 
-    grad_hidden, grad_mixed, turned, norm_part, output_sums = call(
+    result = exchange_expert(after(own_result, home).reshape(experts, quarter, width)).reshape(chunk_rows, width)
+
+    grad_hidden, grad_mixed, turned, norm_part, output_sums, router_part = call(
         functools.partial(hidden_back_kernel, devices),
         "hidden_back",
         (
             ((tok_rows, width), F32), ((tok_rows, columns), BF16), ((columns, tok_rows), BF16), ((8, width), F32),
-            ((width // 4, 4 * columns) if paired else (width, columns), BF16),
+            ((width // 4 + devices * experts, 4 * columns) if paired else (width, columns), BF16),
+            (router.shape, F32),
         ),
         (),
-        (place[:, None], hidden, *returned_back, cotangent, norm_second, w_output, mixed),
+        (place[:, None], hidden, *returned_back, cotangent, norm_second, w_output, mixed, router_a, router_b),
         scratch=(((tok_rows, width), BF16),),
     )
 
-    own_result = own_result.reshape(experts, quarter, width)
-    if paired:
-        both = exchange_expert(
-            jnp.concatenate([own_result, output_sums.reshape(experts, quarter, width)], axis=1)
-        )
-        result, output_sums = both[:, :quarter].reshape(chunk_rows, width), both[:, quarter:]
-    else:
-        result = exchange_expert(own_result).reshape(chunk_rows, width)
-        both = output_sums = exchange_expert(output_sums.reshape(devices, -1, columns))
+    grad_hidden, grad_mixed, turned, norm_part, output_sums, _ = lax.optimization_barrier(
+        (grad_hidden, grad_mixed, turned, norm_part, output_sums, result)
+    )
+
+    output_sums = exchange_expert(output_sums.reshape(devices, -1, output_sums.shape[1]))
+    result_far = swap(result, "tensor", 2)
     sums, keep, send, small = call(
         functools.partial(back_kernel, heads_here, columns // heads_here, devices),
         "layer_back",
         (
-            ((3 * width // 4 + devices * (experts + 8), 4 * columns) if paired else (width, 3 * columns), BF16),
-            ((half, width), F32), ((half, width), BF16), ((experts + 8, width), F32),
+            ((3 * width // 4 + devices * 8, 4 * columns) if paired else (width, 3 * columns), BF16),
+            ((half, width), F32), ((half, width), BF16), ((8, width), F32),
         ),
         (table, core.reshape(1, 1)),
         (
-            queries, keys, values, grad_mixed, turned, totals, tokens, norm_first, *weights,
-            router_a, router_b, norm_part,
-        ),
+            queries, keys, values, grad_mixed, turned, totals, tokens, norm_first, *weights, norm_part,
+        ),
+        first=6,
         scratch=(
             ((2 * columns, tok_rows), F32), ((2 * columns, tok_rows), BF16), ((tok_rows, width), F32),
             ((tok_rows, width), BF16), ((tok_rows, columns), BF16),
         ),
     )
-    sums, keep, send, small = lax.optimization_barrier((sums, keep, send, small, both))[:4]
+    sums, keep, send, small = lax.optimization_barrier((sums, keep, send, small, output_sums, result_far))[:4]
 
     sums = exchange_expert(sums.reshape(devices, -1, sums.shape[1]))
 
     pair = (keep + swap(send, "tensor", 1).astype(F32)).astype(BF16)
     total = (pair.astype(F32) + swap(pair, "tensor", 2).astype(F32)).astype(BF16)
-    result_far = swap(after(result, total), "tensor", 2)
 
     grads = jnp.sum(sums.astype(F32), axis=0)
     grad_output = jnp.sum(output_sums.astype(F32), axis=0)
@@ -668,9 +684,11 @@
         split = width // PAIRED // 2
         small = grads[3 * split // 2 :]
         grads = jnp.concatenate([unpacked(grads[:split], 2), unpacked(grads[split : 3 * split // 2], 4)], axis=1)
-        grad_output = unpacked(grad_output, 4)
+        grad_router = grad_output[split // 2 :]
+        grad_output = unpacked(grad_output[: split // 2], 4)
     else:
         small = sum_expert(small)
+        grad_router = sum_expert(router_part)
 
     near = swap(total, "tensor", 1)
     low = jnp.where(core == 1, near, total).astype(F32)
@@ -687,22 +705,22 @@
     ).astype(BF16)
     layer_out = (hidden + gate[:, :1] * dot(place_hot, jnp.concatenate(returned))).astype(BF16)
 
-    summed = small[: experts + 1]
-    summed = after(summed, result_far)
-    summed = summed + swap(summed, "tensor", 1)
-    summed = summed + swap(summed, "tensor", 2)
+    grad_router = grad_router + swap(after(grad_router, total), "tensor", 1)
+    grad_router = grad_router + swap(grad_router, "tensor", 2)
+    first = small + swap(small, "tensor", 1)
+    first = first + swap(after(first, (result_far, grad_router)), "tensor", 2)
     bias_size = BUCKETS * heads_here
     return (
         layer_out,
         grad_tokens,
-        summed[experts],
+        first[0],
         grads[:, :columns],
         grads[:, columns : 2 * columns],
         grads[:, 2 * columns :],
         grad_output.T,
-        small[experts + 2, :bias_size].reshape(heads_here, BUCKETS).T,
-        small[experts + 1],
-        summed[:experts].T,
+        small[2, :bias_size].reshape(heads_here, BUCKETS).T,
+        small[1],
+        grad_router.T,
         grad_expert_in[None],
         grad_expert_out[None],
     )

time: 187 us -> 185 us (0.989)
  waiting for transfers between devices: 58.5 us -> 45.2 us
  starting transfers between devices: 26.4 us -> 35.2 us
    ppermute x29 -> x31, waiting for transfers between devices: 47.3 us -> 35.5 us  [swap(): return lax.ppermute(values, axis, [(i, i ^ mask) for i in range(size)])]
    all_to_all x3 -> x4, starting transfers between devices: 12.6 us -> 20.1 us  [exchange_expert(): lax.all_to_all(blocks, 'expert', split_axis=0, concat_axis=0, tiled=True)]
    all_to_all x3 -> x4, waiting for transfers between devices: 11.2 us -> 9.68 us  [exchange_expert(): lax.all_to_all(blocks, 'expert', split_axis=0, concat_axis=0, tiled=True)]
    ppermute x29 -> x31, starting transfers between devices: 13.8 us -> 15.1 us  [swap(): return lax.ppermute(values, axis, [(i, i ^ mask) for i in range(size)])]
  transfers between devices with their start and end apart: 32 -> 35, of which waited for: 17 -> 17; matrix products, arithmetic and copies ran while one was open for 7% -> 9% of each run, Pallas kernels for 19% -> 23%
where the time goes in v2:
time: 185 us; the launch traced here: 184 us
  Pallas kernels  56.1 us (30%)
  waiting for transfers between devices  45.2 us (24%)
  starting transfers between devices  35.2 us (19%)
  blocking collectives  22.6 us (12%)
  other arithmetic  12.2 us (7%)
  local copies, waits for them, and re-layouts  7.87 us (4%)
  matrix products  3.23 us (2%)
    pallas_call x7, Pallas kernels, call(): pl.pallas_call(body, out_shape=tuple((jax.ShapeDtypeStruct(shape, kind) f...  56.1 us
    ppermute x31, waiting for transfers between devices, swap(): return lax.ppermute(values, axis, [(i, i ^ mask) for i in range(size)])  35.5 us
    all_to_all x1, blocking collectives, exchange_expert(): lax.all_to_all(blocks, 'expert', split_axis=0, concat_axis=0, tiled=True)  22.6 us
    all_to_all x4, starting transfers between devices, exchange_expert(): lax.all_to_all(blocks, 'expert', split_axis=0, concat_axis=0, tiled=True)  20.1 us
    ppermute x31, starting transfers between devices, swap(): return lax.ppermute(values, axis, [(i, i ^ mask) for i in range(size)])  15.1 us
    all_to_all x4, waiting for transfers between devices, exchange_expert(): lax.all_to_all(blocks, 'expert', split_axis=0, concat_axis=0, tiled=True)  9.68 us
    unnamed x60, local copies, waits for them, and re-layouts  5.68 us
  transfers between devices with their start and end apart: 35, of which 17 were waited for; matrix products, arithmetic and copies ran while one was open for 9% of the time, Pallas kernels for 23%

profile of v2, /device:TPU:0, one launch (start us, length us, event | category | flops | bytes accessed | tf_op | source)
XLA Modules:
  0.0 183.7 jit_solution(4399873659756937753)
XLA Ops:
  0.7 3.0 %collective-permute-start = (bf16[192,768]{1,0:T(8,128)(2,1)}, bf16[192,768]{1,0:T(8,128)(2,1)S(1)}, u32[]{:S(2)}, u32[]{:S(2)}) collective-permute-start(bf16[192,768]{1,0:T(8,128)(2,1)} %refs_8_.2), channel_id=1, source_target_pairs={{0,2},{1,3},{2,0},{3,1},{4,6},{5,7},{6,4},{7,5},{8,10},{9,11},{10,... | collective-permute-start | bytes 884744 | tf_op jit(solution)/shard_map/ppermute | solution.py:516
  3.7 1.3 convert_bitcast_fusion.refs_0_
  4.9 7.8 %attend.1 = (bf16[512,192]{1,0:T(8,128)(2,1)}, bf16[512,192]{1,0:T(8,128)(2,1)}, bf16[512,192]{1,0:T(8,128)(2,1)}, bf16[512,192]{1,0:T(8,128)(2,1)}, f32[512,128]{1,0:T(8,128)}) custom-call(f32[3,32]{1,0:T(4,128)} %convert_bitcast_fusion.refs_0_, bf16[512,768]{1,0:T(8,128)(2,1)} %refs_8_.3, bf16[768]{0:T(1024)(128)(2,1)} %refs_9_.1, ...), custom_call_target="tpu_custom_call" | custom-call | flops 100000 | bytes 10000 | tf_op jit(solution)/shard_map/attend/pallas_call | solution.py:217
  13.7 0.9 copy.42.refs_13_
  14.6 7.4 %collective-permute-done.2.refs_5_ = bf16[512,192]{1,0:T(8,128)(2,1)S(1)} collective-permute-done((bf16[512,192]{1,0:T(8,128)(2,1)}, bf16[512,192]{1,0:T(8,128)(2,1)S(1)}, u32[]{:S(2)}, u32[]{:S(2)}) %collective-permute-start.2) | collective-permute-done | bytes 196640 | tf_op jit(solution)/shard_map/ppermute | solution.py:516
  22.0 0.6 fusion.20.refs_1_
  22.7 0.8 collective-permute-done.3.refs_6_
  23.6 0.7 copy-done.23
  24.3 6.6 %hidden.1 = (f32[512,768]{1,0:T(8,128)}, bf16[192,1536]{1,0:T(8,128)(2,1)}, f32[512,128]{1,0:T(8,128)}) custom-call(s32[1,1]{1,0:T(1,128)} %bitcast.refs_0_, s32[1,512]{1,0:T(1,128)} %fusion.20.refs_1_, bf16[512,768]{1,0:T(8,128)(2,1)} %refs_8_.3, bf16[512,192]{1,0:T(8,128)(2,1)} %get-tuple-element.65.refs_3_.refs_9_, bf16[512,192]{1,0:T(8,128)(2,1)} %copy-done.22, ...), custom_call_target="tpu_custom_call" | custom-call | flops 100000 | bytes 10000 | tf_op jit(solution)/shard_map/hidden/pallas_call | solution.py:217
  30.9 22.6 %all_to_all.25 = bf16[8,24,1536]{2,1,0:T(8,128)(2,1)S(1)} all-to-all(bf16[8,24,1536]{2,1,0:T(8,128)(2,1)} %bitcast.50), channel_id=1, replica_groups=mesh['expert'=8,'tensor'=4] {'expert'}, dimensions={0} | all-to-all | bytes 1179648 | tf_op jit(solution)/shard_map/all_to_all | solution.py:526
  54.6 1.5 collective-permute-start.10
  56.2 0.7 copy-done.5
  57.0 7.6 %expert_pair.2 = (f32[192,768]{1,0:T(8,128)}, bf16[192,768]{1,0:T(8,128)(2,1)}, f32[192,768]{1,0:T(8,128)}, bf16[192,768]{1,0:T(8,128)(2,1)}, bf16[384,768]{1,0:...) custom-call(s32[1,1]{1,0:T(1,128)} %bitcast.12.refs_0_, bf16[192,768]{1,0:T(8,128)(2,1)} %copy-done.5, ...), custom_call_target="tpu_custom_call" | custom-call | flops 100000 | bytes 10000 | tf_op jit(solution)/shard_map/expert_pair/pallas_call | solution.py:217
  64.7 4.8 %collective-permute-done.10.refs_7_.refs_6_ = bf16[192,768]{1,0:T(8,128)(2,1)S(1)} collective-permute-done((bf16[192,768]{1,0:T(8,128)(2,1)S(1)}, bf16[192,768]{1,0:T(8,128)(2,1)S(1)}, u32[]{:S(2)}, u32[]{:S(2)}) %collective-permute-start.10) | collective-permute-done | bytes 294944 | tf_op jit(solution)/shard_map/ppermute | solution.py:516
  69.5 1.6 collective-permute-done.11.refs_3_.refs_7_
  71.1 0.7 copy-done.10
  71.8 7.6 %expert_pair.3 = (f32[192,768]{1,0:T(8,128)}, bf16[192,768]{1,0:T(8,128)(2,1)}, f32[192,768]{1,0:T(8,128)}, bf16[192,768]{1,0:T(8,128)(2,1)}, bf16[384,768]{1,0:...) custom-call(s32[1,1]{1,0:T(1,128)} %bitcast.12.refs_0_, bf16[192,768]{1,0:T(8,128)(2,1)} %copy-done.9, ...), custom_call_target="tpu_custom_call" | custom-call | flops 100000 | bytes 10000 | tf_op jit(solution)/shard_map/expert_pair/pallas_call | solution.py:217
  79.6 1.7 collective-permute-done.12
  81.2 1.1 add_convert_fusion.6
  83.5 0.8 collective-permute-done.14
  84.4 7.6 %collective-permute-done.16 = bf16[192,768]{1,0:T(8,128)(2,1)S(1)} collective-permute-done((bf16[192,768]{1,0:T(8,128)(2,1)S(1)}, bf16[192,768]{1,0:T(8,128)(2,1)S(1)}, u32[]{:S(2)}, u32[]{:S(2)}) %collective-permute-start.16) | collective-permute-done | bytes 294944 | tf_op jit(solution)/shard_map/ppermute | solution.py:516
  92.0 0.8 add_convert_fusion.4
  93.3 3.4 %all-to-all-start.1 = ((bf16[8,24,768]{2,1,0:T(8,128)(2,1)}), bf16[8,24,768]{2,1,0:T(8,128)(2,1)S(1)}, u32[]{:S(2)}, u32[]{:S(2)}) async-start(bf16[8,24,768]{2,1,0:T(8,128)(2,1)} %bitcast.17), calls=%async_computation.1 | async-start | bytes 589824 | tf_op jit(solution)/shard_map/all_to_all | solution.py:526
  96.7 6.8 %expert_grads.1 = (f32[768,768]{1,0:T(8,128)}, f32[768,768]{1,0:T(8,128)}) custom-call(bf16[192,768]{1,0:T(8,128)(2,1)} %copy-done.2, bf16[192,768]{1,0:T(8,128)(2,1)} %copy-done.5, bf16[192,768]{1,0:T(8,128)(2,1)} %copy-done.7, bf16[192,768]{1,0:T(8,128)(2,1)} %copy-done.9, bf16[192,768]{1,0:T(8,128)(2,1)} %copy-done.1, bf16[192,768]{1,0:T(8,128)(2,1)} %copy-done.6, ...), custom_call_target="tpu_custom_call" | custom-call | flops 100000 | bytes 10000 | tf_op jit(solution)/shard_map/expert_grads/pallas_call | solution.py:217
  103.6 0.8 add_convert_fusion.3
  104.4 1.3 all-to-all-done.1
  105.7 1.5 collective-permute-start.19
  107.5 4.7 %all-to-all-start.2 = ((bf16[8,24,768]{2,1,0:T(8,128)(2,1)}), bf16[8,24,768]{2,1,0:T(8,128)(2,1)}, u32[]{:S(2)}, u32[]{:S(2)}) async-start(bf16[8,24,768]{2,1,0:T(8,128)(2,1)} %bitcast.19), calls=%async_computation.2 | async-start | bytes 589824 | tf_op jit(solution)/shard_map/all_to_all | solution.py:526
  113.2 0.8 fusion.26
  115.2 6.5 %hidden_back.1 = (f32[512,768]{1,0:T(8,128)}, bf16[512,192]{1,0:T(8,128)(2,1)}, bf16[192,512]{1,0:T(8,128)(2,1)}, f32[8,768]{1,0:T(8,128)}, bf16[256,768]{1,0:T(8,128)(2,1)}, /*index=5*/f32[8,768]{1,0:T(8,128)}) custom-call(s32[512,1]{1,0:T(8,128)} %get-tuple-element.155.refs_0_, f32[512,768]{1,0:T(8,128)} %get-tuple-element.66.refs_1_, ...), custom_call_target="tpu_custom_call" | custom-call | flops 100000 | bytes 10000 | tf_op jit(solution)/shard_map/hidden_back/pallas_call | solution.py:217
  121.8 6.0 %all-to-all-start.3 = ((bf16[8,32,768]{2,1,0:T(8,128)(2,1)}), bf16[8,32,768]{2,1,0:T(8,128)(2,1)S(1)}, u32[]{:S(2)}, u32[]{:S(2)}) async-start(bf16[8,32,768]{2,1,0:T(8,128)(2,1)} %bitcast.51), calls=%async_computation.3 | async-start | bytes 786432 | tf_op jit(solution)/shard_map/all_to_all | solution.py:526
  128.4 13.2 %layer_back.1 = (bf16[640,768]{1,0:T(8,128)(2,1)}, f32[256,768]{1,0:T(8,128)}, bf16[256,768]{1,0:T(8,128)(2,1)}, f32[8,768]{1,0:T(8,128)}) custom-call(f32[3,32]{1,0:T(4,128)} %convert_bitcast_fusion.refs_0_, s32[1,1]{1,0:T(1,128)} %bitcast.21.refs_1_, bf16[512,192]{1,0:T(8,128)(2,1)} %get-tuple-element.90.refs_2_, ...), custom_call_target="tpu_custom_call" | custom-call | flops 100000 | bytes 10000 | tf_op jit(solution)/shard_map/layer_back/pallas_call | solution.py:217
  141.8 1.9 %collective-permute-done.22 = bf16[256,768]{1,0:T(8,128)(2,1)S(1)} collective-permute-done((bf16[256,768]{1,0:T(8,128)(2,1)}, bf16[256,768]{1,0:T(8,128)(2,1)S(1)}, u32[]{:S(2)}, u32[]{:S(2)}) %collective-permute-start.22) | collective-permute-done | bytes 393248 | tf_op jit(solution)/shard_map/ppermute | solution.py:516
  143.7 1.2 add_convert_fusion.2
  144.9 1.5 collective-permute-start.23
  146.6 6.0 %all-to-all-start.4 = ((bf16[8,80,768]{2,1,0:T(8,128)(2,1)}), bf16[8,80,768]{2,1,0:T(8,128)(2,1)S(1)}, u32[]{:S(2)}, u32[]{:S(2)}) async-start(bf16[8,80,768]{2,1,0:T(8,128)(2,1)} %bitcast.23), calls=%async_computation.4 | async-start | bytes 1966080 | tf_op jit(solution)/shard_map/all_to_all | solution.py:526
  152.7 3.5 %collective-permute-done.23 = bf16[256,768]{1,0:T(8,128)(2,1)} collective-permute-done((bf16[256,768]{1,0:T(8,128)(2,1)S(1)}, bf16[256,768]{1,0:T(8,128)(2,1)}, u32[]{:S(2)}, u32[]{:S(2)}) %collective-permute-start.23) | collective-permute-done | bytes 393248 | tf_op jit(solution)/shard_map/ppermute | solution.py:516
  156.2 1.1 add_convert_fusion.1
  158.6 1.4 collective-permute-start.29
  160.0 0.7 copy.54
  160.7 1.7 collective-permute-done.29
  163.0 3.0 %add_convert_fusion = bf16[512,768]{1,0:T(8,128)(2,1)} fusion(f32[512,768]{1,0:T(8,128)S(1)} %copy-done.3, f32[512]{0:T(512)S(1)} %slice_reduce_fusion, bf16[192,768]{1,0:T(8,128)(2,1)} %collective-permute-done.25, bf16[192,768]{1,0:T(8,128)(2,1)} %collective-permute-done.21, bf16[192,768]{1,0:T(8,128)(2,1)} %collective-permute-done.24, ...), kind=kOutput, calls=%fused_computation.9 | convolution fusion | flops 610271232 | bytes 3543040 | tf_op jit(solution)/shard_map/dot_general | solution.py:25
  166.1 1.1 copy-done
  167.6 1.5 fusion.3
  169.2 8.4 %all-to-all-done.4 = bf16[8,80,768]{2,1,0:T(8,128)(2,1)S(1)} async-done(((bf16[8,80,768]{2,1,0:T(8,128)(2,1)}), bf16[8,80,768]{2,1,0:T(8,128)(2,1)S(1)}, u32[]{:S(2)}, u32[]{:S(2)}) %all-to-all-start.4) | async-done | bytes 983072 | tf_op jit(solution)/shard_map/all_to_all | solution.py:526
  177.9 0.7 pad_maximum_fusion.1
  179.9 0.7 reshape_squeeze.3
  180.5 2.5 %collective-permute-done.30 = f32[8,768]{1,0:T(8,128)S(1)} collective-permute-done((f32[8,768]{1,0:T(8,128)S(1)}, f32[8,768]{1,0:T(8,128)S(1)}, u32[]{:S(2)}, u32[]{:S(2)}) %collective-permute-start.30) | collective-permute-done | bytes 24608 | tf_op jit(solution)/shard_map/ppermute | solution.py:516
  (132 shorter events, 12.4 us)
Async XLA Ops:
  0.6 12.1 %copy-start.25 = (s32[512,1]{0,1:T(1,128)S(1)}, s32[512,1]{0,1:T(1,128)}, u32[]{:S(2)}) copy-start(s32[512,1]{0,1:T(1,128)} %param.24) | copy-start | bytes 6148
  0.7 12.4 %collective-permute-start = (bf16[192,768]{1,0:T(8,128)(2,1)}, bf16[192,768]{1,0:T(8,128)(2,1)S(1)}, u32[]{:S(2)}, u32[]{:S(2)}) collective-permute-start(bf16[192,768]{1,0:T(8,128)(2,1)} %refs_8_.2), channel_id=1, source_target_pairs={{0,2},{1,3},{2,0},{3,1},{4,6},{5,7},{6,4},{7,5},{8,10},{9,11},{10,... | collective-permute-start | bytes 884744 | tf_op jit(solution)/shard_map/ppermute | solution.py:516
  3.7 19.0 %collective-permute-start.4 = (bf16[192,768]{1,0:T(8,128)(2,1)}, bf16[192,768]{1,0:T(8,128)(2,1)S(1)}, u32[]{:S(2)}, u32[]{:S(2)}) collective-permute-start(bf16[192,768]{1,0:T(8,128)(2,1)} %refs_8_.2), channel_id=1, source_target_pairs={{0,1},{1,0},{2,3},{3,2},{4,5},{5,4},{6,7},{7,6},{8,9},{9,8},{10,11... | collective-permute-start | bytes 884744 | tf_op jit(solution)/shard_map/ppermute | solution.py:516
  13.0 10.6 %copy-start.15 = (bf16[192,768]{1,0:T(8,128)(2,1)}, bf16[192,768]{1,0:T(8,128)(2,1)S(1)}, u32[]{:S(2)}) copy-start(bf16[192,768]{1,0:T(8,128)(2,1)S(1)} %collective-permute-done.refs_9_) | copy-start | bytes 884740
  13.0 9.0 %collective-permute-start.2 = (bf16[512,192]{1,0:T(8,128)(2,1)}, bf16[512,192]{1,0:T(8,128)(2,1)S(1)}, u32[]{:S(2)}, u32[]{:S(2)}) collective-permute-start(bf16[512,192]{1,0:T(8,128)(2,1)} %get-tuple-element.65.refs_3_.refs_9_), channel_id=1, source_target_pairs={{0,2},{1,3},{2,0},{3,1},{4,6},{5,7},{6,4},{7,5},{8,10},{9,11},{10,... | collective-permute-start | bytes 589832 | tf_op jit(solution)/shard_map/ppermute | solution.py:516
  13.2 9.5 %collective-permute-start.5 = (bf16[192,768]{1,0:T(8,128)(2,1)S(1)}, bf16[192,768]{1,0:T(8,128)(2,1)S(1)}, u32[]{:S(2)}, u32[]{:S(2)}) collective-permute-start(bf16[192,768]{1,0:T(8,128)(2,1)S(1)} %collective-permute-done.refs_9_), channel_id=1, source_target_pairs={{0,1},{1,0},{2,3},{3,2},{4,5},{5,4},{6,7},{7,6},{8,9},{9,8},{10,11... | collective-permute-start | bytes 884744 | tf_op jit(solution)/shard_map/ppermute | solution.py:516
  14.6 8.1 %collective-permute-start.1 = (bf16[512,192]{1,0:T(8,128)(2,1)}, bf16[512,192]{1,0:T(8,128)(2,1)S(1)}, u32[]{:S(2)}, u32[]{:S(2)}) collective-permute-start(bf16[512,192]{1,0:T(8,128)(2,1)} %get-tuple-element.65.refs_3_.refs_9_), channel_id=1, source_target_pairs={{0,1},{1,0},{2,3},{3,2},{4,5},{5,4},{6,7},{7,6},{8,9},{9,8},{10,11... | collective-permute-start | bytes 589832 | tf_op jit(solution)/shard_map/ppermute | solution.py:516
  22.0 1.5 collective-permute-start.3
  53.5 2.6 %copy-start.1 = (bf16[192,768]{1,0:T(8,128)(2,1)}, bf16[192,768]{1,0:T(8,128)(2,1)S(1)}, u32[]{:S(2)}) copy-start(bf16[192,768]{1,0:T(8,128)(2,1)S(1)} %get-tuple-element.158.refs_7_.refs_4_) | copy-start | bytes 884740
  53.6 2.6 %collective-permute-start.6 = (bf16[192,768]{1,0:T(8,128)(2,1)S(1)}, bf16[192,768]{1,0:T(8,128)(2,1)S(1)}, u32[]{:S(2)}, u32[]{:S(2)}) collective-permute-start(bf16[192,768]{1,0:T(8,128)(2,1)S(1)} %get-tuple-element.159.refs_6_.refs_0_), channel_id=1, source_target_pairs={{0,1},{1,0},{2,3},{3,2},{4,5},{5,4},{6,7},{7,6},{8,9},{9,8},{10,11... | collective-permute-start | bytes 884744 | tf_op jit(solution)/shard_map/ppermute | solution.py:516
  53.6 2.5 %collective-permute-start.7 = (bf16[192,768]{1,0:T(8,128)(2,1)S(1)}, bf16[192,768]{1,0:T(8,128)(2,1)S(1)}, u32[]{:S(2)}, u32[]{:S(2)}) collective-permute-start(bf16[192,768]{1,0:T(8,128)(2,1)S(1)} %get-tuple-element.158.refs_7_.refs_4_), channel_id=1, source_target_pairs={{0,1},{1,0},{2,3},{3,2},{4,5},{5,4},{6,7},{7,6},{8,9},{9,8},{10,11... | collective-permute-start | bytes 884744 | tf_op jit(solution)/shard_map/ppermute | solution.py:516
  54.1 10.4 %collective-permute-start.8 = (bf16[192,768]{1,0:T(8,128)(2,1)S(1)}, bf16[192,768]{1,0:T(8,128)(2,1)S(1)}, u32[]{:S(2)}, u32[]{:S(2)}) collective-permute-start(bf16[192,768]{1,0:T(8,128)(2,1)S(1)} %get-tuple-element.159.refs_6_.refs_0_), channel_id=1, source_target_pairs={{0,2},{1,3},{2,0},{3,1},{4,6},{5,7},{6,4},{7,5},{8,10},{9,11},{10,... | collective-permute-start | bytes 884744 | tf_op jit(solution)/shard_map/ppermute | solution.py:516
  54.6 14.8 %collective-permute-start.10 = (bf16[192,768]{1,0:T(8,128)(2,1)S(1)}, bf16[192,768]{1,0:T(8,128)(2,1)S(1)}, u32[]{:S(2)}, u32[]{:S(2)}) collective-permute-start(bf16[192,768]{1,0:T(8,128)(2,1)S(1)} %get-tuple-element.158.refs_7_.refs_4_), channel_id=1, source_target_pairs={{0,2},{1,3},{2,0},{3,1},{4,6},{5,7},{6,4},{7,5},{8,10},{9,11},{10,... | collective-permute-start | bytes 884744 | tf_op jit(solution)/shard_map/ppermute | solution.py:516
  64.6 6.5 %copy-start.7 = (bf16[192,768]{1,0:T(8,128)(2,1)}, bf16[192,768]{1,0:T(8,128)(2,1)S(1)}, u32[]{:S(2)}) copy-start(bf16[192,768]{1,0:T(8,128)(2,1)S(1)} %collective-permute-done.8.refs_6_.refs_2_) | copy-start | bytes 884740
  64.6 18.0 %copy-start.28 = (bf16[192,768]{1,0:T(8,128)(2,1)S(1)}, bf16[192,768]{1,0:T(8,128)(2,1)}, u32[]{:S(2)}) copy-start(bf16[192,768]{1,0:T(8,128)(2,1)} %get-tuple-element.81) | copy-start | bytes 884740
  64.6 18.9 %copy-start.27 = (bf16[192,768]{1,0:T(8,128)(2,1)S(1)}, bf16[192,768]{1,0:T(8,128)(2,1)}, u32[]{:S(2)}) copy-start(bf16[192,768]{1,0:T(8,128)(2,1)} %get-tuple-element.76) | copy-start | bytes 884740
  64.6 4.9 %collective-permute-start.9 = (bf16[192,768]{1,0:T(8,128)(2,1)S(1)}, bf16[192,768]{1,0:T(8,128)(2,1)S(1)}, u32[]{:S(2)}, u32[]{:S(2)}) collective-permute-start(bf16[192,768]{1,0:T(8,128)(2,1)S(1)} %collective-permute-done.8.refs_6_.refs_2_), channel_id=1, source_target_pairs={{0,1},{1,0},{2,3},{3,2},{4,5},{5,4},{6,7},{7,6},{8,9},{9,8},{10,11... | collective-permute-start | bytes 884744 | tf_op jit(solution)/shard_map/ppermute | solution.py:516
  69.4 1.6 collective-permute-start.11
  79.4 4.9 %copy-start.12 = (f32[192,768]{1,0:T(8,128)S(1)}, f32[192,768]{1,0:T(8,128)}, u32[]{:S(2)}) copy-start(f32[192,768]{1,0:T(8,128)} %get-tuple-element.77) | copy-start | bytes 1769476
  79.4 12.6 %copy-start.14 = (f32[192,768]{1,0:T(8,128)S(1)}, f32[192,768]{1,0:T(8,128)}, u32[]{:S(2)}) copy-start(f32[192,768]{1,0:T(8,128)} %get-tuple-element.80) | copy-start | bytes 1769476
  79.4 1.9 %collective-permute-start.12 = (bf16[192,768]{1,0:T(8,128)(2,1)}, bf16[192,768]{1,0:T(8,128)(2,1)S(1)}, u32[]{:S(2)}, u32[]{:S(2)}) collective-permute-start(bf16[192,768]{1,0:T(8,128)(2,1)} %get-tuple-element.75), channel_id=1, source_target_pairs={{0,1},{1,0},{2,3},{3,2},{4,5},{5,4},{6,7},{7,6},{8,9},{9,8},{10,11... | collective-permute-start | bytes 884744 | tf_op jit(solution)/shard_map/ppermute | solution.py:516
  82.4 1.9 %collective-permute-start.14 = (bf16[192,768]{1,0:T(8,128)(2,1)}, bf16[192,768]{1,0:T(8,128)(2,1)S(1)}, u32[]{:S(2)}, u32[]{:S(2)}) collective-permute-start(bf16[192,768]{1,0:T(8,128)(2,1)} %get-tuple-element.79), channel_id=1, source_target_pairs={{0,1},{1,0},{2,3},{3,2},{4,5},{5,4},{6,7},{7,6},{8,9},{9,8},{10,11... | collective-permute-start | bytes 884744 | tf_op jit(solution)/shard_map/ppermute | solution.py:516
  82.6 1.9 %collective-permute-start.15 = (bf16[192,768]{1,0:T(8,128)(2,1)S(1)}, bf16[192,768]{1,0:T(8,128)(2,1)S(1)}, u32[]{:S(2)}, u32[]{:S(2)}) collective-permute-start(bf16[192,768]{1,0:T(8,128)(2,1)S(1)} %copy-done.28), channel_id=1, source_target_pairs={{0,1},{1,0},{2,3},{3,2},{4,5},{5,4},{6,7},{7,6},{8,9},{9,8},{10,11... | collective-permute-start | bytes 884744 | tf_op jit(solution)/shard_map/ppermute | solution.py:516
  82.9 9.0 %collective-permute-start.16 = (bf16[192,768]{1,0:T(8,128)(2,1)S(1)}, bf16[192,768]{1,0:T(8,128)(2,1)S(1)}, u32[]{:S(2)}, u32[]{:S(2)}) collective-permute-start(bf16[192,768]{1,0:T(8,128)(2,1)S(1)} %add_convert_fusion.6), channel_id=1, source_target_pairs={{0,2},{1,3},{2,0},{3,1},{4,6},{5,7},{6,4},{7,5},{8,10},{9,11},{10,... | collective-permute-start | bytes 884744 | tf_op jit(solution)/shard_map/ppermute | solution.py:516
  83.5 20.1 %collective-permute-start.13 = (bf16[192,768]{1,0:T(8,128)(2,1)S(1)}, bf16[192,768]{1,0:T(8,128)(2,1)S(1)}, u32[]{:S(2)}, u32[]{:S(2)}) collective-permute-start(bf16[192,768]{1,0:T(8,128)(2,1)S(1)} %copy-done.27), channel_id=1, source_target_pairs={{0,1},{1,0},{2,3},{3,2},{4,5},{5,4},{6,7},{7,6},{8,9},{9,8},{10,11... | collective-permute-start | bytes 884744 | tf_op jit(solution)/shard_map/ppermute | solution.py:516
  92.8 10.8 %collective-permute-start.17 = (bf16[192,768]{1,0:T(8,128)(2,1)S(1)}, bf16[192,768]{1,0:T(8,128)(2,1)S(1)}, u32[]{:S(2)}, u32[]{:S(2)}) collective-permute-start(bf16[192,768]{1,0:T(8,128)(2,1)S(1)} %add_convert_fusion.5), channel_id=1, source_target_pairs={{0,2},{1,3},{2,0},{3,1},{4,6},{5,7},{6,4},{7,5},{8,10},{9,11},{10,... | collective-permute-start | bytes 884744 | tf_op jit(solution)/shard_map/ppermute | solution.py:516
  93.3 12.4 %all-to-all-start.1 = ((bf16[8,24,768]{2,1,0:T(8,128)(2,1)}), bf16[8,24,768]{2,1,0:T(8,128)(2,1)S(1)}, u32[]{:S(2)}, u32[]{:S(2)}) async-start(bf16[8,24,768]{2,1,0:T(8,128)(2,1)} %bitcast.17), calls=%async_computation.1 | async-start | bytes 589824 | tf_op jit(solution)/shard_map/all_to_all | solution.py:526
  96.7 6.9 %copy-start.13 = (f32[192,768]{1,0:T(8,128)S(1)}, f32[192,768]{1,0:T(8,128)}, u32[]{:S(2)}) copy-start(f32[192,768]{1,0:T(8,128)} %get-tuple-element.69) | copy-start | bytes 1769476
  105.7 8.3 %copy-start.11 = (bf16[8,24,768]{2,1,0:T(8,128)(2,1)}, bf16[8,24,768]{2,1,0:T(8,128)(2,1)S(1)}, u32[]{:S(2)}) copy-start(bf16[8,24,768]{2,1,0:T(8,128)(2,1)S(1)} %all-to-all-done.1) | copy-start | bytes 884740
  105.7 6.8 %collective-permute-start.19 = (bf16[192,768]{1,0:T(8,128)(2,1)S(1)}, bf16[192,768]{1,0:T(8,128)(2,1)S(1)}, u32[]{:S(2)}, u32[]{:S(2)}) collective-permute-start(bf16[192,768]{1,0:T(8,128)(2,1)S(1)} %bitcast.47), channel_id=1, source_target_pairs={{0,2},{1,3},{2,0},{3,1},{4,6},{5,7},{6,4},{7,5},{8,10},{9,11},{10,... | collective-permute-start | bytes 884744 | tf_op jit(solution)/shard_map/ppermute | solution.py:516
  107.5 14.2 %all-to-all-start.2 = ((bf16[8,24,768]{2,1,0:T(8,128)(2,1)}), bf16[8,24,768]{2,1,0:T(8,128)(2,1)}, u32[]{:S(2)}, u32[]{:S(2)}) async-start(bf16[8,24,768]{2,1,0:T(8,128)(2,1)} %bitcast.19), calls=%async_computation.2 | async-start | bytes 589824 | tf_op jit(solution)/shard_map/all_to_all | solution.py:526
  112.5 1.6 collective-permute-start.18
  112.5 2.0 %collective-permute-start.20 = (bf16[192,768]{1,0:T(8,128)(2,1)S(1)}, bf16[192,768]{1,0:T(8,128)(2,1)S(1)}, u32[]{:S(2)}, u32[]{:S(2)}) collective-permute-start(bf16[192,768]{1,0:T(8,128)(2,1)S(1)} %collective-permute-done.19.refs_4_), channel_id=1, source_target_pairs={{0,1},{1,0},{2,3},{3,2},{4,5},{5,4},{6,7},{7,6},{8,9},{9,8},{10,11... | collective-permute-start | bytes 884744 | tf_op jit(solution)/shard_map/ppermute | solution.py:516
  121.8 19.9 %all-to-all-start.3 = ((bf16[8,32,768]{2,1,0:T(8,128)(2,1)}), bf16[8,32,768]{2,1,0:T(8,128)(2,1)S(1)}, u32[]{:S(2)}, u32[]{:S(2)}) async-start(bf16[8,32,768]{2,1,0:T(8,128)(2,1)} %bitcast.51), calls=%async_computation.3 | async-start | bytes 786432 | tf_op jit(solution)/shard_map/all_to_all | solution.py:526
  127.8 13.9 %collective-permute-start.21 = (bf16[192,768]{1,0:T(8,128)(2,1)}, bf16[192,768]{1,0:T(8,128)(2,1)}, u32[]{:S(2)}, u32[]{:S(2)}) collective-permute-start(bf16[192,768]{1,0:T(8,128)(2,1)} %bitcast.20), channel_id=1, source_target_pairs={{0,2},{1,3},{2,0},{3,1},{4,6},{5,7},{6,4},{7,5},{8,10},{9,11},{10,... | collective-permute-start | bytes 884744 | tf_op jit(solution)/shard_map/ppermute | solution.py:516
  141.6 4.7 %copy-start.26 = (bf16[768]{0:T(1024)(128)(2,1)S(1)}, bf16[768]{0:T(1024)(128)(2,1)}, u32[]{:S(2)}) copy-start(bf16[768]{0:T(1024)(128)(2,1)} %refs_9_.1) | copy-start | bytes 4612
  141.6 4.7 %copy-start.24 = (f32[512,128]{1,0:T(8,128)S(1)}, f32[512,128]{1,0:T(8,128)}, u32[]{:S(2)}) copy-start(f32[512,128]{1,0:T(8,128)} %get-tuple-element.67) | copy-start | bytes 786436
  141.7 2.0 %collective-permute-start.22 = (bf16[256,768]{1,0:T(8,128)(2,1)}, bf16[256,768]{1,0:T(8,128)(2,1)S(1)}, u32[]{:S(2)}, u32[]{:S(2)}) collective-permute-start(bf16[256,768]{1,0:T(8,128)(2,1)} %get-tuple-element.109), channel_id=1, source_target_pairs={{0,1},{1,0},{2,3},{3,2},{4,5},{5,4},{6,7},{7,6},{8,9},{9,8},{10,11... | collective-permute-start | bytes 1179656 | tf_op jit(solution)/shard_map/ppermute | solution.py:516
  144.9 11.3 %collective-permute-start.23 = (bf16[256,768]{1,0:T(8,128)(2,1)S(1)}, bf16[256,768]{1,0:T(8,128)(2,1)}, u32[]{:S(2)}, u32[]{:S(2)}) collective-permute-start(bf16[256,768]{1,0:T(8,128)(2,1)S(1)} %add_convert_fusion.2), channel_id=1, source_target_pairs={{0,2},{1,3},{2,0},{3,1},{4,6},{5,7},{6,4},{7,5},{8,10},{9,11},{10,... | collective-permute-start | bytes 1179656 | tf_op jit(solution)/shard_map/ppermute | solution.py:516
  146.5 16.5 %collective-permute-start.25 = (bf16[192,768]{1,0:T(8,128)(2,1)}, bf16[192,768]{1,0:T(8,128)(2,1)}, u32[]{:S(2)}, u32[]{:S(2)}) collective-permute-start(bf16[192,768]{1,0:T(8,128)(2,1)} %collective-permute-done.21), channel_id=1, source_target_pairs={{0,1},{1,0},{2,3},{3,2},{4,5},{5,4},{6,7},{7,6},{8,9},{9,8},{10,11... | collective-permute-start | bytes 884744 | tf_op jit(solution)/shard_map/ppermute | solution.py:516
  146.6 31.0 %all-to-all-start.4 = ((bf16[8,80,768]{2,1,0:T(8,128)(2,1)}), bf16[8,80,768]{2,1,0:T(8,128)(2,1)S(1)}, u32[]{:S(2)}, u32[]{:S(2)}) async-start(bf16[8,80,768]{2,1,0:T(8,128)(2,1)} %bitcast.23), calls=%async_computation.4 | async-start | bytes 1966080 | tf_op jit(solution)/shard_map/all_to_all | solution.py:526
  152.6 10.4 %copy-start.3 = (f32[512,768]{1,0:T(8,128)S(1)}, f32[512,768]{1,0:T(8,128)}, u32[]{:S(2)}) copy-start(f32[512,768]{1,0:T(8,128)} %get-tuple-element.66.refs_1_) | copy-start | bytes 4718596
  157.3 1.3 collective-permute-start.28
  157.5 8.5 %collective-permute-start.26 = (bf16[256,768]{1,0:T(8,128)(2,1)S(1)}, bf16[256,768]{1,0:T(8,128)(2,1)S(1)}, u32[]{:S(2)}, u32[]{:S(2)}) collective-permute-start(bf16[256,768]{1,0:T(8,128)(2,1)S(1)} %add_convert_fusion.1), channel_id=1, source_target_pairs={{0,1},{1,0},{2,3},{3,2},{4,5},{5,4},{6,7},{7,6},{8,9},{9,8},{10,11... | collective-permute-start | bytes 1179656 | tf_op jit(solution)/shard_map/ppermute | solution.py:516
  158.0 5.1 %collective-permute-start.24 = (bf16[192,768]{1,0:T(8,128)(2,1)}, bf16[192,768]{1,0:T(8,128)(2,1)}, u32[]{:S(2)}, u32[]{:S(2)}) collective-permute-start(bf16[192,768]{1,0:T(8,128)(2,1)} %bitcast.20), channel_id=1, source_target_pairs={{0,1},{1,0},{2,3},{3,2},{4,5},{5,4},{6,7},{7,6},{8,9},{9,8},{10,11... | collective-permute-start | bytes 884744 | tf_op jit(solution)/shard_map/ppermute | solution.py:516
  158.6 3.8 %collective-permute-start.29 = (f32[8,768]{1,0:T(8,128)S(1)}, f32[8,768]{1,0:T(8,128)S(1)}, u32[]{:S(2)}, u32[]{:S(2)}) collective-permute-start(f32[8,768]{1,0:T(8,128)S(1)} %slice_add_fusion.1), channel_id=1, source_target_pairs={{0,2},{1,3},{2,0},{3,1},{4,6},{5,7},{6,4},{7,5},{8,10},{9,11},{10,... | collective-permute-start | bytes 73736 | tf_op jit(solution)/shard_map/ppermute | solution.py:516
  177.8 1.4 collective-permute-start.27
  179.2 3.8 %collective-permute-start.30 = (f32[8,768]{1,0:T(8,128)S(1)}, f32[8,768]{1,0:T(8,128)S(1)}, u32[]{:S(2)}, u32[]{:S(2)}) collective-permute-start(f32[8,768]{1,0:T(8,128)S(1)} %slice_add_fusion.2), channel_id=1, source_target_pairs={{0,2},{1,3},{2,0},{3,1},{4,6},{5,7},{6,4},{7,5},{8,10},{9,11},{10,... | collective-permute-start | bytes 73736 | tf_op jit(solution)/shard_map/ppermute | solution.py:516
  (16 other events, 19.2 us)

commit v3 on v2

--- a/solution.py
+++ b/solution.py
@@ -645,6 +645,7 @@
         ),
         (),
         (place[:, None], hidden, *returned_back, cotangent, norm_second, w_output, mixed, router_a, router_b),
+        first=9,
         scratch=(((tok_rows, width), BF16),),
     )
 

time: 185 us -> 185 us (level)
  no operation moved by 1% of the time
where the time goes in v3:
time: 185 us; the launch traced here: 184 us
  Pallas kernels  56.1 us (30%)
  waiting for transfers between devices  45.2 us (24%)
  starting transfers between devices  35.2 us (19%)
  blocking collectives  22.6 us (12%)
  other arithmetic  12.2 us (7%)
  local copies, waits for them, and re-layouts  7.87 us (4%)
  matrix products  3.23 us (2%)
    pallas_call x7, Pallas kernels, call(): pl.pallas_call(body, out_shape=tuple((jax.ShapeDtypeStruct(shape, kind) f...  56.1 us
    ppermute x31, waiting for transfers between devices, swap(): return lax.ppermute(values, axis, [(i, i ^ mask) for i in range(size)])  35.5 us
    all_to_all x1, blocking collectives, exchange_expert(): lax.all_to_all(blocks, 'expert', split_axis=0, concat_axis=0, tiled=True)  22.6 us
    all_to_all x4, starting transfers between devices, exchange_expert(): lax.all_to_all(blocks, 'expert', split_axis=0, concat_axis=0, tiled=True)  20.1 us
    ppermute x31, starting transfers between devices, swap(): return lax.ppermute(values, axis, [(i, i ^ mask) for i in range(size)])  15.1 us
    all_to_all x4, waiting for transfers between devices, exchange_expert(): lax.all_to_all(blocks, 'expert', split_axis=0, concat_axis=0, tiled=True)  9.68 us
    unnamed x60, local copies, waits for them, and re-layouts  5.68 us
  transfers between devices with their start and end apart: 35, of which 17 were waited for; matrix products, arithmetic and copies ran while one was open for 9% of the time, Pallas kernels for 23%

profile of v3, /device:TPU:0, one launch (start us, length us, event | category | flops | bytes accessed | tf_op | source)
XLA Modules:
  0.0 183.7 jit_solution(13353630720276903273)
XLA Ops:
  0.7 3.0 %collective-permute-start = (bf16[192,768]{1,0:T(8,128)(2,1)}, bf16[192,768]{1,0:T(8,128)(2,1)S(1)}, u32[]{:S(2)}, u32[]{:S(2)}) collective-permute-start(bf16[192,768]{1,0:T(8,128)(2,1)} %refs_8_.2), channel_id=1, source_target_pairs={{0,2},{1,3},{2,0},{3,1},{4,6},{5,7},{6,4},{7,5},{8,10},{9,11},{10,... | collective-permute-start | bytes 884744 | tf_op jit(solution)/shard_map/ppermute | solution.py:516
  3.7 1.3 convert_bitcast_fusion.refs_0_
  4.9 7.8 %attend.1 = (bf16[512,192]{1,0:T(8,128)(2,1)}, bf16[512,192]{1,0:T(8,128)(2,1)}, bf16[512,192]{1,0:T(8,128)(2,1)}, bf16[512,192]{1,0:T(8,128)(2,1)}, f32[512,128]{1,0:T(8,128)}) custom-call(f32[3,32]{1,0:T(4,128)} %convert_bitcast_fusion.refs_0_, bf16[512,768]{1,0:T(8,128)(2,1)} %refs_8_.3, bf16[768]{0:T(1024)(128)(2,1)} %refs_9_.1, ...), custom_call_target="tpu_custom_call" | custom-call | flops 100000 | bytes 10000 | tf_op jit(solution)/shard_map/attend/pallas_call | solution.py:217
  13.7 0.9 copy.42.refs_13_
  14.6 7.4 %collective-permute-done.2.refs_5_ = bf16[512,192]{1,0:T(8,128)(2,1)S(1)} collective-permute-done((bf16[512,192]{1,0:T(8,128)(2,1)}, bf16[512,192]{1,0:T(8,128)(2,1)S(1)}, u32[]{:S(2)}, u32[]{:S(2)}) %collective-permute-start.2) | collective-permute-done | bytes 196640 | tf_op jit(solution)/shard_map/ppermute | solution.py:516
  22.0 0.6 fusion.20.refs_1_
  22.7 0.8 collective-permute-done.3.refs_6_
  23.6 0.7 copy-done.23
  24.3 6.6 %hidden.1 = (f32[512,768]{1,0:T(8,128)}, bf16[192,1536]{1,0:T(8,128)(2,1)}, f32[512,128]{1,0:T(8,128)}) custom-call(s32[1,1]{1,0:T(1,128)} %bitcast.refs_0_, s32[1,512]{1,0:T(1,128)} %fusion.20.refs_1_, bf16[512,768]{1,0:T(8,128)(2,1)} %refs_8_.3, bf16[512,192]{1,0:T(8,128)(2,1)} %get-tuple-element.65.refs_3_.refs_9_, bf16[512,192]{1,0:T(8,128)(2,1)} %copy-done.22, ...), custom_call_target="tpu_custom_call" | custom-call | flops 100000 | bytes 10000 | tf_op jit(solution)/shard_map/hidden/pallas_call | solution.py:217
  30.9 22.6 %all_to_all.25 = bf16[8,24,1536]{2,1,0:T(8,128)(2,1)S(1)} all-to-all(bf16[8,24,1536]{2,1,0:T(8,128)(2,1)} %bitcast.50), channel_id=1, replica_groups=mesh['expert'=8,'tensor'=4] {'expert'}, dimensions={0} | all-to-all | bytes 1179648 | tf_op jit(solution)/shard_map/all_to_all | solution.py:526
  54.6 1.5 collective-permute-start.10
  56.2 0.7 copy-done.5
  57.0 7.6 %expert_pair.2 = (f32[192,768]{1,0:T(8,128)}, bf16[192,768]{1,0:T(8,128)(2,1)}, f32[192,768]{1,0:T(8,128)}, bf16[192,768]{1,0:T(8,128)(2,1)}, bf16[384,768]{1,0:...) custom-call(s32[1,1]{1,0:T(1,128)} %bitcast.12.refs_0_, bf16[192,768]{1,0:T(8,128)(2,1)} %copy-done.5, ...), custom_call_target="tpu_custom_call" | custom-call | flops 100000 | bytes 10000 | tf_op jit(solution)/shard_map/expert_pair/pallas_call | solution.py:217
  64.7 4.8 %collective-permute-done.10.refs_7_.refs_6_ = bf16[192,768]{1,0:T(8,128)(2,1)S(1)} collective-permute-done((bf16[192,768]{1,0:T(8,128)(2,1)S(1)}, bf16[192,768]{1,0:T(8,128)(2,1)S(1)}, u32[]{:S(2)}, u32[]{:S(2)}) %collective-permute-start.10) | collective-permute-done | bytes 294944 | tf_op jit(solution)/shard_map/ppermute | solution.py:516
  69.5 1.6 collective-permute-done.11.refs_3_.refs_7_
  71.1 0.7 copy-done.10
  71.8 7.6 %expert_pair.3 = (f32[192,768]{1,0:T(8,128)}, bf16[192,768]{1,0:T(8,128)(2,1)}, f32[192,768]{1,0:T(8,128)}, bf16[192,768]{1,0:T(8,128)(2,1)}, bf16[384,768]{1,0:...) custom-call(s32[1,1]{1,0:T(1,128)} %bitcast.12.refs_0_, bf16[192,768]{1,0:T(8,128)(2,1)} %copy-done.9, ...), custom_call_target="tpu_custom_call" | custom-call | flops 100000 | bytes 10000 | tf_op jit(solution)/shard_map/expert_pair/pallas_call | solution.py:217
  79.6 1.7 collective-permute-done.12
  81.2 1.1 add_convert_fusion.6
  83.5 0.8 collective-permute-done.14
  84.4 7.6 %collective-permute-done.16 = bf16[192,768]{1,0:T(8,128)(2,1)S(1)} collective-permute-done((bf16[192,768]{1,0:T(8,128)(2,1)S(1)}, bf16[192,768]{1,0:T(8,128)(2,1)S(1)}, u32[]{:S(2)}, u32[]{:S(2)}) %collective-permute-start.16) | collective-permute-done | bytes 294944 | tf_op jit(solution)/shard_map/ppermute | solution.py:516
  92.0 0.8 add_convert_fusion.4
  93.3 3.4 %all-to-all-start.1 = ((bf16[8,24,768]{2,1,0:T(8,128)(2,1)}), bf16[8,24,768]{2,1,0:T(8,128)(2,1)S(1)}, u32[]{:S(2)}, u32[]{:S(2)}) async-start(bf16[8,24,768]{2,1,0:T(8,128)(2,1)} %bitcast.17), calls=%async_computation.1 | async-start | bytes 589824 | tf_op jit(solution)/shard_map/all_to_all | solution.py:526
  96.7 6.8 %expert_grads.1 = (f32[768,768]{1,0:T(8,128)}, f32[768,768]{1,0:T(8,128)}) custom-call(bf16[192,768]{1,0:T(8,128)(2,1)} %copy-done.2, bf16[192,768]{1,0:T(8,128)(2,1)} %copy-done.5, bf16[192,768]{1,0:T(8,128)(2,1)} %copy-done.7, bf16[192,768]{1,0:T(8,128)(2,1)} %copy-done.9, bf16[192,768]{1,0:T(8,128)(2,1)} %copy-done.1, bf16[192,768]{1,0:T(8,128)(2,1)} %copy-done.6, ...), custom_call_target="tpu_custom_call" | custom-call | flops 100000 | bytes 10000 | tf_op jit(solution)/shard_map/expert_grads/pallas_call | solution.py:217
  103.6 0.8 add_convert_fusion.3
  104.4 1.3 all-to-all-done.1
  105.7 1.5 collective-permute-start.19
  107.5 4.7 %all-to-all-start.2 = ((bf16[8,24,768]{2,1,0:T(8,128)(2,1)}), bf16[8,24,768]{2,1,0:T(8,128)(2,1)}, u32[]{:S(2)}, u32[]{:S(2)}) async-start(bf16[8,24,768]{2,1,0:T(8,128)(2,1)} %bitcast.19), calls=%async_computation.2 | async-start | bytes 589824 | tf_op jit(solution)/shard_map/all_to_all | solution.py:526
  113.2 0.8 fusion.26
  115.2 6.5 %hidden_back.1 = (f32[512,768]{1,0:T(8,128)}, bf16[512,192]{1,0:T(8,128)(2,1)}, bf16[192,512]{1,0:T(8,128)(2,1)}, f32[8,768]{1,0:T(8,128)}, bf16[256,768]{1,0:T(8,128)(2,1)}, /*index=5*/f32[8,768]{1,0:T(8,128)}) custom-call(s32[512,1]{1,0:T(8,128)} %get-tuple-element.155.refs_0_, f32[512,768]{1,0:T(8,128)} %get-tuple-element.66.refs_1_, ...), custom_call_target="tpu_custom_call" | custom-call | flops 100000 | bytes 10000 | tf_op jit(solution)/shard_map/hidden_back/pallas_call | solution.py:217
  121.8 6.0 %all-to-all-start.3 = ((bf16[8,32,768]{2,1,0:T(8,128)(2,1)}), bf16[8,32,768]{2,1,0:T(8,128)(2,1)S(1)}, u32[]{:S(2)}, u32[]{:S(2)}) async-start(bf16[8,32,768]{2,1,0:T(8,128)(2,1)} %bitcast.51), calls=%async_computation.3 | async-start | bytes 786432 | tf_op jit(solution)/shard_map/all_to_all | solution.py:526
  128.4 13.2 %layer_back.1 = (bf16[640,768]{1,0:T(8,128)(2,1)}, f32[256,768]{1,0:T(8,128)}, bf16[256,768]{1,0:T(8,128)(2,1)}, f32[8,768]{1,0:T(8,128)}) custom-call(f32[3,32]{1,0:T(4,128)} %convert_bitcast_fusion.refs_0_, s32[1,1]{1,0:T(1,128)} %bitcast.21.refs_1_, bf16[512,192]{1,0:T(8,128)(2,1)} %get-tuple-element.90.refs_2_, ...), custom_call_target="tpu_custom_call" | custom-call | flops 100000 | bytes 10000 | tf_op jit(solution)/shard_map/layer_back/pallas_call | solution.py:217
  141.8 1.9 %collective-permute-done.22 = bf16[256,768]{1,0:T(8,128)(2,1)S(1)} collective-permute-done((bf16[256,768]{1,0:T(8,128)(2,1)}, bf16[256,768]{1,0:T(8,128)(2,1)S(1)}, u32[]{:S(2)}, u32[]{:S(2)}) %collective-permute-start.22) | collective-permute-done | bytes 393248 | tf_op jit(solution)/shard_map/ppermute | solution.py:516
  143.7 1.2 add_convert_fusion.2
  144.9 1.5 collective-permute-start.23
  146.6 6.0 %all-to-all-start.4 = ((bf16[8,80,768]{2,1,0:T(8,128)(2,1)}), bf16[8,80,768]{2,1,0:T(8,128)(2,1)S(1)}, u32[]{:S(2)}, u32[]{:S(2)}) async-start(bf16[8,80,768]{2,1,0:T(8,128)(2,1)} %bitcast.23), calls=%async_computation.4 | async-start | bytes 1966080 | tf_op jit(solution)/shard_map/all_to_all | solution.py:526
  152.7 3.5 %collective-permute-done.23 = bf16[256,768]{1,0:T(8,128)(2,1)} collective-permute-done((bf16[256,768]{1,0:T(8,128)(2,1)S(1)}, bf16[256,768]{1,0:T(8,128)(2,1)}, u32[]{:S(2)}, u32[]{:S(2)}) %collective-permute-start.23) | collective-permute-done | bytes 393248 | tf_op jit(solution)/shard_map/ppermute | solution.py:516
  156.2 1.1 add_convert_fusion.1
  158.6 1.4 collective-permute-start.29
  160.0 0.7 copy.54
  160.7 1.7 collective-permute-done.29
  163.0 3.0 %add_convert_fusion = bf16[512,768]{1,0:T(8,128)(2,1)} fusion(f32[512,768]{1,0:T(8,128)S(1)} %copy-done.3, f32[512]{0:T(512)S(1)} %slice_reduce_fusion, bf16[192,768]{1,0:T(8,128)(2,1)} %collective-permute-done.25, bf16[192,768]{1,0:T(8,128)(2,1)} %collective-permute-done.21, bf16[192,768]{1,0:T(8,128)(2,1)} %collective-permute-done.24, ...), kind=kOutput, calls=%fused_computation.9 | convolution fusion | flops 610271232 | bytes 3543040 | tf_op jit(solution)/shard_map/dot_general | solution.py:25
  166.1 1.1 copy-done
  167.6 1.5 fusion.3
  169.2 8.4 %all-to-all-done.4 = bf16[8,80,768]{2,1,0:T(8,128)(2,1)S(1)} async-done(((bf16[8,80,768]{2,1,0:T(8,128)(2,1)}), bf16[8,80,768]{2,1,0:T(8,128)(2,1)S(1)}, u32[]{:S(2)}, u32[]{:S(2)}) %all-to-all-start.4) | async-done | bytes 983072 | tf_op jit(solution)/shard_map/all_to_all | solution.py:526
  177.9 0.7 pad_maximum_fusion.1
  179.9 0.7 reshape_squeeze.3
  180.5 2.5 %collective-permute-done.30 = f32[8,768]{1,0:T(8,128)S(1)} collective-permute-done((f32[8,768]{1,0:T(8,128)S(1)}, f32[8,768]{1,0:T(8,128)S(1)}, u32[]{:S(2)}, u32[]{:S(2)}) %collective-permute-start.30) | collective-permute-done | bytes 24608 | tf_op jit(solution)/shard_map/ppermute | solution.py:516
  (132 shorter events, 12.4 us)
Async XLA Ops:
  0.6 12.1 %copy-start.25 = (s32[512,1]{0,1:T(1,128)S(1)}, s32[512,1]{0,1:T(1,128)}, u32[]{:S(2)}) copy-start(s32[512,1]{0,1:T(1,128)} %param.24) | copy-start | bytes 6148
  0.7 12.4 %collective-permute-start = (bf16[192,768]{1,0:T(8,128)(2,1)}, bf16[192,768]{1,0:T(8,128)(2,1)S(1)}, u32[]{:S(2)}, u32[]{:S(2)}) collective-permute-start(bf16[192,768]{1,0:T(8,128)(2,1)} %refs_8_.2), channel_id=1, source_target_pairs={{0,2},{1,3},{2,0},{3,1},{4,6},{5,7},{6,4},{7,5},{8,10},{9,11},{10,... | collective-permute-start | bytes 884744 | tf_op jit(solution)/shard_map/ppermute | solution.py:516
  3.7 19.0 %collective-permute-start.4 = (bf16[192,768]{1,0:T(8,128)(2,1)}, bf16[192,768]{1,0:T(8,128)(2,1)S(1)}, u32[]{:S(2)}, u32[]{:S(2)}) collective-permute-start(bf16[192,768]{1,0:T(8,128)(2,1)} %refs_8_.2), channel_id=1, source_target_pairs={{0,1},{1,0},{2,3},{3,2},{4,5},{5,4},{6,7},{7,6},{8,9},{9,8},{10,11... | collective-permute-start | bytes 884744 | tf_op jit(solution)/shard_map/ppermute | solution.py:516
  13.0 10.6 %copy-start.15 = (bf16[192,768]{1,0:T(8,128)(2,1)}, bf16[192,768]{1,0:T(8,128)(2,1)S(1)}, u32[]{:S(2)}) copy-start(bf16[192,768]{1,0:T(8,128)(2,1)S(1)} %collective-permute-done.refs_9_) | copy-start | bytes 884740
  13.0 9.0 %collective-permute-start.2 = (bf16[512,192]{1,0:T(8,128)(2,1)}, bf16[512,192]{1,0:T(8,128)(2,1)S(1)}, u32[]{:S(2)}, u32[]{:S(2)}) collective-permute-start(bf16[512,192]{1,0:T(8,128)(2,1)} %get-tuple-element.65.refs_3_.refs_9_), channel_id=1, source_target_pairs={{0,2},{1,3},{2,0},{3,1},{4,6},{5,7},{6,4},{7,5},{8,10},{9,11},{10,... | collective-permute-start | bytes 589832 | tf_op jit(solution)/shard_map/ppermute | solution.py:516
  13.2 9.5 %collective-permute-start.5 = (bf16[192,768]{1,0:T(8,128)(2,1)S(1)}, bf16[192,768]{1,0:T(8,128)(2,1)S(1)}, u32[]{:S(2)}, u32[]{:S(2)}) collective-permute-start(bf16[192,768]{1,0:T(8,128)(2,1)S(1)} %collective-permute-done.refs_9_), channel_id=1, source_target_pairs={{0,1},{1,0},{2,3},{3,2},{4,5},{5,4},{6,7},{7,6},{8,9},{9,8},{10,11... | collective-permute-start | bytes 884744 | tf_op jit(solution)/shard_map/ppermute | solution.py:516
  14.6 8.1 %collective-permute-start.1 = (bf16[512,192]{1,0:T(8,128)(2,1)}, bf16[512,192]{1,0:T(8,128)(2,1)S(1)}, u32[]{:S(2)}, u32[]{:S(2)}) collective-permute-start(bf16[512,192]{1,0:T(8,128)(2,1)} %get-tuple-element.65.refs_3_.refs_9_), channel_id=1, source_target_pairs={{0,1},{1,0},{2,3},{3,2},{4,5},{5,4},{6,7},{7,6},{8,9},{9,8},{10,11... | collective-permute-start | bytes 589832 | tf_op jit(solution)/shard_map/ppermute | solution.py:516
  22.0 1.5 collective-permute-start.3
  53.5 2.6 %copy-start.1 = (bf16[192,768]{1,0:T(8,128)(2,1)}, bf16[192,768]{1,0:T(8,128)(2,1)S(1)}, u32[]{:S(2)}) copy-start(bf16[192,768]{1,0:T(8,128)(2,1)S(1)} %get-tuple-element.158.refs_7_.refs_4_) | copy-start | bytes 884740
  53.6 2.6 %collective-permute-start.6 = (bf16[192,768]{1,0:T(8,128)(2,1)S(1)}, bf16[192,768]{1,0:T(8,128)(2,1)S(1)}, u32[]{:S(2)}, u32[]{:S(2)}) collective-permute-start(bf16[192,768]{1,0:T(8,128)(2,1)S(1)} %get-tuple-element.159.refs_6_.refs_0_), channel_id=1, source_target_pairs={{0,1},{1,0},{2,3},{3,2},{4,5},{5,4},{6,7},{7,6},{8,9},{9,8},{10,11... | collective-permute-start | bytes 884744 | tf_op jit(solution)/shard_map/ppermute | solution.py:516
  53.6 2.5 %collective-permute-start.7 = (bf16[192,768]{1,0:T(8,128)(2,1)S(1)}, bf16[192,768]{1,0:T(8,128)(2,1)S(1)}, u32[]{:S(2)}, u32[]{:S(2)}) collective-permute-start(bf16[192,768]{1,0:T(8,128)(2,1)S(1)} %get-tuple-element.158.refs_7_.refs_4_), channel_id=1, source_target_pairs={{0,1},{1,0},{2,3},{3,2},{4,5},{5,4},{6,7},{7,6},{8,9},{9,8},{10,11... | collective-permute-start | bytes 884744 | tf_op jit(solution)/shard_map/ppermute | solution.py:516
  54.1 10.4 %collective-permute-start.8 = (bf16[192,768]{1,0:T(8,128)(2,1)S(1)}, bf16[192,768]{1,0:T(8,128)(2,1)S(1)}, u32[]{:S(2)}, u32[]{:S(2)}) collective-permute-start(bf16[192,768]{1,0:T(8,128)(2,1)S(1)} %get-tuple-element.159.refs_6_.refs_0_), channel_id=1, source_target_pairs={{0,2},{1,3},{2,0},{3,1},{4,6},{5,7},{6,4},{7,5},{8,10},{9,11},{10,... | collective-permute-start | bytes 884744 | tf_op jit(solution)/shard_map/ppermute | solution.py:516
  54.6 14.8 %collective-permute-start.10 = (bf16[192,768]{1,0:T(8,128)(2,1)S(1)}, bf16[192,768]{1,0:T(8,128)(2,1)S(1)}, u32[]{:S(2)}, u32[]{:S(2)}) collective-permute-start(bf16[192,768]{1,0:T(8,128)(2,1)S(1)} %get-tuple-element.158.refs_7_.refs_4_), channel_id=1, source_target_pairs={{0,2},{1,3},{2,0},{3,1},{4,6},{5,7},{6,4},{7,5},{8,10},{9,11},{10,... | collective-permute-start | bytes 884744 | tf_op jit(solution)/shard_map/ppermute | solution.py:516
  64.6 6.5 %copy-start.7 = (bf16[192,768]{1,0:T(8,128)(2,1)}, bf16[192,768]{1,0:T(8,128)(2,1)S(1)}, u32[]{:S(2)}) copy-start(bf16[192,768]{1,0:T(8,128)(2,1)S(1)} %collective-permute-done.8.refs_6_.refs_2_) | copy-start | bytes 884740
  64.6 18.0 %copy-start.28 = (bf16[192,768]{1,0:T(8,128)(2,1)S(1)}, bf16[192,768]{1,0:T(8,128)(2,1)}, u32[]{:S(2)}) copy-start(bf16[192,768]{1,0:T(8,128)(2,1)} %get-tuple-element.81) | copy-start | bytes 884740
  64.6 18.9 %copy-start.27 = (bf16[192,768]{1,0:T(8,128)(2,1)S(1)}, bf16[192,768]{1,0:T(8,128)(2,1)}, u32[]{:S(2)}) copy-start(bf16[192,768]{1,0:T(8,128)(2,1)} %get-tuple-element.76) | copy-start | bytes 884740
  64.6 4.9 %collective-permute-start.9 = (bf16[192,768]{1,0:T(8,128)(2,1)S(1)}, bf16[192,768]{1,0:T(8,128)(2,1)S(1)}, u32[]{:S(2)}, u32[]{:S(2)}) collective-permute-start(bf16[192,768]{1,0:T(8,128)(2,1)S(1)} %collective-permute-done.8.refs_6_.refs_2_), channel_id=1, source_target_pairs={{0,1},{1,0},{2,3},{3,2},{4,5},{5,4},{6,7},{7,6},{8,9},{9,8},{10,11... | collective-permute-start | bytes 884744 | tf_op jit(solution)/shard_map/ppermute | solution.py:516
  69.4 1.6 collective-permute-start.11
  79.4 4.9 %copy-start.12 = (f32[192,768]{1,0:T(8,128)S(1)}, f32[192,768]{1,0:T(8,128)}, u32[]{:S(2)}) copy-start(f32[192,768]{1,0:T(8,128)} %get-tuple-element.77) | copy-start | bytes 1769476
  79.4 12.6 %copy-start.14 = (f32[192,768]{1,0:T(8,128)S(1)}, f32[192,768]{1,0:T(8,128)}, u32[]{:S(2)}) copy-start(f32[192,768]{1,0:T(8,128)} %get-tuple-element.80) | copy-start | bytes 1769476
  79.4 1.9 %collective-permute-start.12 = (bf16[192,768]{1,0:T(8,128)(2,1)}, bf16[192,768]{1,0:T(8,128)(2,1)S(1)}, u32[]{:S(2)}, u32[]{:S(2)}) collective-permute-start(bf16[192,768]{1,0:T(8,128)(2,1)} %get-tuple-element.75), channel_id=1, source_target_pairs={{0,1},{1,0},{2,3},{3,2},{4,5},{5,4},{6,7},{7,6},{8,9},{9,8},{10,11... | collective-permute-start | bytes 884744 | tf_op jit(solution)/shard_map/ppermute | solution.py:516
  82.4 1.9 %collective-permute-start.14 = (bf16[192,768]{1,0:T(8,128)(2,1)}, bf16[192,768]{1,0:T(8,128)(2,1)S(1)}, u32[]{:S(2)}, u32[]{:S(2)}) collective-permute-start(bf16[192,768]{1,0:T(8,128)(2,1)} %get-tuple-element.79), channel_id=1, source_target_pairs={{0,1},{1,0},{2,3},{3,2},{4,5},{5,4},{6,7},{7,6},{8,9},{9,8},{10,11... | collective-permute-start | bytes 884744 | tf_op jit(solution)/shard_map/ppermute | solution.py:516
  82.6 1.9 %collective-permute-start.15 = (bf16[192,768]{1,0:T(8,128)(2,1)S(1)}, bf16[192,768]{1,0:T(8,128)(2,1)S(1)}, u32[]{:S(2)}, u32[]{:S(2)}) collective-permute-start(bf16[192,768]{1,0:T(8,128)(2,1)S(1)} %copy-done.28), channel_id=1, source_target_pairs={{0,1},{1,0},{2,3},{3,2},{4,5},{5,4},{6,7},{7,6},{8,9},{9,8},{10,11... | collective-permute-start | bytes 884744 | tf_op jit(solution)/shard_map/ppermute | solution.py:516
  82.9 9.0 %collective-permute-start.16 = (bf16[192,768]{1,0:T(8,128)(2,1)S(1)}, bf16[192,768]{1,0:T(8,128)(2,1)S(1)}, u32[]{:S(2)}, u32[]{:S(2)}) collective-permute-start(bf16[192,768]{1,0:T(8,128)(2,1)S(1)} %add_convert_fusion.6), channel_id=1, source_target_pairs={{0,2},{1,3},{2,0},{3,1},{4,6},{5,7},{6,4},{7,5},{8,10},{9,11},{10,... | collective-permute-start | bytes 884744 | tf_op jit(solution)/shard_map/ppermute | solution.py:516
  83.5 20.1 %collective-permute-start.13 = (bf16[192,768]{1,0:T(8,128)(2,1)S(1)}, bf16[192,768]{1,0:T(8,128)(2,1)S(1)}, u32[]{:S(2)}, u32[]{:S(2)}) collective-permute-start(bf16[192,768]{1,0:T(8,128)(2,1)S(1)} %copy-done.27), channel_id=1, source_target_pairs={{0,1},{1,0},{2,3},{3,2},{4,5},{5,4},{6,7},{7,6},{8,9},{9,8},{10,11... | collective-permute-start | bytes 884744 | tf_op jit(solution)/shard_map/ppermute | solution.py:516
  92.8 10.8 %collective-permute-start.17 = (bf16[192,768]{1,0:T(8,128)(2,1)S(1)}, bf16[192,768]{1,0:T(8,128)(2,1)S(1)}, u32[]{:S(2)}, u32[]{:S(2)}) collective-permute-start(bf16[192,768]{1,0:T(8,128)(2,1)S(1)} %add_convert_fusion.5), channel_id=1, source_target_pairs={{0,2},{1,3},{2,0},{3,1},{4,6},{5,7},{6,4},{7,5},{8,10},{9,11},{10,... | collective-permute-start | bytes 884744 | tf_op jit(solution)/shard_map/ppermute | solution.py:516
  93.3 12.4 %all-to-all-start.1 = ((bf16[8,24,768]{2,1,0:T(8,128)(2,1)}), bf16[8,24,768]{2,1,0:T(8,128)(2,1)S(1)}, u32[]{:S(2)}, u32[]{:S(2)}) async-start(bf16[8,24,768]{2,1,0:T(8,128)(2,1)} %bitcast.17), calls=%async_computation.1 | async-start | bytes 589824 | tf_op jit(solution)/shard_map/all_to_all | solution.py:526
  96.7 6.9 %copy-start.13 = (f32[192,768]{1,0:T(8,128)S(1)}, f32[192,768]{1,0:T(8,128)}, u32[]{:S(2)}) copy-start(f32[192,768]{1,0:T(8,128)} %get-tuple-element.69) | copy-start | bytes 1769476
  105.7 8.3 %copy-start.11 = (bf16[8,24,768]{2,1,0:T(8,128)(2,1)}, bf16[8,24,768]{2,1,0:T(8,128)(2,1)S(1)}, u32[]{:S(2)}) copy-start(bf16[8,24,768]{2,1,0:T(8,128)(2,1)S(1)} %all-to-all-done.1) | copy-start | bytes 884740
  105.7 6.8 %collective-permute-start.19 = (bf16[192,768]{1,0:T(8,128)(2,1)S(1)}, bf16[192,768]{1,0:T(8,128)(2,1)S(1)}, u32[]{:S(2)}, u32[]{:S(2)}) collective-permute-start(bf16[192,768]{1,0:T(8,128)(2,1)S(1)} %bitcast.47), channel_id=1, source_target_pairs={{0,2},{1,3},{2,0},{3,1},{4,6},{5,7},{6,4},{7,5},{8,10},{9,11},{10,... | collective-permute-start | bytes 884744 | tf_op jit(solution)/shard_map/ppermute | solution.py:516
  107.5 14.2 %all-to-all-start.2 = ((bf16[8,24,768]{2,1,0:T(8,128)(2,1)}), bf16[8,24,768]{2,1,0:T(8,128)(2,1)}, u32[]{:S(2)}, u32[]{:S(2)}) async-start(bf16[8,24,768]{2,1,0:T(8,128)(2,1)} %bitcast.19), calls=%async_computation.2 | async-start | bytes 589824 | tf_op jit(solution)/shard_map/all_to_all | solution.py:526
  112.5 1.6 collective-permute-start.18
  112.5 2.0 %collective-permute-start.20 = (bf16[192,768]{1,0:T(8,128)(2,1)S(1)}, bf16[192,768]{1,0:T(8,128)(2,1)S(1)}, u32[]{:S(2)}, u32[]{:S(2)}) collective-permute-start(bf16[192,768]{1,0:T(8,128)(2,1)S(1)} %collective-permute-done.19.refs_4_), channel_id=1, source_target_pairs={{0,1},{1,0},{2,3},{3,2},{4,5},{5,4},{6,7},{7,6},{8,9},{9,8},{10,11... | collective-permute-start | bytes 884744 | tf_op jit(solution)/shard_map/ppermute | solution.py:516
  121.8 19.9 %all-to-all-start.3 = ((bf16[8,32,768]{2,1,0:T(8,128)(2,1)}), bf16[8,32,768]{2,1,0:T(8,128)(2,1)S(1)}, u32[]{:S(2)}, u32[]{:S(2)}) async-start(bf16[8,32,768]{2,1,0:T(8,128)(2,1)} %bitcast.51), calls=%async_computation.3 | async-start | bytes 786432 | tf_op jit(solution)/shard_map/all_to_all | solution.py:526
  127.8 13.9 %collective-permute-start.21 = (bf16[192,768]{1,0:T(8,128)(2,1)}, bf16[192,768]{1,0:T(8,128)(2,1)}, u32[]{:S(2)}, u32[]{:S(2)}) collective-permute-start(bf16[192,768]{1,0:T(8,128)(2,1)} %bitcast.20), channel_id=1, source_target_pairs={{0,2},{1,3},{2,0},{3,1},{4,6},{5,7},{6,4},{7,5},{8,10},{9,11},{10,... | collective-permute-start | bytes 884744 | tf_op jit(solution)/shard_map/ppermute | solution.py:516
  141.6 4.7 %copy-start.26 = (bf16[768]{0:T(1024)(128)(2,1)S(1)}, bf16[768]{0:T(1024)(128)(2,1)}, u32[]{:S(2)}) copy-start(bf16[768]{0:T(1024)(128)(2,1)} %refs_9_.1) | copy-start | bytes 4612
  141.6 4.7 %copy-start.24 = (f32[512,128]{1,0:T(8,128)S(1)}, f32[512,128]{1,0:T(8,128)}, u32[]{:S(2)}) copy-start(f32[512,128]{1,0:T(8,128)} %get-tuple-element.67) | copy-start | bytes 786436
  141.7 2.0 %collective-permute-start.22 = (bf16[256,768]{1,0:T(8,128)(2,1)}, bf16[256,768]{1,0:T(8,128)(2,1)S(1)}, u32[]{:S(2)}, u32[]{:S(2)}) collective-permute-start(bf16[256,768]{1,0:T(8,128)(2,1)} %get-tuple-element.109), channel_id=1, source_target_pairs={{0,1},{1,0},{2,3},{3,2},{4,5},{5,4},{6,7},{7,6},{8,9},{9,8},{10,11... | collective-permute-start | bytes 1179656 | tf_op jit(solution)/shard_map/ppermute | solution.py:516
  144.9 11.3 %collective-permute-start.23 = (bf16[256,768]{1,0:T(8,128)(2,1)S(1)}, bf16[256,768]{1,0:T(8,128)(2,1)}, u32[]{:S(2)}, u32[]{:S(2)}) collective-permute-start(bf16[256,768]{1,0:T(8,128)(2,1)S(1)} %add_convert_fusion.2), channel_id=1, source_target_pairs={{0,2},{1,3},{2,0},{3,1},{4,6},{5,7},{6,4},{7,5},{8,10},{9,11},{10,... | collective-permute-start | bytes 1179656 | tf_op jit(solution)/shard_map/ppermute | solution.py:516
  146.5 16.5 %collective-permute-start.25 = (bf16[192,768]{1,0:T(8,128)(2,1)}, bf16[192,768]{1,0:T(8,128)(2,1)}, u32[]{:S(2)}, u32[]{:S(2)}) collective-permute-start(bf16[192,768]{1,0:T(8,128)(2,1)} %collective-permute-done.21), channel_id=1, source_target_pairs={{0,1},{1,0},{2,3},{3,2},{4,5},{5,4},{6,7},{7,6},{8,9},{9,8},{10,11... | collective-permute-start | bytes 884744 | tf_op jit(solution)/shard_map/ppermute | solution.py:516
  146.6 31.0 %all-to-all-start.4 = ((bf16[8,80,768]{2,1,0:T(8,128)(2,1)}), bf16[8,80,768]{2,1,0:T(8,128)(2,1)S(1)}, u32[]{:S(2)}, u32[]{:S(2)}) async-start(bf16[8,80,768]{2,1,0:T(8,128)(2,1)} %bitcast.23), calls=%async_computation.4 | async-start | bytes 1966080 | tf_op jit(solution)/shard_map/all_to_all | solution.py:526
  152.6 10.4 %copy-start.3 = (f32[512,768]{1,0:T(8,128)S(1)}, f32[512,768]{1,0:T(8,128)}, u32[]{:S(2)}) copy-start(f32[512,768]{1,0:T(8,128)} %get-tuple-element.66.refs_1_) | copy-start | bytes 4718596
  157.3 1.3 collective-permute-start.28
  157.5 8.5 %collective-permute-start.26 = (bf16[256,768]{1,0:T(8,128)(2,1)S(1)}, bf16[256,768]{1,0:T(8,128)(2,1)S(1)}, u32[]{:S(2)}, u32[]{:S(2)}) collective-permute-start(bf16[256,768]{1,0:T(8,128)(2,1)S(1)} %add_convert_fusion.1), channel_id=1, source_target_pairs={{0,1},{1,0},{2,3},{3,2},{4,5},{5,4},{6,7},{7,6},{8,9},{9,8},{10,11... | collective-permute-start | bytes 1179656 | tf_op jit(solution)/shard_map/ppermute | solution.py:516
  158.0 5.1 %collective-permute-start.24 = (bf16[192,768]{1,0:T(8,128)(2,1)}, bf16[192,768]{1,0:T(8,128)(2,1)}, u32[]{:S(2)}, u32[]{:S(2)}) collective-permute-start(bf16[192,768]{1,0:T(8,128)(2,1)} %bitcast.20), channel_id=1, source_target_pairs={{0,1},{1,0},{2,3},{3,2},{4,5},{5,4},{6,7},{7,6},{8,9},{9,8},{10,11... | collective-permute-start | bytes 884744 | tf_op jit(solution)/shard_map/ppermute | solution.py:516
  158.6 3.8 %collective-permute-start.29 = (f32[8,768]{1,0:T(8,128)S(1)}, f32[8,768]{1,0:T(8,128)S(1)}, u32[]{:S(2)}, u32[]{:S(2)}) collective-permute-start(f32[8,768]{1,0:T(8,128)S(1)} %slice_add_fusion.1), channel_id=1, source_target_pairs={{0,2},{1,3},{2,0},{3,1},{4,6},{5,7},{6,4},{7,5},{8,10},{9,11},{10,... | collective-permute-start | bytes 73736 | tf_op jit(solution)/shard_map/ppermute | solution.py:516
  177.8 1.4 collective-permute-start.27
  179.2 3.8 %collective-permute-start.30 = (f32[8,768]{1,0:T(8,128)S(1)}, f32[8,768]{1,0:T(8,128)S(1)}, u32[]{:S(2)}, u32[]{:S(2)}) collective-permute-start(f32[8,768]{1,0:T(8,128)S(1)} %slice_add_fusion.2), channel_id=1, source_target_pairs={{0,2},{1,3},{2,0},{3,1},{4,6},{5,7},{6,4},{7,5},{8,10},{9,11},{10,... | collective-permute-start | bytes 73736 | tf_op jit(solution)/shard_map/ppermute | solution.py:516
  (16 other events, 19.2 us)
